TPU v7x, 256 devices: a whole 4x4x8 slice. The times are simulated.
256 devices in a mesh: pipe: 8 (over y_hi, x), fsdp: 16 (over z, core), rep: 2 (over y_lo).
Axes of the slice: x: 4, y: 4 (y_hi: 2, y_lo: 2; y = y_hi * 2 + y_lo), z: 8, core: 2. Of those that a mesh axis runs over, the one named last changes fastest.
Arguments:
- activations: bfloat16 [8, 2, 2048, 8192], P('pipe', 'rep', 'fsdp'), may hold values from -6 to 6
- query_rows: bfloat16 [8, 2, 2048, 8192], P('pipe', 'rep', 'fsdp'), may hold values from -6 to 6
- key_rows: bfloat16 [8, 2, 2048, 512], P('pipe', 'rep', 'fsdp'), may hold values from -6 to 6
- out_grad: bfloat16 [8, 2, 2048, 8192], P('pipe', 'rep', 'fsdp'), may hold values from -6 to 6
- value_weight: bfloat16 [8, 8192, 512], P('pipe', 'fsdp'), may hold values from -0.0625 to 0.0625
- doc_lengths: int32 [2, 4], P('rep'), may hold values from 1 to 1024, 2048 in all within a row
Outputs:
- upstream_grad: bfloat16 [8, 2, 2048, 8192], P('pipe', 'rep', 'fsdp')
- query_grad: bfloat16 [8, 2, 2048, 8192], P('pipe', 'rep', 'fsdp')
- key_grad: bfloat16 [8, 2, 2048, 512], P('pipe', 'rep', 'fsdp')
- weight_grad: bfloat16 [8, 8192, 512], P('pipe', 'fsdp')
Inputs may be any that keep to these rules, and one draw needn't show every extreme that they name: `doc_lengths`: each row sums to 2048; each row's longest document has exactly 1024 tokens.
All inputs are finite; a program needn't handle non-finite values.
Results may differ from a plain program's by a relative error of at most 0.027.
Values may be sent and summed in bfloat16 or wider, within the bound.
No kernel may reach another device: no remote copies, remote signals or barrier semaphores. Data moves between devices by JAX's collectives and lax.ppermute only.
A program may use at most 128 MiB of HBM per device.

v0:
```python
import jax
import jax.numpy as jnp
from jax import lax
from jax.experimental import pallas as pl
from jax.experimental.pallas import tpu as pltpu
from jax.sharding import PartitionSpec as P

HQ = 64
KV = 4
HD = 128
DOCS = 4
TOK = 128
LONGEST = 1024
BACK = LONGEST // TOK
BLOCKS = BACK + 1
HOPS = BACK // 2
WINDOW = BLOCKS * TOK
GROUP = HQ // KV
PAIRS = GROUP // 2
STEP_PAIRS = 2
STEPS = PAIRS // STEP_PAIRS
SCALE = HD ** (-0.5)
LOG2E = 1.4426950408889634
MASKED = -1e30
NT = (((1,), (1,)), ((), ()))
NN = (((1,), (0,)), ((), ()))
QUAD = ((0, 0), (1, 0), (0, 1), (1, 1))


def dot(left, right, numbers):
    return lax.dot_general(left, right, numbers, preferred_element_type=jnp.float32)


def stacked(ref, pair):
    first = 2 * pair * HD
    return jnp.concatenate([ref[:, first : first + HD], ref[:, first + HD : first + 2 * HD]], axis=0)


def probs_kernel(info_ref, query_ref, grad_ref, key_ref, probs_ref, value_ref, bias_ref, *score_refs):
    group, step = pl.program_id(0), pl.program_id(1)

    @pl.when((group == 0) & (step == 0))
    def _():
        begin = info_ref[0]
        query_pos = begin + lax.broadcasted_iota(jnp.int32, (1, TOK), 1)
        doc_start = jnp.zeros((1, TOK), jnp.int32)
        doc_end = 0
        for doc in range(DOCS):
            doc_end = doc_end + info_ref[1 + doc]
            doc_start = jnp.where(query_pos >= doc_end, doc_end, doc_start)
        key_pos = begin - BACK * TOK + lax.broadcasted_iota(jnp.int32, (WINDOW, TOK), 0)
        visible = (key_pos >= doc_start) & (key_pos <= query_pos)
        bias_ref[...] = jnp.where(visible, 0.0, MASKED)

    @pl.when(step == 0)
    def _():
        value_ref[...] = jnp.zeros_like(value_ref)

    for pair in range(STEP_PAIRS):
        score_ref = score_refs[pair]
        query_pair = stacked(query_ref, pair)
        grad_pair = stacked(grad_ref, pair)
        most = jnp.full((1, 2 * TOK), MASKED, jnp.float32)
        for block in range(BLOCKS):
            rows = slice(block * TOK, (block + 1) * TOK)
            bias = bias_ref[rows, :]
            scores = dot(key_ref[rows, :], query_pair, NT) * (SCALE * LOG2E) + jnp.concatenate([bias, bias], axis=1)
            score_ref[rows, :] = scores
            most = jnp.maximum(most, jnp.max(scores, axis=0, keepdims=True))
        total = jnp.zeros((1, 2 * TOK), jnp.float32)
        for block in range(BLOCKS):
            rows = slice(block * TOK, (block + 1) * TOK)
            numer = jnp.exp2(score_ref[rows, :] - most)
            score_ref[rows, :] = numer
            total = total + jnp.sum(numer, axis=0, keepdims=True)
        inverse = 1.0 / total
        for block in range(BLOCKS):
            rows = slice(block * TOK, (block + 1) * TOK)
            probs = (score_ref[rows, :] * inverse).astype(jnp.bfloat16)
            probs_ref[pair, rows, :] = probs
            value_ref[rows, :] += dot(probs, grad_pair, NN)


def grads_kernel(query_ref, grad_ref, key_ref, value_ref, probs_ref, query_out_ref, key_out_ref, flip_ref, *scratch):
    step = pl.program_id(1)
    dprobs_refs, dscores_refs = scratch[:STEP_PAIRS], scratch[STEP_PAIRS:]

    @pl.when(step == 0)
    def _():
        key_out_ref[...] = jnp.zeros_like(key_out_ref)
        for block in range(BLOCKS):
            rows = slice(block * TOK, (block + 1) * TOK)
            flip_ref[:, rows] = key_ref[rows, :].T

    for pair in range(STEP_PAIRS):
        dprobs_ref, dscores_ref = dprobs_refs[pair], dscores_refs[pair]
        query_pair = stacked(query_ref, pair)
        grad_pair = stacked(grad_ref, pair)
        delta = jnp.zeros((1, 2 * TOK), jnp.float32)
        for block in range(BLOCKS):
            rows = slice(block * TOK, (block + 1) * TOK)
            dprobs = dot(value_ref[rows, :], grad_pair, NT)
            dprobs_ref[rows, :] = dprobs
            delta = delta + jnp.sum(probs_ref[pair, rows, :].astype(jnp.float32) * dprobs, axis=0, keepdims=True)
        for block in range(BLOCKS):
            rows = slice(block * TOK, (block + 1) * TOK)
            probs = probs_ref[pair, rows, :].astype(jnp.float32)
            dscores = (probs * (dprobs_ref[rows, :] - delta)).astype(jnp.bfloat16)
            dscores_ref[rows, :] = dscores
            key_out_ref[rows, :] += dot(dscores, query_pair, NN)
        flipped = dot(flip_ref[...], dscores_ref[...], NN) * SCALE
        for half in range(2):
            columns = slice((2 * pair + half) * HD, (2 * pair + half + 1) * HD)
            query_out_ref[:, columns] = flipped[:, half * TOK : (half + 1) * TOK].T.astype(jnp.bfloat16)


def head_spec():
    return pl.BlockSpec((TOK, 2 * STEP_PAIRS * HD), lambda group, step: (0, group * STEPS + step))


def window_spec():
    return pl.BlockSpec((WINDOW, HD), lambda group, step: (0, group))


def probs_spec():
    return pl.BlockSpec((STEP_PAIRS, WINDOW, 2 * TOK), lambda group, step: (group * STEPS + step, 0, 0))


def probs_and_value_grad(info, queries, grads, key_window):
    return pl.pallas_call(
        probs_kernel,
        grid=(KV, STEPS),
        in_specs=[pl.BlockSpec(memory_space=pltpu.SMEM), head_spec(), head_spec(), window_spec()],
        out_specs=[probs_spec(), window_spec()],
        out_shape=[
            jax.ShapeDtypeStruct((HQ // 2, WINDOW, 2 * TOK), jnp.bfloat16),
            jax.ShapeDtypeStruct((WINDOW, KV * HD), jnp.float32),
        ],
        scratch_shapes=[pltpu.VMEM((WINDOW, TOK), jnp.float32)]
        + [pltpu.VMEM((WINDOW, 2 * TOK), jnp.float32)] * STEP_PAIRS,
        compiler_params=pltpu.CompilerParams(vmem_limit_bytes=40 * 1024 * 1024),
        cost_estimate=pl.CostEstimate(
            flops=2 * 2 * HQ * TOK * WINDOW * HD, bytes_accessed=26 << 20, transcendentals=HQ * TOK * WINDOW
        ),
    )(info, queries, grads, key_window)


def query_and_key_grad(queries, grads, key_window, value_window, probs):
    return pl.pallas_call(
        grads_kernel,
        grid=(KV, STEPS),
        in_specs=[head_spec(), head_spec(), window_spec(), window_spec(), probs_spec()],
        out_specs=[head_spec(), window_spec()],
        out_shape=[
            jax.ShapeDtypeStruct((TOK, HQ * HD), jnp.bfloat16),
            jax.ShapeDtypeStruct((WINDOW, KV * HD), jnp.float32),
        ],
        scratch_shapes=[pltpu.VMEM((HD, WINDOW), jnp.bfloat16)]
        + [pltpu.VMEM((WINDOW, 2 * TOK), jnp.float32)] * STEP_PAIRS
        + [pltpu.VMEM((WINDOW, 2 * TOK), jnp.bfloat16)] * STEP_PAIRS,
        compiler_params=pltpu.CompilerParams(vmem_limit_bytes=40 * 1024 * 1024),
        cost_estimate=pl.CostEstimate(
            flops=3 * 2 * HQ * TOK * WINDOW * HD, bytes_accessed=30 << 20, transcendentals=0
        ),
    )(queries, grads, key_window, value_window, probs)


def shifted(value, axis, steps):
    count = lax.axis_size(axis)
    initial, last = (max(0, -steps), min(count, count - steps))
    return lax.ppermute(value, axis, [(source, source + steps) for source in range(initial, last)])


def permuted(value, steps):
    count = lax.axis_size("fsdp")
    return lax.ppermute(value, "fsdp", [(source, (source + steps) % count) for source in range(count)])


def core_swapped(value):
    count = lax.axis_size("fsdp")
    return lax.ppermute(value, "fsdp", [(source, source ^ 1) for source in range(count)])


def window_of(block, odd):
    own = [block] + [permuted(block, 2 * hop) for hop in range(1, HOPS + 1)]
    given = jnp.concatenate([lax.select(odd, own[hop + 1], own[hop]) for hop in range(HOPS)], axis=0)
    taken = core_swapped(given)
    pieces = [own[HOPS]]
    for hop in reversed(range(HOPS)):
        pieces += [taken[hop * TOK : (hop + 1) * TOK], own[hop]]
    return jnp.concatenate(pieces, axis=0)


def window_sum(window, odd):
    part = [window[block * TOK : (block + 1) * TOK] for block in range(BLOCKS)]
    kept = [part[BACK - 2 * hop] for hop in range(HOPS + 1)]
    given = jnp.concatenate([part[BACK - 2 * hop - 1] for hop in range(HOPS)], axis=0).astype(jnp.bfloat16)
    taken = core_swapped(given).astype(jnp.float32).reshape(HOPS, TOK, -1)
    none = jnp.zeros((1,) + taken.shape[1:], taken.dtype)
    added = lax.select(odd, jnp.concatenate([none, taken]), jnp.concatenate([taken, none]))
    total = kept[0] + added[0]
    for hop in range(1, HOPS + 1):
        sent = (kept[hop] + added[hop]).astype(jnp.bfloat16)
        total = total + permuted(sent, -2 * hop).astype(jnp.float32)
    return total


def quad_partner(value, core, micro):
    chips, cores, reps = lax.axis_size("fsdp") // 2, 2, lax.axis_size("rep")
    moves = [
        ((chip * cores + here) * reps + rep, (chip * cores + (here ^ core)) * reps + (rep ^ micro))
        for chip in range(chips)
        for here in range(cores)
        for rep in range(reps)
    ]
    return lax.ppermute(value, ("fsdp", "rep"), moves)


def gathered_in_quad(value):
    return [value] + [quad_partner(value, core, micro) for core, micro in QUAD[1:]]


def inputs_in_quad(inputs, core, micro):
    chips, width = lax.axis_size("fsdp") // 2, inputs.shape[1] // 32
    pieces = inputs.reshape(TOK, chips, 2, 2, width).transpose(2, 3, 0, 1, 4).reshape(4, TOK, chips * width)
    own = [lax.dynamic_index_in_dim(pieces, 2 * (core ^ dc) + (micro ^ dm), 0, False) for dc, dm in QUAD]
    return [own[0]] + [quad_partner(piece, dc, dm) for piece, (dc, dm) in zip(own[1:], QUAD[1:])]


def shards(activations, query_rows, key_rows, out_grad, value_weight, doc_lengths):
    inputs = activations[0, 0]
    queries = query_rows[0, 0]
    keys = key_rows[0, 0]
    grads = out_grad[0, 0]
    weight_rows = value_weight[0]
    place = lax.axis_index("fsdp")
    core, micro = place % 2, lax.axis_index("rep")
    odd = core == 1
    info = jnp.concatenate([(place * TOK).reshape(1), doc_lengths[0]]).astype(jnp.int32)

    full_weight = lax.all_gather(weight_rows, "fsdp", axis=0, tiled=True)
    key_window = window_of(keys, odd)
    quad_inputs = jnp.concatenate(inputs_in_quad(inputs, core, micro), axis=0)

    probs, value_part = probs_and_value_grad(info, queries, grads, key_window)
    values = jnp.dot(inputs, full_weight, preferred_element_type=jnp.float32).astype(jnp.bfloat16)
    value_window = window_of(values, odd)
    value_grad = window_sum(value_part, odd).astype(jnp.bfloat16)

    quad_grads = jnp.concatenate(gathered_in_quad(value_grad), axis=0)
    weight_part = lax.dot_general(
        quad_inputs, quad_grads, (((0,), (0,)), ((), ())), preferred_element_type=jnp.float32
    ).astype(jnp.bfloat16)
    columns = [list(range(start, lax.axis_size("fsdp"), 2)) for start in range(2)]
    weight_half = lax.psum_scatter(
        weight_part, "fsdp", scatter_dimension=0, tiled=True, axis_index_groups=columns
    )
    other_half = lax.ppermute(weight_half, "rep", [(0, 1), (1, 0)])
    first = lax.select(micro == 0, weight_half, other_half)
    second = lax.select(micro == 0, other_half, weight_half)
    weight_grad = jnp.concatenate([first, second], axis=0)

    input_grad = lax.dot_general(
        value_grad, full_weight, (((1,), (1,)), ((), ())), preferred_element_type=jnp.float32
    ).astype(jnp.bfloat16)
    upstream = shifted(input_grad, "pipe", -1)

    query_out, key_part = query_and_key_grad(queries, grads, key_window, value_window, probs)
    key_grad = window_sum(key_part * SCALE, odd).astype(jnp.bfloat16)
    return (
        upstream[None, None],
        query_out[None, None],
        key_grad[None, None],
        weight_grad[None],
    )


def solution(mesh):
    tokens = P("pipe", "rep", "fsdp", None)
    weights = P("pipe", "fsdp", None)
    return jax.shard_map(
        shards,
        mesh=mesh,
        in_specs=(tokens, tokens, tokens, tokens, weights, P("rep", None)),
        out_specs=(tokens, tokens, tokens, weights),
        check_vma=False,
    )
```

profile of v0, /device:TPU:14, one launch (start us, length us, event | category | flops | bytes accessed | tf_op | source)
XLA Modules:
  0.0 235.9 jit_solution(12559018079461847119)
XLA Ops:
  8.8 2.0 collective-permute-start.1
  10.8 3.3 %collective-permute-start.2 = (bf16[128,512]{1,0:T(8,128)(2,1)}, bf16[128,512]{1,0:T(8,128)(2,1)S(1)}, u32[]{:S(2)}, u32[]{:S(2)}) collective-permute-start(bf16[128,512]{1,0:T(8,128)(2,1)} %bitcast.128), channel_id=1, source_target_pairs={{0,8},{2,10},{4,12},{6,14},{8,16},{10,18},{12,20},{14,22},{16,24},... | collective-permute-start | bytes 393224 | tf_op jit(solution)/shard_map/ppermute | solution.py:176
  14.1 4.0 %collective-permute-start.3 = (bf16[128,512]{1,0:T(8,128)(2,1)}, bf16[128,512]{1,0:T(8,128)(2,1)S(1)}, u32[]{:S(2)}, u32[]{:S(2)}) collective-permute-start(bf16[128,512]{1,0:T(8,128)(2,1)} %bitcast.129), channel_id=1, source_target_pairs={{0,12},{2,14},{4,16},{6,18},{8,20},{10,22},{12,24},{14,26},{16,28}... | collective-permute-start | bytes 393224 | tf_op jit(solution)/shard_map/ppermute | solution.py:176
  19.7 8.1 %collective-permute-done.2 = bf16[128,512]{1,0:T(8,128)(2,1)S(1)} collective-permute-done((bf16[128,512]{1,0:T(8,128)(2,1)}, bf16[128,512]{1,0:T(8,128)(2,1)S(1)}, u32[]{:S(2)}, u32[]{:S(2)}) %collective-permute-start.2) | collective-permute-done | bytes 131104 | tf_op jit(solution)/shard_map/ppermute | solution.py:176
  27.9 11.3 %collective-permute-done.3 = bf16[128,512]{1,0:T(8,128)(2,1)S(1)} collective-permute-done((bf16[128,512]{1,0:T(8,128)(2,1)}, bf16[128,512]{1,0:T(8,128)(2,1)S(1)}, u32[]{:S(2)}, u32[]{:S(2)}) %collective-permute-start.3) | collective-permute-done | bytes 131104 | tf_op jit(solution)/shard_map/ppermute | solution.py:176
  39.1 3.3 %collective-permute-done = bf16[128,512]{1,0:T(8,128)(2,1)S(1)} collective-permute-done((bf16[128,512]{1,0:T(8,128)(2,1)}, bf16[128,512]{1,0:T(8,128)(2,1)S(1)}, u32[]{:S(2)}, u32[]{:S(2)}) %collective-permute-start) | collective-permute-done | bytes 131104 | tf_op jit(solution)/shard_map/ppermute | solution.py:176
  48.9 27.8 %shard_map.93 = (bf16[32,1152,256]{2,1,0:T(8,128)(2,1)}, f32[1152,512]{1,0:T(8,128)S(1)}) custom-call(s32[5]{0:T(128)S(1)} %pad_add_fusion.info_ref, bf16[128,8192]{1,0:T(8,128)(2,1)S(1)} %bitcast.120, bf16[128,8192]{1,0:T(8,128)(2,1)S(1)} %bitcast.122, bf16[1152,512]{1,0:T(8,128)(2,1)S(1)} %constant_dynamic-update-slice_fusion.key_ref), custom_call_target="tpu_custom_call" | custom-call | flops 4831838208 | bytes 27262976 | tf_op jit(solution)/shard_map/pallas_call | solution.py:130
  77.8 4.1 %copy.10 = bf16[1,1,128,8192]{2,3,1,0:T(8,128)(2,1)} copy(bf16[1,1,128,8192]{3,2,1,0:T(8,128)(2,1)} %param.6) | data formatting | bytes 4194304 | tf_op args[0]
  81.9 3.1 %copy.11 = bf16[2,2,128,8,256]{2,4,3,1,0:T(8,128)(2,1)} copy(bf16[2,2,128,8,256]{2,4,1,0,3:T(8,128)(2,1)} %bitcast.125) | data formatting | bytes 4194304 | tf_op jit(solution)/shard_map/transpose | solution.py:225
  85.1 2.7 %dynamic-slice_bitcast_fusion.3 = (bf16[128,2048]{0,1:T(8,128)(2,1)}, bf16[128,2048]{0,1:T(8,128)(2,1)S(1)}, bf16[128,2048]{0,1:T(8,128)(2,1)}, bf16[128,2048]{0,1:T(8,128)(2,1)}) fusion(bf16[4,128,2048]{1,2,0:T(8,128)(2,1)} %bitcast.124, s32[]{:T(128)S(6)} %select_n.88, s32[]{:T(128)S(6)} %select_n.91, s32[]{:T(128)S(6)} %select_n.90, s32[]{:T(128)S(6)} %select_n.89), kind=kLoop, calls=%fused_computation.32 | loop fusion | bytes 4194320 | tf_op jit(solution)/shard_map/jit(dynamic_index_in_dim)/squeeze | solution.py:226
  89.8 3.0 %collective-permute-start.8 = (bf16[128,512]{1,0:T(8,128)(2,1)S(1)}, bf16[128,512]{1,0:T(8,128)(2,1)S(1)}, u32[]{:S(2)}, u32[]{:S(2)}) collective-permute-start(bf16[128,512]{1,0:T(8,128)(2,1)S(1)} %get-tuple-element.18), channel_id=1, source_target_pairs={{0,20},{2,22},{4,24},{6,26},{8,28},{10,30},{12,0},{14,2},{16,4},{1... | collective-permute-start | bytes 393224 | tf_op jit(solution)/shard_map/ppermute | solution.py:176
  92.9 5.0 %collective-permute-start.7 = (bf16[128,512]{1,0:T(8,128)(2,1)S(1)}, bf16[128,512]{1,0:T(8,128)(2,1)S(1)}, u32[]{:S(2)}, u32[]{:S(2)}) collective-permute-start(bf16[128,512]{1,0:T(8,128)(2,1)S(1)} %get-tuple-element.19), channel_id=1, source_target_pairs={{0,24},{2,26},{4,28},{6,30},{8,0},{10,2},{12,4},{14,6},{16,8},{18,... | collective-permute-start | bytes 393224 | tf_op jit(solution)/shard_map/ppermute | solution.py:176
  97.8 3.9 %collective-permute-start.6 = (bf16[128,512]{1,0:T(8,128)(2,1)S(1)}, bf16[128,512]{1,0:T(8,128)(2,1)S(1)}, u32[]{:S(2)}, u32[]{:S(2)}) collective-permute-start(bf16[128,512]{1,0:T(8,128)(2,1)S(1)} %get-tuple-element.16), channel_id=1, source_target_pairs={{0,28},{2,30},{4,0},{6,2},{8,4},{10,6},{12,8},{14,10},{16,12},{18,... | collective-permute-start | bytes 393224 | tf_op jit(solution)/shard_map/ppermute | solution.py:176
  103.3 2.8 %collective-permute-done.8 = bf16[128,512]{1,0:T(8,128)(2,1)S(1)} collective-permute-done((bf16[128,512]{1,0:T(8,128)(2,1)S(1)}, bf16[128,512]{1,0:T(8,128)(2,1)S(1)}, u32[]{:S(2)}, u32[]{:S(2)}) %collective-permute-start.8) | collective-permute-done | bytes 131104 | tf_op jit(solution)/shard_map/ppermute | solution.py:176
  106.1 5.3 %collective-permute-done.7 = bf16[128,512]{1,0:T(8,128)(2,1)S(1)} collective-permute-done((bf16[128,512]{1,0:T(8,128)(2,1)S(1)}, bf16[128,512]{1,0:T(8,128)(2,1)S(1)}, u32[]{:S(2)}, u32[]{:S(2)}) %collective-permute-start.7) | collective-permute-done | bytes 131104 | tf_op jit(solution)/shard_map/ppermute | solution.py:176
  111.4 3.5 %collective-permute-done.6 = bf16[128,512]{1,0:T(8,128)(2,1)S(1)} collective-permute-done((bf16[128,512]{1,0:T(8,128)(2,1)S(1)}, bf16[128,512]{1,0:T(8,128)(2,1)S(1)}, u32[]{:S(2)}, u32[]{:S(2)}) %collective-permute-start.6) | collective-permute-done | bytes 131104 | tf_op jit(solution)/shard_map/ppermute | solution.py:176
  118.4 5.3 %fusion.11 = bf16[128,512]{1,0:T(8,128)(2,1)S(1)} fusion(bf16[1,8192,512]{2,1,0:T(8,128)(2,1)} %all-gather.3.cloned.1.call-done, bf16[1,1,128,8192]{3,2,1,0:T(8,128)(2,1)} %param.6), kind=kOutput, calls=%fused_computation.16 | convolution fusion | flops 1073807360 | bytes 10616832 | tf_op jit(solution)/shard_map/dot_general | solution.py:246
  123.8 3.6 %collective-permute-start.13 = (bf16[128,512]{1,0:T(8,128)(2,1)S(1)}, bf16[128,512]{1,0:T(8,128)(2,1)S(1)}, u32[]{:S(2)}, u32[]{:S(2)}) collective-permute-start(bf16[128,512]{1,0:T(8,128)(2,1)S(1)} %fusion.11), channel_id=1, source_target_pairs={{0,8},{2,10},{4,12},{6,14},{8,16},{10,18},{12,20},{14,22},{16,24},... | collective-permute-start | bytes 393224 | tf_op jit(solution)/shard_map/ppermute | solution.py:176
  127.4 1.8 collective-permute-start.14
  130.8 3.9 %convolution_convert_fusion.1 = bf16[2048,512]{1,0:T(8,128)(2,1)} fusion(bf16[128,2048]{0,1:T(8,128)(2,1)S(1)} %copy-done.9, bf16[128,2048]{0,1:T(8,128)(2,1)} %collective-permute-done.22, bf16[128,2048]{0,1:T(8,128)(2,1)} %collective-permute-done.21, bf16[128,2048]{0,1:T(8,128)(2,1)S(1)} %copy-done.6, bf16[128,512]{1,0:T(8,128)(2,1)S(1)} %collective-permute-done.26, ...), kind=kOutput, calls=%fused_computation.4 | convolution fusion | flops 1085276160 | bytes 4718592 | tf_op jit(solution)/shard_map/dot_general | solution.py:251
  135.5 11.3 %collective-permute-done.14 = bf16[128,512]{1,0:T(8,128)(2,1)S(1)} collective-permute-done((bf16[128,512]{1,0:T(8,128)(2,1)S(1)}, bf16[128,512]{1,0:T(8,128)(2,1)S(1)}, u32[]{:S(2)}, u32[]{:S(2)}) %collective-permute-start.14) | collective-permute-done | bytes 131104 | tf_op jit(solution)/shard_map/ppermute | solution.py:176
  147.0 7.8 %convolution_convert_fusion = bf16[128,8192]{1,0:T(8,128)(2,1)} fusion(bf16[128,512]{1,0:T(8,128)(2,1)} %fusion.50, bf16[1,8192,512]{2,1,0:T(8,128)(2,1)} %all-gather.3.cloned.1.call-done), kind=kOutput, calls=%fused_computation | convolution fusion | flops 1074790400 | bytes 10616832 | tf_op jit(solution)/shard_map/dot_general | solution.py:263
  154.9 2.8 %collective-permute-start.10 = (bf16[128,8192]{1,0:T(8,128)(2,1)}, bf16[128,8192]{1,0:T(8,128)(2,1)}, u32[]{:S(2)}, u32[]{:S(2)}) collective-permute-start(bf16[128,8192]{1,0:T(8,128)(2,1)} %convolution_convert_fusion), channel_id=1, source_target_pairs={{32,0},{64,32},{96,64},{128,96},{160,128},{192,160},{224,192},{33,... | collective-permute-start | bytes 6291464 | tf_op jit(solution)/shard_map/ppermute | solution.py:171
  157.9 31.3 %shard_map.94 = (bf16[128,8192]{1,0:T(8,128)(2,1)}, f32[1152,512]{1,0:T(8,128)S(1)}) custom-call(bf16[128,8192]{1,0:T(8,128)(2,1)S(1)} %bitcast.121, bf16[128,8192]{1,0:T(8,128)(2,1)S(1)} %bitcast.123, bf16[1152,512]{1,0:T(8,128)(2,1)S(1)} %constant_dynamic-update-slice_fusion.key_ref, bf16[1152,512]{1,0:T(8,128)(2,1)S(1)} %constant_dynamic-update-slice_fusion.5.value_ref, ...), custom_call_target="tpu_custom_call" | custom-call | flops 7247757312 | bytes 31457280 | tf_op jit(solution)/shard_map/pallas_call | solution.py:149
  194.1 3.8 %collective-permute-start.20 = (bf16[128,512]{1,0:T(8,128)(2,1)S(1)}, bf16[128,512]{1,0:T(8,128)(2,1)S(1)}, u32[]{:S(2)}, u32[]{:S(2)}) collective-permute-start(bf16[128,512]{1,0:T(8,128)(2,1)S(1)} %get-tuple-element.13), channel_id=1, source_target_pairs={{0,16},{2,18},{4,20},{6,22},{8,24},{10,26},{12,28},{14,30},{16,0},... | collective-permute-start | bytes 393224 | tf_op jit(solution)/shard_map/ppermute | solution.py:176
  197.9 2.9 %collective-permute-start.19 = (bf16[128,512]{1,0:T(8,128)(2,1)S(1)}, bf16[128,512]{1,0:T(8,128)(2,1)S(1)}, u32[]{:S(2)}, u32[]{:S(2)}) collective-permute-start(bf16[128,512]{1,0:T(8,128)(2,1)S(1)} %get-tuple-element.14), channel_id=1, source_target_pairs={{0,20},{2,22},{4,24},{6,26},{8,28},{10,30},{12,0},{14,2},{16,4},{1... | collective-permute-start | bytes 393224 | tf_op jit(solution)/shard_map/ppermute | solution.py:176
  200.8 3.4 %collective-permute-start.18 = (bf16[128,512]{1,0:T(8,128)(2,1)S(1)}, bf16[128,512]{1,0:T(8,128)(2,1)S(1)}, u32[]{:S(2)}, u32[]{:S(2)}) collective-permute-start(bf16[128,512]{1,0:T(8,128)(2,1)S(1)} %get-tuple-element.15), channel_id=1, source_target_pairs={{0,24},{2,26},{4,28},{6,30},{8,0},{10,2},{12,4},{14,6},{16,8},{18,... | collective-permute-start | bytes 393224 | tf_op jit(solution)/shard_map/ppermute | solution.py:176
  204.2 6.3 %collective-permute-start.17 = (bf16[128,512]{1,0:T(8,128)(2,1)S(1)}, bf16[128,512]{1,0:T(8,128)(2,1)S(1)}, u32[]{:S(2)}, u32[]{:S(2)}) collective-permute-start(bf16[128,512]{1,0:T(8,128)(2,1)S(1)} %get-tuple-element.12), channel_id=1, source_target_pairs={{0,28},{2,30},{4,0},{6,2},{8,4},{10,6},{12,8},{14,10},{16,12},{18,... | collective-permute-start | bytes 393224 | tf_op jit(solution)/shard_map/ppermute | solution.py:176
  211.4 2.4 %collective-permute-done.19 = bf16[128,512]{1,0:T(8,128)(2,1)S(1)} collective-permute-done((bf16[128,512]{1,0:T(8,128)(2,1)S(1)}, bf16[128,512]{1,0:T(8,128)(2,1)S(1)}, u32[]{:S(2)}, u32[]{:S(2)}) %collective-permute-start.19) | collective-permute-done | bytes 131104 | tf_op jit(solution)/shard_map/ppermute | solution.py:176
  213.8 7.5 %collective-permute-done.18 = bf16[128,512]{1,0:T(8,128)(2,1)S(1)} collective-permute-done((bf16[128,512]{1,0:T(8,128)(2,1)S(1)}, bf16[128,512]{1,0:T(8,128)(2,1)S(1)}, u32[]{:S(2)}, u32[]{:S(2)}) %collective-permute-start.18) | collective-permute-done | bytes 131104 | tf_op jit(solution)/shard_map/ppermute | solution.py:176
  221.3 3.3 %collective-permute-done.17 = bf16[128,512]{1,0:T(8,128)(2,1)S(1)} collective-permute-done((bf16[128,512]{1,0:T(8,128)(2,1)S(1)}, bf16[128,512]{1,0:T(8,128)(2,1)S(1)}, u32[]{:S(2)}, u32[]{:S(2)}) %collective-permute-start.17) | collective-permute-done | bytes 131104 | tf_op jit(solution)/shard_map/ppermute | solution.py:176
  225.4 3.1 %copy.29 = bf16[1,1,128,8192]{3,2,1,0:T(8,128)(2,1)} copy(bf16[1,1,128,8192]{3,2,1,0:T(8,128)(2,1)} %bitcast.13) | data formatting | bytes 4194304
  (98 shorter events, 26.1 us)
Async XLA Ops:
  8.0 110.4 %all-gather.3.cloned.1.call-start = ((), (), s32[]{:S(2)}) async-start(), calls=%async_computation.2 | async-start | bytes 8912896 | tf_op jit(solution)/shard_map/all_gather | solution.py:241
  8.7 34.9 %copy-start.10 = (s32[1,4]{1,0:T(1,128)S(1)}, s32[1,4]{1,0:T(1,128)}, u32[]{:S(2)}) copy-start(s32[1,4]{1,0:T(1,128)} %param.11) | copy-start | bytes 52
  8.7 181.2 %reduce-scatter.2.cloned.1.call-start = ((), (), s32[]{:S(2)}) async-start(), calls=%async_computation.1 | async-start | bytes 2359296 | tf_op jit(solution)/shard_map/reduce_scatter | solution.py:255
  8.8 10.9 %collective-permute-start.1 = (bf16[128,512]{1,0:T(8,128)(2,1)}, bf16[128,512]{1,0:T(8,128)(2,1)S(1)}, u32[]{:S(2)}, u32[]{:S(2)}) collective-permute-start(bf16[128,512]{1,0:T(8,128)(2,1)} %bitcast.127), channel_id=1, source_target_pairs={{0,4},{2,6},{4,8},{6,10},{8,12},{10,14},{12,16},{14,18},{16,20},{1... | collective-permute-start | bytes 393224 | tf_op jit(solution)/shard_map/ppermute | solution.py:176
  10.8 17.1 %collective-permute-start.2 = (bf16[128,512]{1,0:T(8,128)(2,1)}, bf16[128,512]{1,0:T(8,128)(2,1)S(1)}, u32[]{:S(2)}, u32[]{:S(2)}) collective-permute-start(bf16[128,512]{1,0:T(8,128)(2,1)} %bitcast.128), channel_id=1, source_target_pairs={{0,8},{2,10},{4,12},{6,14},{8,16},{10,18},{12,20},{14,22},{16,24},... | collective-permute-start | bytes 393224 | tf_op jit(solution)/shard_map/ppermute | solution.py:176
  14.1 25.1 %collective-permute-start.3 = (bf16[128,512]{1,0:T(8,128)(2,1)}, bf16[128,512]{1,0:T(8,128)(2,1)S(1)}, u32[]{:S(2)}, u32[]{:S(2)}) collective-permute-start(bf16[128,512]{1,0:T(8,128)(2,1)} %bitcast.129), channel_id=1, source_target_pairs={{0,12},{2,14},{4,16},{6,18},{8,20},{10,22},{12,24},{14,26},{16,28}... | collective-permute-start | bytes 393224 | tf_op jit(solution)/shard_map/ppermute | solution.py:176
  18.1 24.4 %collective-permute-start = (bf16[128,512]{1,0:T(8,128)(2,1)}, bf16[128,512]{1,0:T(8,128)(2,1)S(1)}, u32[]{:S(2)}, u32[]{:S(2)}) collective-permute-start(bf16[128,512]{1,0:T(8,128)(2,1)} %bitcast.130), channel_id=1, source_target_pairs={{0,16},{2,18},{4,20},{6,22},{8,24},{10,26},{12,28},{14,30},{16,0},... | collective-permute-start | bytes 393224 | tf_op jit(solution)/shard_map/ppermute | solution.py:176
  43.5 2.0 collective-permute-start.4
  77.7 10.4 %collective-permute-start.5 = (bf16[512,512]{1,0:T(8,128)(2,1)}, bf16[512,512]{1,0:T(8,128)(2,1)}, u32[]{:S(2)}, u32[]{:S(2)}) collective-permute-start(bf16[512,512]{1,0:T(8,128)(2,1)} %pad_maximum_fusion.1), channel_id=1, source_target_pairs={{0,2},{2,0},{4,6},{6,4},{8,10},{10,8},{12,14},{14,12},{16,18},{18,... | collective-permute-start | bytes 1572872 | tf_op jit(solution)/shard_map/ppermute | solution.py:181
  87.7 29.6 %collective-permute-start.23 = (bf16[128,2048]{0,1:T(8,128)(2,1)S(1)}, bf16[128,2048]{0,1:T(8,128)(2,1)S(1)}, u32[]{:S(2)}, u32[]{:S(2)}) collective-permute-start(bf16[128,2048]{0,1:T(8,128)(2,1)S(1)} %get-tuple-element.23), channel_id=1, source_target_pairs={{0,3},{1,2},{2,1},{3,0},{4,7},{5,6},{6,5},{7,4},{8,11},{9,10},{10,... | collective-permute-start | bytes 1572872 | tf_op jit(solution)/shard_map/ppermute | solution.py:216
  89.7 12.0 %collective-permute-start.9 = (bf16[128,512]{1,0:T(8,128)(2,1)S(1)}, bf16[128,512]{1,0:T(8,128)(2,1)S(1)}, u32[]{:S(2)}, u32[]{:S(2)}) collective-permute-start(bf16[128,512]{1,0:T(8,128)(2,1)S(1)} %get-tuple-element.17), channel_id=1, source_target_pairs={{0,16},{2,18},{4,20},{6,22},{8,24},{10,26},{12,28},{14,30},{16,0},... | collective-permute-start | bytes 393224 | tf_op jit(solution)/shard_map/ppermute | solution.py:176
  89.8 16.3 %collective-permute-start.8 = (bf16[128,512]{1,0:T(8,128)(2,1)S(1)}, bf16[128,512]{1,0:T(8,128)(2,1)S(1)}, u32[]{:S(2)}, u32[]{:S(2)}) collective-permute-start(bf16[128,512]{1,0:T(8,128)(2,1)S(1)} %get-tuple-element.18), channel_id=1, source_target_pairs={{0,20},{2,22},{4,24},{6,26},{8,28},{10,30},{12,0},{14,2},{16,4},{1... | collective-permute-start | bytes 393224 | tf_op jit(solution)/shard_map/ppermute | solution.py:176
  92.9 18.5 %collective-permute-start.7 = (bf16[128,512]{1,0:T(8,128)(2,1)S(1)}, bf16[128,512]{1,0:T(8,128)(2,1)S(1)}, u32[]{:S(2)}, u32[]{:S(2)}) collective-permute-start(bf16[128,512]{1,0:T(8,128)(2,1)S(1)} %get-tuple-element.19), channel_id=1, source_target_pairs={{0,24},{2,26},{4,28},{6,30},{8,0},{10,2},{12,4},{14,6},{16,8},{18,... | collective-permute-start | bytes 393224 | tf_op jit(solution)/shard_map/ppermute | solution.py:176
  97.8 17.1 %collective-permute-start.6 = (bf16[128,512]{1,0:T(8,128)(2,1)S(1)}, bf16[128,512]{1,0:T(8,128)(2,1)S(1)}, u32[]{:S(2)}, u32[]{:S(2)}) collective-permute-start(bf16[128,512]{1,0:T(8,128)(2,1)S(1)} %get-tuple-element.16), channel_id=1, source_target_pairs={{0,28},{2,30},{4,0},{6,2},{8,4},{10,6},{12,8},{14,10},{16,12},{18,... | collective-permute-start | bytes 393224 | tf_op jit(solution)/shard_map/ppermute | solution.py:176
  101.7 22.0 %collective-permute-start.22 = (bf16[128,2048]{0,1:T(8,128)(2,1)}, bf16[128,2048]{0,1:T(8,128)(2,1)}, u32[]{:S(2)}, u32[]{:S(2)}) collective-permute-start(bf16[128,2048]{0,1:T(8,128)(2,1)} %get-tuple-element.24), channel_id=1, source_target_pairs={{0,1},{1,0},{2,3},{3,2},{4,5},{5,4},{6,7},{7,6},{8,9},{9,8},{10,11... | collective-permute-start | bytes 1572872 | tf_op jit(solution)/shard_map/ppermute | solution.py:216
  106.1 17.7 %collective-permute-start.21 = (bf16[128,2048]{0,1:T(8,128)(2,1)}, bf16[128,2048]{0,1:T(8,128)(2,1)}, u32[]{:S(2)}, u32[]{:S(2)}) collective-permute-start(bf16[128,2048]{0,1:T(8,128)(2,1)} %get-tuple-element.25), channel_id=1, source_target_pairs={{0,2},{1,3},{2,0},{3,1},{4,6},{5,7},{6,4},{7,5},{8,10},{9,11},{10,... | collective-permute-start | bytes 1572872 | tf_op jit(solution)/shard_map/ppermute | solution.py:216
  115.7 11.7 %collective-permute-start.26 = (bf16[128,512]{1,0:T(8,128)(2,1)}, bf16[128,512]{1,0:T(8,128)(2,1)S(1)}, u32[]{:S(2)}, u32[]{:S(2)}) collective-permute-start(bf16[128,512]{1,0:T(8,128)(2,1)} %fusion.50), channel_id=1, source_target_pairs={{0,3},{1,2},{2,1},{3,0},{4,7},{5,6},{6,5},{7,4},{8,11},{9,10},{10,... | collective-permute-start | bytes 393224 | tf_op jit(solution)/shard_map/ppermute | solution.py:216
  116.0 13.2 %collective-permute-start.25 = (bf16[128,512]{1,0:T(8,128)(2,1)}, bf16[128,512]{1,0:T(8,128)(2,1)S(1)}, u32[]{:S(2)}, u32[]{:S(2)}) collective-permute-start(bf16[128,512]{1,0:T(8,128)(2,1)} %fusion.50), channel_id=1, source_target_pairs={{0,1},{1,0},{2,3},{3,2},{4,5},{5,4},{6,7},{7,6},{8,9},{9,8},{10,11... | collective-permute-start | bytes 393224 | tf_op jit(solution)/shard_map/ppermute | solution.py:216
  118.1 12.7 %collective-permute-start.24 = (bf16[128,512]{1,0:T(8,128)(2,1)}, bf16[128,512]{1,0:T(8,128)(2,1)S(1)}, u32[]{:S(2)}, u32[]{:S(2)}) collective-permute-start(bf16[128,512]{1,0:T(8,128)(2,1)} %fusion.50), channel_id=1, source_target_pairs={{0,2},{1,3},{2,0},{3,1},{4,6},{5,7},{6,4},{7,5},{8,10},{9,11},{10,... | collective-permute-start | bytes 393224 | tf_op jit(solution)/shard_map/ppermute | solution.py:216
  123.7 11.0 %collective-permute-start.12 = (bf16[128,512]{1,0:T(8,128)(2,1)S(1)}, bf16[128,512]{1,0:T(8,128)(2,1)S(1)}, u32[]{:S(2)}, u32[]{:S(2)}) collective-permute-start(bf16[128,512]{1,0:T(8,128)(2,1)S(1)} %fusion.11), channel_id=1, source_target_pairs={{0,4},{2,6},{4,8},{6,10},{8,12},{10,14},{12,16},{14,18},{16,20},{1... | collective-permute-start | bytes 393224 | tf_op jit(solution)/shard_map/ppermute | solution.py:176
  123.8 11.6 %collective-permute-start.13 = (bf16[128,512]{1,0:T(8,128)(2,1)S(1)}, bf16[128,512]{1,0:T(8,128)(2,1)S(1)}, u32[]{:S(2)}, u32[]{:S(2)}) collective-permute-start(bf16[128,512]{1,0:T(8,128)(2,1)S(1)} %fusion.11), channel_id=1, source_target_pairs={{0,8},{2,10},{4,12},{6,14},{8,16},{10,18},{12,20},{14,22},{16,24},... | collective-permute-start | bytes 393224 | tf_op jit(solution)/shard_map/ppermute | solution.py:176
  127.4 19.3 %collective-permute-start.14 = (bf16[128,512]{1,0:T(8,128)(2,1)S(1)}, bf16[128,512]{1,0:T(8,128)(2,1)S(1)}, u32[]{:S(2)}, u32[]{:S(2)}) collective-permute-start(bf16[128,512]{1,0:T(8,128)(2,1)S(1)} %fusion.11), channel_id=1, source_target_pairs={{0,12},{2,14},{4,16},{6,18},{8,20},{10,22},{12,24},{14,26},{16,28}... | collective-permute-start | bytes 393224 | tf_op jit(solution)/shard_map/ppermute | solution.py:176
  129.3 17.5 %collective-permute-start.11 = (bf16[128,512]{1,0:T(8,128)(2,1)S(1)}, bf16[128,512]{1,0:T(8,128)(2,1)S(1)}, u32[]{:S(2)}, u32[]{:S(2)}) collective-permute-start(bf16[128,512]{1,0:T(8,128)(2,1)S(1)} %fusion.11), channel_id=1, source_target_pairs={{0,16},{2,18},{4,20},{6,22},{8,24},{10,26},{12,28},{14,30},{16,0},... | collective-permute-start | bytes 393224 | tf_op jit(solution)/shard_map/ppermute | solution.py:176
  146.9 10.8 %collective-permute-start.15 = (bf16[512,512]{1,0:T(8,128)(2,1)S(1)}, bf16[512,512]{1,0:T(8,128)(2,1)S(1)}, u32[]{:S(2)}, u32[]{:S(2)}) collective-permute-start(bf16[512,512]{1,0:T(8,128)(2,1)S(1)} %pad_maximum_fusion.2), channel_id=1, source_target_pairs={{0,2},{2,0},{4,6},{6,4},{8,10},{10,8},{12,14},{14,12},{16,18},{18,... | collective-permute-start | bytes 1572872 | tf_op jit(solution)/shard_map/ppermute | solution.py:181
  154.9 70.5 %collective-permute-start.10 = (bf16[128,8192]{1,0:T(8,128)(2,1)}, bf16[128,8192]{1,0:T(8,128)(2,1)}, u32[]{:S(2)}, u32[]{:S(2)}) collective-permute-start(bf16[128,8192]{1,0:T(8,128)(2,1)} %convolution_convert_fusion), channel_id=1, source_target_pairs={{32,0},{64,32},{96,64},{128,96},{160,128},{192,160},{224,192},{33,... | collective-permute-start | bytes 6291464 | tf_op jit(solution)/shard_map/ppermute | solution.py:171
  189.7 2.0 collective-permute-start.16
  190.0 14.2 %collective-permute-start.27 = (bf16[256,512]{1,0:T(8,128)(2,1)}, bf16[256,512]{1,0:T(8,128)(2,1)S(1)}, u32[]{:S(2)}, u32[]{:S(2)}) collective-permute-start(bf16[256,512]{1,0:T(8,128)(2,1)} %reduce-scatter.2.cloned.1.call-done), channel_id=1, source_target_pairs={{0,1},{1,0},{2,3},{3,2},{4,5},{5,4},{6,7},{7,6},{8,9},{9,8},{10,11... | collective-permute-start | bytes 786440 | tf_op jit(solution)/shard_map/ppermute | solution.py:258
  193.9 16.6 %copy-start.7 = (bf16[256,512]{1,0:T(8,128)(2,1)S(1)}, bf16[256,512]{1,0:T(8,128)(2,1)}, u32[]{:S(2)}) copy-start(bf16[256,512]{1,0:T(8,128)(2,1)} %reduce-scatter.2.cloned.1.call-done) | copy-start | bytes 786436
  194.1 17.2 %collective-permute-start.20 = (bf16[128,512]{1,0:T(8,128)(2,1)S(1)}, bf16[128,512]{1,0:T(8,128)(2,1)S(1)}, u32[]{:S(2)}, u32[]{:S(2)}) collective-permute-start(bf16[128,512]{1,0:T(8,128)(2,1)S(1)} %get-tuple-element.13), channel_id=1, source_target_pairs={{0,16},{2,18},{4,20},{6,22},{8,24},{10,26},{12,28},{14,30},{16,0},... | collective-permute-start | bytes 393224 | tf_op jit(solution)/shard_map/ppermute | solution.py:176
  197.9 15.9 %collective-permute-start.19 = (bf16[128,512]{1,0:T(8,128)(2,1)S(1)}, bf16[128,512]{1,0:T(8,128)(2,1)S(1)}, u32[]{:S(2)}, u32[]{:S(2)}) collective-permute-start(bf16[128,512]{1,0:T(8,128)(2,1)S(1)} %get-tuple-element.14), channel_id=1, source_target_pairs={{0,20},{2,22},{4,24},{6,26},{8,28},{10,30},{12,0},{14,2},{16,4},{1... | collective-permute-start | bytes 393224 | tf_op jit(solution)/shard_map/ppermute | solution.py:176
  200.8 20.6 %collective-permute-start.18 = (bf16[128,512]{1,0:T(8,128)(2,1)S(1)}, bf16[128,512]{1,0:T(8,128)(2,1)S(1)}, u32[]{:S(2)}, u32[]{:S(2)}) collective-permute-start(bf16[128,512]{1,0:T(8,128)(2,1)S(1)} %get-tuple-element.15), channel_id=1, source_target_pairs={{0,24},{2,26},{4,28},{6,30},{8,0},{10,2},{12,4},{14,6},{16,8},{18,... | collective-permute-start | bytes 393224 | tf_op jit(solution)/shard_map/ppermute | solution.py:176
  204.2 20.4 %collective-permute-start.17 = (bf16[128,512]{1,0:T(8,128)(2,1)S(1)}, bf16[128,512]{1,0:T(8,128)(2,1)S(1)}, u32[]{:S(2)}, u32[]{:S(2)}) collective-permute-start(bf16[128,512]{1,0:T(8,128)(2,1)S(1)} %get-tuple-element.12), channel_id=1, source_target_pairs={{0,28},{2,30},{4,0},{6,2},{8,4},{10,6},{12,8},{14,10},{16,12},{18,... | collective-permute-start | bytes 393224 | tf_op jit(solution)/shard_map/ppermute | solution.py:176
  (9 other events, 48.5 us)
Sparse Core Ops, SparseCore 0:
  10.7 68.8 all-gather.2
Sparse Core Ops, SparseCore 1:
  134.8 45.0 reduce-scatter.1
where the time goes:
time: 239 us; the launch traced here: 236 us
  waiting for transfers between devices  63.4 us (27%)
  Pallas kernels  59.1 us (25%)
  starting transfers between devices  54.1 us (23%)
  local copies, waits for them, and re-layouts  18.1 us (8%)
  matrix products  17.1 us (7%)
  between operations  15.9 us (7%)
  other arithmetic  8.23 us (3%)
    ppermute x16, waiting for transfers between devices, permuted(): lax.ppermute(value, 'fsdp', [(source, (source + steps) % count) for sourc...  60.7 us
    ppermute x16, starting transfers between devices, permuted(): lax.ppermute(value, 'fsdp', [(source, (source + steps) % count) for sourc...  45.3 us
    pallas_call x1, Pallas kernels, query_and_key_grad(): pl.pallas_call(grads_kernel, grid=(KV, STEPS), in_specs=[head_spec(), hea...  31.3 us
    pallas_call x1, Pallas kernels, probs_and_value_grad(): pl.pallas_call(probs_kernel, grid=(KV, STEPS), in_specs=[pl.BlockSpec(mem...  27.8 us
    unnamed x38, local copies, waits for them, and re-layouts  12.2 us
    dot_general x1, matrix products, shards(): lax.dot_general(value_grad, full_weight, (((1,), (1,)), ((), ())), prefer...  7.83 us
    dot_general x1, matrix products, shards(): jnp.dot(inputs, full_weight, preferred_element_type=jnp.float32)  5.33 us
  transfers between devices with their start and end apart: 30, of which 14 were waited for; matrix products, arithmetic and copies ran while one was open for 15% of the time, Pallas kernels for 25%

commit v1 on v0

v1 whole, which is shorter than its diff:
```python
import jax
import jax.numpy as jnp
from jax import lax
from jax.experimental import pallas as pl
from jax.experimental.pallas import tpu as pltpu
from jax.sharding import PartitionSpec as P

HQ = 64
KV = 4
HD = 128
DOCS = 4
TOK = 128
LONGEST = 1024
BACK = LONGEST // TOK
BLOCKS = BACK + 1
HOPS = BACK // 2
WINDOW = BLOCKS * TOK
GROUP = HQ // KV
PAIRS = GROUP // 2
STEP_PAIRS = 8
STEPS = PAIRS // STEP_PAIRS
PART = 3 * TOK
PARTS = WINDOW // PART
SCALE = HD ** (-0.5)
LOG2E = 1.4426950408889634
MASKED = -1e30
NT = (((1,), (1,)), ((), ()))
NN = (((1,), (0,)), ((), ()))
TN = (((0,), (0,)), ((), ()))
CHIPS = 8
CORES = 2
REPS = 2
SLAB = 256


def dot(left, right, numbers):
    return lax.dot_general(left, right, numbers, preferred_element_type=jnp.float32)


def stacked(ref, pair):
    first = 2 * pair * HD
    return jnp.concatenate([ref[:, first : first + HD], ref[:, first + HD : first + 2 * HD]], axis=0)


def rows_of(block):
    return slice(block * TOK, (block + 1) * TOK)


def part_rows(part):
    return slice(part * PART, (part + 1) * PART)


def window_block(refs, block):
    hop, odd = divmod(BACK - block, 2)
    return refs[HOPS + 1][rows_of(hop), :] if odd else refs[hop][...]


def staggered(first, middle, second, finish=None):
    for pair in range(STEP_PAIRS + 1):
        for part in range(PARTS):
            if pair:
                second(pair - 1, part)
            if pair < STEP_PAIRS:
                first(pair, part)
        if middle and pair < STEP_PAIRS:
            middle(pair)
        if finish and pair:
            finish(pair - 1)


def probs_kernel(info_ref, query_ref, grad_ref, *refs):
    key_refs, (probs_ref, given_ref, kept_ref, bias_ref, total_ref, window_ref), score_refs = refs[:6], refs[-8:-2], refs[-2:]
    group, step = pl.program_id(0), pl.program_id(1)

    @pl.when((group == 0) & (step == 0))
    def _():
        begin = info_ref[0]
        query_pos = begin + lax.broadcasted_iota(jnp.int32, (1, TOK), 1)
        doc_start = jnp.zeros((1, TOK), jnp.int32)
        doc_end = 0
        for doc in range(DOCS):
            doc_end = doc_end + info_ref[1 + doc]
            doc_start = jnp.where(query_pos >= doc_end, doc_end, doc_start)
        key_pos = begin - BACK * TOK + lax.broadcasted_iota(jnp.int32, (WINDOW, TOK), 0)
        visible = (key_pos >= doc_start) & (key_pos <= query_pos)
        bias_ref[...] = jnp.where(visible, 0.0, MASKED)

    @pl.when(step == 0)
    def _():
        total_ref[...] = jnp.zeros_like(total_ref)
        for block in range(BLOCKS):
            window_ref[rows_of(block), :] = window_block(key_refs, block)

    queries = [stacked(query_ref, pair) for pair in range(STEP_PAIRS)]
    grads = [stacked(grad_ref, pair) for pair in range(STEP_PAIRS)]
    most, inverse = {}, {}

    def first(pair, part):
        rows = part_rows(part)
        bias = bias_ref[rows, :]
        scores = dot(window_ref[rows, :], queries[pair], NT) * (SCALE * LOG2E)
        scores = scores + jnp.concatenate([bias, bias], axis=1)
        score_refs[pair % 2][rows, :] = scores
        peak = jnp.max(scores.reshape(PART // 8, 8, 2 * TOK), axis=0)
        most[pair] = peak if part == 0 else jnp.maximum(most[pair], peak)

    def middle(pair):
        peak = jnp.max(most[pair], axis=0, keepdims=True)
        total = jnp.zeros((8, 2 * TOK), jnp.float32)
        for part in range(PARTS):
            numer = jnp.exp2(score_refs[pair % 2][part_rows(part), :] - peak)
            score_refs[pair % 2][part_rows(part), :] = numer
            total = total + jnp.sum(numer.reshape(PART // 8, 8, 2 * TOK), axis=0)
        total = jnp.sum(total, axis=0, keepdims=True)
        inverse[pair] = 1.0 / total

    def second(pair, part):
        rows = part_rows(part)
        probs = (score_refs[pair % 2][rows, :] * inverse[pair]).astype(jnp.bfloat16)
        probs_ref[pair, rows, :] = probs
        total_ref[rows, :] += dot(probs, grads[pair], NN)

    staggered(first, middle, second)

    @pl.when(step == STEPS - 1)
    def _():
        put_window(total_ref, given_ref, kept_ref, 1.0)


def put_window(total_ref, given_ref, kept_ref, factor):
    for block in range(BLOCKS):
        hop, odd = divmod(BACK - block, 2)
        if odd:
            given_ref[rows_of(hop), :] = (total_ref[rows_of(block), :] * factor).astype(jnp.bfloat16)
        else:
            kept_ref[rows_of(hop), :] = total_ref[rows_of(block), :] * factor


def grads_kernel(query_ref, grad_ref, probs_ref, *refs):
    key_refs, value_refs = refs[:6], refs[6:12]
    query_out_ref, given_ref, kept_ref, total_ref, window_ref, flip_ref = refs[-10:-4]
    dprobs_refs, dscores_refs = refs[-4:-2], refs[-2:]
    step = pl.program_id(1)

    @pl.when(step == 0)
    def _():
        total_ref[...] = jnp.zeros_like(total_ref)
        for block in range(BLOCKS):
            window_ref[rows_of(block), :] = window_block(value_refs, block)
            flip_ref[:, rows_of(block)] = window_block(key_refs, block).T

    queries = [stacked(query_ref, pair) for pair in range(STEP_PAIRS)]
    grads = [stacked(grad_ref, pair) for pair in range(STEP_PAIRS)]
    delta = {}

    def first(pair, part):
        rows = part_rows(part)
        dprobs = dot(window_ref[rows, :], grads[pair], NT)
        dprobs_refs[pair % 2][rows, :] = dprobs
        summed = jnp.sum((probs_ref[pair, rows, :].astype(jnp.float32) * dprobs).reshape(PART // 8, 8, 2 * TOK), axis=0)
        delta[pair] = summed if part == 0 else delta[pair] + summed

    def second(pair, part):
        rows = part_rows(part)
        if part == 0:
            delta[pair] = jnp.sum(delta[pair], axis=0, keepdims=True)
        probs = probs_ref[pair, rows, :].astype(jnp.float32)
        dscores = (probs * (dprobs_refs[pair % 2][rows, :] - delta[pair])).astype(jnp.bfloat16)
        dscores_refs[pair % 2][rows, :] = dscores
        total_ref[rows, :] += dot(dscores, queries[pair], NN)

    def finish(pair):
        flipped = dot(flip_ref[...], dscores_refs[pair % 2][...], NN) * SCALE
        for half in range(2):
            columns = slice((2 * pair + half) * HD, (2 * pair + half + 1) * HD)
            query_out_ref[:, columns] = flipped[:, half * TOK : (half + 1) * TOK].T.astype(jnp.bfloat16)

    staggered(first, None, second, finish)

    @pl.when(step == STEPS - 1)
    def _():
        put_window(total_ref, given_ref, kept_ref, SCALE)


def head_spec(first):
    return pl.BlockSpec((TOK, 2 * STEP_PAIRS * HD), lambda group, step: (0, (first + group) * STEPS + step))


def window_specs(first):
    return [pl.BlockSpec((rows, HD), lambda group, step: (0, first + group)) for rows in [TOK] * (HOPS + 1) + [HOPS * TOK]]


def sum_specs(first):
    return [pl.BlockSpec((rows, HD), lambda group, step: (0, first + group)) for rows in (HOPS * TOK, (HOPS + 1) * TOK)]


def probs_spec(first):
    return pl.BlockSpec((STEP_PAIRS, WINDOW, 2 * TOK), lambda group, step: ((first + group) * STEPS + step, 0, 0))


SUMS = [
    jax.ShapeDtypeStruct((HOPS * TOK, KV * HD), jnp.bfloat16),
    jax.ShapeDtypeStruct(((HOPS + 1) * TOK, KV * HD), jnp.float32),
]


def part_call(kernel, first, groups, operands, in_specs, out_shape, out_specs, scratch, earlier, cost):
    earlier = list(earlier or [])
    count = len(operands)
    return pl.pallas_call(
        kernel,
        grid=(groups, STEPS),
        in_specs=in_specs + [pl.BlockSpec(memory_space=pl.ANY)] * len(earlier),
        out_specs=out_specs,
        out_shape=out_shape,
        input_output_aliases={count + place: place for place in range(len(earlier))},
        scratch_shapes=scratch,
        compiler_params=pltpu.CompilerParams(vmem_limit_bytes=48 * 1024 * 1024),
        cost_estimate=cost,
    )(*operands, *earlier)


def probs_and_value_grad(first, groups, info, queries, grads, key_window, earlier=None):
    work = groups * GROUP * TOK * WINDOW
    return part_call(
        probs_kernel,
        first,
        groups,
        [info, queries, grads, *key_window],
        [pl.BlockSpec(memory_space=pltpu.SMEM), head_spec(first), head_spec(first)] + window_specs(first),
        [jax.ShapeDtypeStruct((HQ // 2, WINDOW, 2 * TOK), jnp.bfloat16)] + SUMS,
        [probs_spec(first)] + sum_specs(first),
        [
            pltpu.VMEM((WINDOW, TOK), jnp.float32),
            pltpu.VMEM((WINDOW, HD), jnp.float32),
            pltpu.VMEM((WINDOW, HD), jnp.bfloat16),
        ]
        + [pltpu.VMEM((WINDOW, 2 * TOK), jnp.float32)] * 2,
        earlier,
        pl.CostEstimate(flops=4 * work * HD, bytes_accessed=groups * (6 << 20), transcendentals=work),
    )


def query_and_key_grad(first, groups, queries, grads, probs, key_window, value_window, earlier=None):
    work = groups * GROUP * TOK * WINDOW
    return part_call(
        grads_kernel,
        first,
        groups,
        [queries, grads, probs, *key_window, *value_window],
        [head_spec(first), head_spec(first), probs_spec(first)] + window_specs(first) * 2,
        [jax.ShapeDtypeStruct((TOK, HQ * HD), jnp.bfloat16)] + SUMS,
        [head_spec(first)] + sum_specs(first),
        [
            pltpu.VMEM((WINDOW, HD), jnp.float32),
            pltpu.VMEM((WINDOW, HD), jnp.bfloat16),
            pltpu.VMEM((HD, WINDOW), jnp.bfloat16),
        ]
        + [pltpu.VMEM((WINDOW, 2 * TOK), jnp.float32)] * 2
        + [pltpu.VMEM((WINDOW, 2 * TOK), jnp.bfloat16)] * 2,
        earlier,
        pl.CostEstimate(flops=6 * work * HD, bytes_accessed=groups * (7 << 20), transcendentals=0),
    )


def quarter_columns(mine, offset, chip):
    start = (4 * chip + jnp.bitwise_xor(mine, offset)) * SLAB
    return pl.ds(pl.multiple_of(start, SLAB), SLAB)


def quarters_kernel(mine_ref, whole_ref, *quarter_refs):
    for offset, quarter_ref in enumerate(quarter_refs):
        for chip in range(CHIPS):
            quarter_ref[:, chip * SLAB : (chip + 1) * SLAB] = whole_ref[:, quarter_columns(mine_ref[0], offset, chip)]


def quarters_of(mine, whole):
    return pl.pallas_call(
        quarters_kernel,
        in_specs=[pl.BlockSpec(memory_space=pltpu.SMEM), pl.BlockSpec(memory_space=pltpu.VMEM)],
        out_specs=[pl.BlockSpec(memory_space=pltpu.VMEM)] * 4,
        out_shape=[jax.ShapeDtypeStruct((TOK, CHIPS * SLAB), jnp.bfloat16)] * 4,
        cost_estimate=pl.CostEstimate(flops=0, bytes_accessed=4 << 20, transcendentals=0),
    )(mine, whole)


def permuted(value, steps):
    count = lax.axis_size("fsdp")
    return lax.ppermute(value, "fsdp", [(source, (source + steps) % count) for source in range(count)])


def core_swapped(value):
    count = lax.axis_size("fsdp")
    return lax.ppermute(value, "fsdp", [(source, source ^ 1) for source in range(count)])


def quad_partner(value, offset, back=0):
    core, micro = offset // 2, offset % 2
    sections, places = lax.axis_size("pipe"), CHIPS * CORES
    moves = [
        (
            ((section * places) + place) * REPS + rep,
            (((section - back) * places) + (place ^ core)) * REPS + (rep ^ micro),
        )
        for section in range(back, sections)
        for place in range(places)
        for rep in range(REPS)
    ]
    return lax.ppermute(value, ("pipe", "fsdp", "rep"), moves)


def rounded(value):
    return value.astype(jnp.bfloat16)


def after(value, *earlier):
    return lax.optimization_barrier((value, earlier))[0]


def window_of(block, odd):
    own = [block]
    for hop in range(HOPS):
        own.append(permuted(own[-1], CORES))
    given = jnp.concatenate([lax.select(odd, own[hop + 1], own[hop]) for hop in range(HOPS)], axis=0)
    return own + [core_swapped(given)]


def chip_sums(given, kept, odd):
    taken = core_swapped(given).astype(jnp.float32).reshape(HOPS, TOK, -1)
    kept = kept.reshape(HOPS + 1, TOK, -1)
    none = jnp.zeros((1,) + taken.shape[1:], taken.dtype)
    kept = kept + lax.select(odd, jnp.concatenate([none, taken]), jnp.concatenate([taken, none]))
    return [kept[hop] for hop in range(HOPS)] + [rounded(kept[HOPS])]


def relayed_sum(sums, beside=()):
    total = sums[HOPS]
    for hop in reversed(range(HOPS)):
        total = after(total, *beside[HOPS - 1 - hop : HOPS - hop])
        total = rounded(sums[hop] + permuted(total, -CORES).astype(jnp.float32))
    return total


def shards(activations, query_rows, key_rows, out_grad, value_weight, doc_lengths):
    inputs = activations[0, 0]
    queries = query_rows[0, 0]
    keys = key_rows[0, 0]
    grads = out_grad[0, 0]
    weight_rows = value_weight[0]
    place = lax.axis_index("fsdp")
    core, micro = place % CORES, lax.axis_index("rep")
    odd = core == 1
    mine = (REPS * core + micro).reshape(1).astype(jnp.int32)
    info = jnp.concatenate([(place * TOK).reshape(1), doc_lengths[0]]).astype(jnp.int32)
    columns = [list(range(start, CHIPS * CORES, CORES)) for start in range(CORES)]

    weight = lax.all_gather(weight_rows, "fsdp", axis=0, tiled=True)
    quarters = quarters_of(mine, inputs)
    quad_inputs = [quarters[0]] + [quad_partner(quarters[offset], offset) for offset in range(1, 4)]
    key_window = window_of(after(keys, *quarters), odd)

    queries = after(queries, *quarters)
    probs, given, kept = probs_and_value_grad(0, KV, info, queries, grads, key_window)
    values = rounded(dot(inputs, after(weight, given), NN))
    value_window = window_of(values, odd)
    given = after(given, values, *quad_inputs[1:])
    value_grad = relayed_sum(chip_sums(given, kept, odd), value_window)

    moves = [(section, section - 1) for section in range(1, lax.axis_size("pipe"))]
    middle = weight.shape[0] * 3 // 4
    input_grads = [rounded(dot(value_grad, rows, NT)) for rows in (weight[:middle], weight[middle:])]
    upstreams = [lax.ppermute(part, "pipe", moves) for part in input_grads]
    upstream = jnp.concatenate(upstreams, axis=1)

    quad_grads = [value_grad] + [quad_partner(value_grad, offset) for offset in range(1, 4)]
    quad_grads = jnp.concatenate(after(quad_grads, *value_window[:HOPS], *input_grads), axis=0)
    weight_part = rounded(dot(jnp.concatenate(quad_inputs, axis=0), quad_grads, TN))
    weight_half = lax.psum_scatter(
        weight_part, "fsdp", scatter_dimension=0, tiled=True, axis_index_groups=columns
    )
    other_half = lax.ppermute(weight_half, "rep", [(0, 1), (1, 0)])
    first = lax.select(micro == 0, weight_half, other_half)
    second = lax.select(micro == 0, other_half, weight_half)
    weight_grad = jnp.concatenate([first, second], axis=0)

    queries = after(queries, weight_part)
    query_out, given, kept = query_and_key_grad(0, KV, queries, grads, probs, key_window, value_window)
    given = after(given, upstreams[0])
    key_grad = relayed_sum(chip_sums(given, kept, odd), [given] * (HOPS - 1) + [upstreams[1]])
    return (
        upstream[None, None],
        query_out[None, None],
        key_grad[None, None],
        weight_grad[None],
    )


def solution(mesh):
    tokens = P("pipe", "rep", "fsdp", None)
    weights = P("pipe", "fsdp", None)
    return jax.shard_map(
        shards,
        mesh=mesh,
        in_specs=(tokens, tokens, tokens, tokens, weights, P("rep", None)),
        out_specs=(tokens, tokens, tokens, weights),
        check_vma=False,
    )
```

time: 239 us -> 207 us (0.87); the launches traced: 236 us -> 207 us
  waiting for transfers between devices: 63.4 us -> 95.6 us
  starting transfers between devices: 54.1 us -> 30 us
  local copies, waits for them, and re-layouts: 18.1 us -> 1.72 us
  Pallas kernels: 59.1 us -> 45.8 us
  other arithmetic: 8.23 us -> 5.27 us
  matrix products: 17.1 us -> 14.3 us
    ppermute x16, starting transfers between devices: 45.3 us -> 19.4 us  [permuted(): lax.ppermute(value, 'fsdp', [(source, (source + steps) % count) for sourc...]
    ppermute x7 -> x8, waiting for transfers between devices: 0.02 us -> 21.3 us  [the longest x2 21.3 us: shards(): upstreams = [lax.ppermute(part, 'pipe', moves) for part in input_grads]]
    pallas_call x2 -> x3, Pallas kernels: 59.1 us -> 45.8 us  [the longest x2 42.6 us: part_call(): pl.pallas_call(kernel, grid=(groups, STEPS), in_specs=in_specs + [pl.Bloc...]
    unnamed x38 -> x12, local copies, waits for them, and re-layouts: 12.2 us -> 1.68 us
    all_gather x1, waiting for transfers between devices: 0.01 us -> 4.06 us  [shards(): weight = lax.all_gather(weight_rows, 'fsdp', axis=0, tiled=True)]
    ppermute x4, waiting for transfers between devices: 2 us -> 5.47 us  [core_swapped(): lax.ppermute(value, 'fsdp', [(source, source ^ 1) for source in range(cou...]
    transpose x1 -> x0, local copies, waits for them, and re-layouts: 3.13 us -> none  [inputs_in_quad(): inputs.reshape(TOK, chips, 2, 2, width).transpose(2, 3, 0, 1, 4)]
    dot_general x3 -> x4, matrix products: 17.1 us -> 14.3 us  [dot(): lax.dot_general(left, right, numbers, preferred_element_type=jnp.float32)]
  transfers between devices with their start and end apart: 30 -> 31, of which waited for: 14 -> 23; matrix products, arithmetic and copies ran while one was open for 15% -> 7% of each run, Pallas kernels for 25% -> 22%
where the time goes in v1:
time: 207 us
  waiting for transfers between devices  95.6 us (46%)
  Pallas kernels  45.8 us (22%)
  starting transfers between devices  30 us (14%)
  matrix products  14.3 us (7%)
  between operations  14.3 us (7%)
  other arithmetic  5.27 us (3%)
    ppermute x16, waiting for transfers between devices, permuted(): lax.ppermute(value, 'fsdp', [(source, (source + steps) % count) for sourc...  62.8 us
    pallas_call x2, Pallas kernels, part_call(): pl.pallas_call(kernel, grid=(groups, STEPS), in_specs=in_specs + [pl.Bloc...  42.6 us
    ppermute x2, waiting for transfers between devices, shards(): upstreams = [lax.ppermute(part, 'pipe', moves) for part in input_grads]  21.3 us
    ppermute x16, starting transfers between devices, permuted(): lax.ppermute(value, 'fsdp', [(source, (source + steps) % count) for sourc...  19.4 us
    dot_general x4, matrix products, dot(): lax.dot_general(left, right, numbers, preferred_element_type=jnp.float32)  14.3 us
    ppermute x4, waiting for transfers between devices, core_swapped(): lax.ppermute(value, 'fsdp', [(source, source ^ 1) for source in range(cou...  5.47 us
    ppermute x2, starting transfers between devices, shards(): upstreams = [lax.ppermute(part, 'pipe', moves) for part in input_grads]  4.63 us
    ppermute x6, starting transfers between devices, quad_partner(): return lax.ppermute(value, ('pipe', 'fsdp', 'rep'), moves)  4.45 us
  transfers between devices with their start and end apart: 31, of which 23 were waited for; matrix products, arithmetic and copies ran while one was open for 7% of the time, Pallas kernels for 22%

profile of v1, /device:TPU:14, one launch (start us, length us, event | category | flops | bytes accessed | tf_op | source)
XLA Modules:
  0.0 207.0 jit_solution(14899226135176832089)
XLA Ops:
  8.0 3.2 %shard_map.93 = (bf16[128,2048]{1,0:T(8,128)(2,1)}, bf16[128,2048]{1,0:T(8,128)(2,1)}, bf16[128,2048]{1,0:T(8,128)(2,1)}, bf16[128,2048]{1,0:T(8,128)(2,1)}) custom-call(s32[1]{0:T(128)} %bitcast.3.mine_ref, bf16[128,8192]{1,0:T(8,128)(2,1)} %bitcast.97), custom_call_target="tpu_custom_call" | custom-call | bytes 4194304 | tf_op jit(solution)/shard_map/pallas_call | solution.py:278
  11.2 1.9 collective-permute-start
  13.1 7.4 %collective-permute-done.refs_1_ = bf16[128,512]{1,0:T(8,128)(2,1)S(1)} collective-permute-done((bf16[128,512]{1,0:T(8,128)(2,1)S(1)}, bf16[128,512]{1,0:T(8,128)(2,1)S(1)}, u32[]{:S(2)}, u32[]{:S(2)}) %collective-permute-start) | collective-permute-done | bytes 131104 | tf_op jit(solution)/shard_map/ppermute | solution.py:289
  20.6 6.2 %collective-permute-done.1.refs_2_ = bf16[128,512]{1,0:T(8,128)(2,1)S(1)} collective-permute-done((bf16[128,512]{1,0:T(8,128)(2,1)S(1)}, bf16[128,512]{1,0:T(8,128)(2,1)S(1)}, u32[]{:S(2)}, u32[]{:S(2)}) %collective-permute-start.1) | collective-permute-done | bytes 131104 | tf_op jit(solution)/shard_map/ppermute | solution.py:289
  26.7 9.3 %collective-permute-done.2.refs_3_ = bf16[128,512]{1,0:T(8,128)(2,1)S(1)} collective-permute-done((bf16[128,512]{1,0:T(8,128)(2,1)S(1)}, bf16[128,512]{1,0:T(8,128)(2,1)S(1)}, u32[]{:S(2)}, u32[]{:S(2)}) %collective-permute-start.2) | collective-permute-done | bytes 131104 | tf_op jit(solution)/shard_map/ppermute | solution.py:289
  36.1 9.1 %collective-permute-done.3.refs_4_ = bf16[128,512]{1,0:T(8,128)(2,1)S(1)} collective-permute-done((bf16[128,512]{1,0:T(8,128)(2,1)S(1)}, bf16[128,512]{1,0:T(8,128)(2,1)S(1)}, u32[]{:S(2)}, u32[]{:S(2)}) %collective-permute-start.3) | collective-permute-done | bytes 131104 | tf_op jit(solution)/shard_map/ppermute | solution.py:289
  49.3 20.9 %shard_map.94 = (bf16[32,1152,256]{2,1,0:T(8,128)(2,1)}, bf16[512,512]{1,0:T(8,128)(2,1)S(1)}, f32[640,512]{1,0:T(8,128)S(1)}) custom-call(s32[5]{0:T(128)S(1)} %pad_add_fusion.info_ref, bf16[128,8192]{1,0:T(8,128)(2,1)S(1)} %bitcast.95, bf16[128,8192]{1,0:T(8,128)(2,1)} %bitcast.100, bf16[128,512]{1,0:T(8,128)(2,1)S(1)} %bitcast.92, ...), custom_call_target="tpu_custom_call" | custom-call | flops 4831838208 | bytes 25165824 | tf_op jit(solution)/shard_map/pallas_call | solution.py:210
  70.2 4.1 %all-gather.3.cloned.1.call-done = bf16[1,8192,512]{2,1,0:T(8,128)(2,1)} async-done(((bf16[1,512,512]{2,1,0:T(8,128)(2,1)}), bf16[1,8192,512]{2,1,0:T(8,128)(2,1)}) %all-gather.3.cloned.1.call-update) | async-done | bytes 8388624 | tf_op jit(solution)/shard_map/all_gather | solution.py:357
  74.2 5.4 %fusion.7.refs_6_ = bf16[128,512]{1,0:T(8,128)(2,1)S(1)} fusion(bf16[8192,512]{1,0:T(8,128)(2,1)} %bitcast.96, bf16[1,1,128,8192]{3,2,1,0:T(8,128)(2,1)} %param.6), kind=kOutput, calls=%fused_computation.16 | convolution fusion | flops 1073807360 | bytes 10616832 | tf_op jit(solution)/shard_map/dot_general | solution.py:37
  80.2 1.7 collective-permute-done.8
  84.4 3.6 %collective-permute-done.9 = bf16[128,512]{1,0:T(8,128)(2,1)S(1)} collective-permute-done((bf16[128,512]{1,0:T(8,128)(2,1)S(1)}, bf16[128,512]{1,0:T(8,128)(2,1)S(1)}, u32[]{:S(2)}, u32[]{:S(2)}) %collective-permute-start.9) | collective-permute-done | bytes 131104 | tf_op jit(solution)/shard_map/ppermute | solution.py:289
  91.4 2.9 %collective-permute-done.11 = bf16[128,512]{1,0:T(8,128)(2,1)S(1)} collective-permute-done((bf16[128,512]{1,0:T(8,128)(2,1)S(1)}, bf16[128,512]{1,0:T(8,128)(2,1)S(1)}, u32[]{:S(2)}, u32[]{:S(2)}) %collective-permute-start.11) | collective-permute-done | bytes 131104 | tf_op jit(solution)/shard_map/ppermute | solution.py:289
  98.0 2.9 %collective-permute-done.13 = bf16[128,512]{1,0:T(8,128)(2,1)S(1)} collective-permute-done((bf16[128,512]{1,0:T(8,128)(2,1)S(1)}, bf16[128,512]{1,0:T(8,128)(2,1)S(1)}, u32[]{:S(2)}, u32[]{:S(2)}) %collective-permute-start.13) | collective-permute-done | bytes 131104 | tf_op jit(solution)/shard_map/ppermute | solution.py:289
  101.0 1.7 collective-permute-done.14.refs_9_
  102.8 4.8 %collective-permute-done.15 = bf16[128,512]{1,0:T(8,128)(2,1)S(1)} collective-permute-done((bf16[128,512]{1,0:T(8,128)(2,1)S(1)}, bf16[128,512]{1,0:T(8,128)(2,1)S(1)}, u32[]{:S(2)}, u32[]{:S(2)}) %collective-permute-start.15) | collective-permute-done | bytes 131104 | tf_op jit(solution)/shard_map/ppermute | solution.py:289
  108.2 1.7 collective-permute-start.20
  109.9 3.3 %convolution_convert_fusion = bf16[128,6144]{1,0:T(8,128)(2,1)} fusion(bf16[128,512]{1,0:T(8,128)(2,1)S(1)} %fusion.30, bf16[1,8192,512]{2,1,0:T(8,128)(2,1)S(1)} %copy-done.2), kind=kOutput, calls=%fused_computation | convolution fusion | flops 806092800 | bytes 7995392 | tf_op jit(solution)/shard_map/dot_general | solution.py:37
  114.9 4.0 %convolution_convert_fusion.1 = bf16[2048,512]{1,0:T(8,128)(2,1)} fusion(bf16[128,2048]{1,0:T(8,128)(2,1)} %collective-permute-done.7, bf16[128,2048]{1,0:T(8,128)(2,1)} %collective-permute-done.6, bf16[128,2048]{1,0:T(8,128)(2,1)} %collective-permute-done.5, bf16[128,2048]{1,0:T(8,128)(2,1)S(1)} %copy-done.4, ...), kind=kOutput, calls=%fused_computation.2 | convolution fusion | flops 1085276160 | bytes 4718592 | tf_op jit(solution)/shard_map/dot_general | solution.py:37
  119.2 2.7 %collective-permute-start.16 = (bf16[128,6144]{1,0:T(8,128)(2,1)}, bf16[128,6144]{1,0:T(8,128)(2,1)S(1)}, u32[]{:S(2)}, u32[]{:S(2)}) collective-permute-start(bf16[128,6144]{1,0:T(8,128)(2,1)} %convolution_convert_fusion), channel_id=1, source_target_pairs={{32,0},{64,32},{96,64},{128,96},{160,128},{192,160},{224,192},{33,... | collective-permute-start | bytes 4718600 | tf_op jit(solution)/shard_map/ppermute | solution.py:372
  122.0 4.0 %collective-permute-done.21.refs_10_ = bf16[128,512]{1,0:T(8,128)(2,1)S(1)} collective-permute-done((bf16[128,512]{1,0:T(8,128)(2,1)S(1)}, bf16[128,512]{1,0:T(8,128)(2,1)S(1)}, u32[]{:S(2)}, u32[]{:S(2)}) %collective-permute-start.21) | collective-permute-done | bytes 131104 | tf_op jit(solution)/shard_map/ppermute | solution.py:289
  126.4 1.9 collective-permute-done.22.refs_11_
  128.3 21.7 %shard_map.95 = (bf16[128,8192]{1,0:T(8,128)(2,1)}, bf16[512,512]{1,0:T(8,128)(2,1)S(1)}, f32[640,512]{1,0:T(8,128)S(1)}) custom-call(bf16[128,8192]{1,0:T(8,128)(2,1)} %bitcast.94, bf16[128,8192]{1,0:T(8,128)(2,1)} %bitcast.101, bf16[32,1152,256]{2,1,0:T(8,128)(2,1)} %get-tuple-element.51.probs_ref, bf16[128,512]{1,0:T(8,128)(2,1)S(1)} %bitcast.93, ...), custom_call_target="tpu_custom_call" | custom-call | flops 7247757312 | bytes 29360128 | tf_op jit(solution)/shard_map/pallas_call | solution.py:210
  150.0 11.4 %collective-permute-done.16 = bf16[128,6144]{1,0:T(8,128)(2,1)S(1)} collective-permute-done((bf16[128,6144]{1,0:T(8,128)(2,1)}, bf16[128,6144]{1,0:T(8,128)(2,1)S(1)}, u32[]{:S(2)}, u32[]{:S(2)}) %collective-permute-start.16) | collective-permute-done | bytes 1572896 | tf_op jit(solution)/shard_map/ppermute | solution.py:372
  161.4 1.9 collective-permute-done.23
  163.7 3.0 %collective-permute-start.24 = (bf16[128,512]{1,0:T(8,128)(2,1)S(1)}, bf16[128,512]{1,0:T(8,128)(2,1)S(1)}, u32[]{:S(2)}, u32[]{:S(2)}) collective-permute-start(bf16[128,512]{1,0:T(8,128)(2,1)S(1)} %fusion.33), channel_id=1, source_target_pairs={{0,28},{2,30},{4,0},{6,2},{8,4},{10,6},{12,8},{14,10},{16,12},{18,... | collective-permute-start | bytes 393224 | tf_op jit(solution)/shard_map/ppermute | solution.py:289
  166.7 3.1 %collective-permute-done.24 = bf16[128,512]{1,0:T(8,128)(2,1)S(1)} collective-permute-done((bf16[128,512]{1,0:T(8,128)(2,1)S(1)}, bf16[128,512]{1,0:T(8,128)(2,1)S(1)}, u32[]{:S(2)}, u32[]{:S(2)}) %collective-permute-start.24) | collective-permute-done | bytes 131104 | tf_op jit(solution)/shard_map/ppermute | solution.py:289
  169.8 3.8 %collective-permute-start.25 = (bf16[128,512]{1,0:T(8,128)(2,1)S(1)}, bf16[128,512]{1,0:T(8,128)(2,1)S(1)}, u32[]{:S(2)}, u32[]{:S(2)}) collective-permute-start(bf16[128,512]{1,0:T(8,128)(2,1)S(1)} %fusion.16), channel_id=1, source_target_pairs={{0,28},{2,30},{4,0},{6,2},{8,4},{10,6},{12,8},{14,10},{16,12},{18,... | collective-permute-start | bytes 393224 | tf_op jit(solution)/shard_map/ppermute | solution.py:289
  173.6 1.9 collective-permute-start.17
  176.2 3.7 %collective-permute-start.26 = (bf16[128,512]{1,0:T(8,128)(2,1)S(1)}, bf16[128,512]{1,0:T(8,128)(2,1)S(1)}, u32[]{:S(2)}, u32[]{:S(2)}) collective-permute-start(bf16[128,512]{1,0:T(8,128)(2,1)S(1)} %fusion.18), channel_id=1, source_target_pairs={{0,28},{2,30},{4,0},{6,2},{8,4},{10,6},{12,8},{14,10},{16,12},{18,... | collective-permute-start | bytes 393224 | tf_op jit(solution)/shard_map/ppermute | solution.py:289
  179.9 2.5 %collective-permute-done.26 = bf16[128,512]{1,0:T(8,128)(2,1)S(1)} collective-permute-done((bf16[128,512]{1,0:T(8,128)(2,1)S(1)}, bf16[128,512]{1,0:T(8,128)(2,1)S(1)}, u32[]{:S(2)}, u32[]{:S(2)}) %collective-permute-start.26) | collective-permute-done | bytes 131104 | tf_op jit(solution)/shard_map/ppermute | solution.py:289
  182.4 9.9 %collective-permute-done.17 = bf16[128,2048]{1,0:T(8,128)(2,1)} collective-permute-done((bf16[128,2048]{1,0:T(8,128)(2,1)}, bf16[128,2048]{1,0:T(8,128)(2,1)}, u32[]{:S(2)}, u32[]{:S(2)}) %collective-permute-start.17) | collective-permute-done | bytes 524320 | tf_op jit(solution)/shard_map/ppermute | solution.py:372
  193.2 2.5 %maximum_bitcast_fusion = bf16[1,1,128,8192]{3,2,1,0:T(8,128)(2,1)} fusion(bf16[128,2048]{1,0:T(8,128)(2,1)} %collective-permute-done.17, bf16[128,6144]{1,0:T(8,128)(2,1)S(1)} %collective-permute-done.16), kind=kLoop, calls=%fused_computation.5 | loop fusion | flops 4194304 | bytes 4194304 | tf_op jit(solution)/shard_map/broadcast_in_dim | solution.py:391
  (73 shorter events, 24.5 us)
Async XLA Ops:
  7.2 67.0 %all-gather.3.cloned.1.call-start = ((), (), s32[]{:S(2)}) async-start(), calls=%async_computation.2 | async-start | bytes 8912896 | tf_op jit(solution)/shard_map/all_gather | solution.py:357
  7.9 184.8 %reduce-scatter.2.cloned.1.call-start = ((), (), s32[]{:S(2)}) async-start(), calls=%async_computation.1 | async-start | bytes 2359296 | tf_op jit(solution)/shard_map/reduce_scatter | solution.py:378
  8.0 39.6 %copy-start.5 = (s32[1,4]{1,0:T(1,128)S(1)}, s32[1,4]{1,0:T(1,128)}, u32[]{:S(2)}) copy-start(s32[1,4]{1,0:T(1,128)} %param.11) | copy-start | bytes 52
  11.2 9.4 %collective-permute-start = (bf16[128,512]{1,0:T(8,128)(2,1)S(1)}, bf16[128,512]{1,0:T(8,128)(2,1)S(1)}, u32[]{:S(2)}, u32[]{:S(2)}) collective-permute-start(bf16[128,512]{1,0:T(8,128)(2,1)S(1)} %bitcast.90), channel_id=1, source_target_pairs={{0,4},{2,6},{4,8},{6,10},{8,12},{10,14},{12,16},{14,18},{16,20},{1... | collective-permute-start | bytes 393224 | tf_op jit(solution)/shard_map/ppermute | solution.py:289
  20.6 6.2 %collective-permute-start.1 = (bf16[128,512]{1,0:T(8,128)(2,1)S(1)}, bf16[128,512]{1,0:T(8,128)(2,1)S(1)}, u32[]{:S(2)}, u32[]{:S(2)}) collective-permute-start(bf16[128,512]{1,0:T(8,128)(2,1)S(1)} %collective-permute-done.refs_1_), channel_id=1, source_target_pairs={{0,4},{2,6},{4,8},{6,10},{8,12},{10,14},{12,16},{14,18},{16,20},{1... | collective-permute-start | bytes 393224 | tf_op jit(solution)/shard_map/ppermute | solution.py:289
  26.7 9.3 %collective-permute-start.2 = (bf16[128,512]{1,0:T(8,128)(2,1)S(1)}, bf16[128,512]{1,0:T(8,128)(2,1)S(1)}, u32[]{:S(2)}, u32[]{:S(2)}) collective-permute-start(bf16[128,512]{1,0:T(8,128)(2,1)S(1)} %collective-permute-done.1.refs_2_), channel_id=1, source_target_pairs={{0,4},{2,6},{4,8},{6,10},{8,12},{10,14},{12,16},{14,18},{16,20},{1... | collective-permute-start | bytes 393224 | tf_op jit(solution)/shard_map/ppermute | solution.py:289
  36.1 9.1 %collective-permute-start.3 = (bf16[128,512]{1,0:T(8,128)(2,1)S(1)}, bf16[128,512]{1,0:T(8,128)(2,1)S(1)}, u32[]{:S(2)}, u32[]{:S(2)}) collective-permute-start(bf16[128,512]{1,0:T(8,128)(2,1)S(1)} %collective-permute-done.2.refs_3_), channel_id=1, source_target_pairs={{0,4},{2,6},{4,8},{6,10},{8,12},{10,14},{12,16},{14,18},{16,20},{1... | collective-permute-start | bytes 393224 | tf_op jit(solution)/shard_map/ppermute | solution.py:289
  45.2 2.4 %collective-permute-start.4 = (bf16[512,512]{1,0:T(8,128)(2,1)S(1)}, bf16[512,512]{1,0:T(8,128)(2,1)S(1)}, u32[]{:S(2)}, u32[]{:S(2)}) collective-permute-start(bf16[512,512]{1,0:T(8,128)(2,1)S(1)} %pad_maximum_fusion), channel_id=1, source_target_pairs={{0,2},{2,0},{4,6},{6,4},{8,10},{10,8},{12,14},{14,12},{16,18},{18,... | collective-permute-start | bytes 1572872 | tf_op jit(solution)/shard_map/ppermute | solution.py:294
  45.3 34.3 %collective-permute-start.5 = (bf16[128,2048]{1,0:T(8,128)(2,1)}, bf16[128,2048]{1,0:T(8,128)(2,1)}, u32[]{:S(2)}, u32[]{:S(2)}) collective-permute-start(bf16[128,2048]{1,0:T(8,128)(2,1)} %get-tuple-element.33), channel_id=1, source_target_pairs={{0,1},{1,0},{2,3},{3,2},{4,5},{5,4},{6,7},{7,6},{8,9},{9,8},{10,11... | collective-permute-start | bytes 1572872 | tf_op jit(solution)/shard_map/ppermute | solution.py:309
  45.8 33.8 %collective-permute-start.6 = (bf16[128,2048]{1,0:T(8,128)(2,1)}, bf16[128,2048]{1,0:T(8,128)(2,1)}, u32[]{:S(2)}, u32[]{:S(2)}) collective-permute-start(bf16[128,2048]{1,0:T(8,128)(2,1)} %get-tuple-element.34), channel_id=1, source_target_pairs={{0,2},{1,3},{2,0},{3,1},{4,6},{5,7},{6,4},{7,5},{8,10},{9,11},{10,... | collective-permute-start | bytes 1572872 | tf_op jit(solution)/shard_map/ppermute | solution.py:309
  46.0 33.7 %collective-permute-start.7 = (bf16[128,2048]{1,0:T(8,128)(2,1)}, bf16[128,2048]{1,0:T(8,128)(2,1)}, u32[]{:S(2)}, u32[]{:S(2)}) collective-permute-start(bf16[128,2048]{1,0:T(8,128)(2,1)} %get-tuple-element.35), channel_id=1, source_target_pairs={{0,3},{1,2},{2,1},{3,0},{4,7},{5,6},{6,5},{7,4},{8,11},{9,10},{10,... | collective-permute-start | bytes 1572872 | tf_op jit(solution)/shard_map/ppermute | solution.py:309
  79.7 2.2 %collective-permute-start.8 = (bf16[512,512]{1,0:T(8,128)(2,1)S(1)}, bf16[512,512]{1,0:T(8,128)(2,1)S(1)}, u32[]{:S(2)}, u32[]{:S(2)}) collective-permute-start(bf16[512,512]{1,0:T(8,128)(2,1)S(1)} %get-tuple-element.41), channel_id=1, source_target_pairs={{0,2},{2,0},{4,6},{6,4},{8,10},{10,8},{12,14},{14,12},{16,18},{18,... | collective-permute-start | bytes 1572872 | tf_op jit(solution)/shard_map/ppermute | solution.py:294
  82.3 5.7 %collective-permute-start.9 = (bf16[128,512]{1,0:T(8,128)(2,1)S(1)}, bf16[128,512]{1,0:T(8,128)(2,1)S(1)}, u32[]{:S(2)}, u32[]{:S(2)}) collective-permute-start(bf16[128,512]{1,0:T(8,128)(2,1)S(1)} %fusion.31), channel_id=1, source_target_pairs={{0,28},{2,30},{4,0},{6,2},{8,4},{10,6},{12,8},{14,10},{16,12},{18,... | collective-permute-start | bytes 393224 | tf_op jit(solution)/shard_map/ppermute | solution.py:289
  82.8 6.6 %collective-permute-start.10 = (bf16[128,512]{1,0:T(8,128)(2,1)S(1)}, bf16[128,512]{1,0:T(8,128)(2,1)S(1)}, u32[]{:S(2)}, u32[]{:S(2)}) collective-permute-start(bf16[128,512]{1,0:T(8,128)(2,1)S(1)} %fusion.7.refs_6_), channel_id=1, source_target_pairs={{0,4},{2,6},{4,8},{6,10},{8,12},{10,14},{12,16},{14,18},{16,20},{1... | collective-permute-start | bytes 393224 | tf_op jit(solution)/shard_map/ppermute | solution.py:289
  89.3 5.0 %collective-permute-start.11 = (bf16[128,512]{1,0:T(8,128)(2,1)S(1)}, bf16[128,512]{1,0:T(8,128)(2,1)S(1)}, u32[]{:S(2)}, u32[]{:S(2)}) collective-permute-start(bf16[128,512]{1,0:T(8,128)(2,1)S(1)} %fusion.24), channel_id=1, source_target_pairs={{0,28},{2,30},{4,0},{6,2},{8,4},{10,6},{12,8},{14,10},{16,12},{18,... | collective-permute-start | bytes 393224 | tf_op jit(solution)/shard_map/ppermute | solution.py:289
  89.8 6.2 %collective-permute-start.12 = (bf16[128,512]{1,0:T(8,128)(2,1)S(1)}, bf16[128,512]{1,0:T(8,128)(2,1)S(1)}, u32[]{:S(2)}, u32[]{:S(2)}) collective-permute-start(bf16[128,512]{1,0:T(8,128)(2,1)S(1)} %collective-permute-done.10.refs_7_), channel_id=1, source_target_pairs={{0,4},{2,6},{4,8},{6,10},{8,12},{10,14},{12,16},{14,18},{16,20},{1... | collective-permute-start | bytes 393224 | tf_op jit(solution)/shard_map/ppermute | solution.py:289
  96.0 5.0 %collective-permute-start.13 = (bf16[128,512]{1,0:T(8,128)(2,1)S(1)}, bf16[128,512]{1,0:T(8,128)(2,1)S(1)}, u32[]{:S(2)}, u32[]{:S(2)}) collective-permute-start(bf16[128,512]{1,0:T(8,128)(2,1)S(1)} %fusion.26), channel_id=1, source_target_pairs={{0,28},{2,30},{4,0},{6,2},{8,4},{10,6},{12,8},{14,10},{16,12},{18,... | collective-permute-start | bytes 393224 | tf_op jit(solution)/shard_map/ppermute | solution.py:289
  96.5 6.2 %collective-permute-start.14 = (bf16[128,512]{1,0:T(8,128)(2,1)S(1)}, bf16[128,512]{1,0:T(8,128)(2,1)S(1)}, u32[]{:S(2)}, u32[]{:S(2)}) collective-permute-start(bf16[128,512]{1,0:T(8,128)(2,1)S(1)} %collective-permute-done.12.refs_8_), channel_id=1, source_target_pairs={{0,4},{2,6},{4,8},{6,10},{8,12},{10,14},{12,16},{14,18},{16,20},{1... | collective-permute-start | bytes 393224 | tf_op jit(solution)/shard_map/ppermute | solution.py:289
  102.7 5.0 %collective-permute-start.15 = (bf16[128,512]{1,0:T(8,128)(2,1)S(1)}, bf16[128,512]{1,0:T(8,128)(2,1)S(1)}, u32[]{:S(2)}, u32[]{:S(2)}) collective-permute-start(bf16[128,512]{1,0:T(8,128)(2,1)S(1)} %fusion.28), channel_id=1, source_target_pairs={{0,28},{2,30},{4,0},{6,2},{8,4},{10,6},{12,8},{14,10},{16,12},{18,... | collective-permute-start | bytes 393224 | tf_op jit(solution)/shard_map/ppermute | solution.py:289
  107.7 7.1 %collective-permute-start.18 = (bf16[128,512]{1,0:T(8,128)(2,1)S(1)}, bf16[128,512]{1,0:T(8,128)(2,1)S(1)}, u32[]{:S(2)}, u32[]{:S(2)}) collective-permute-start(bf16[128,512]{1,0:T(8,128)(2,1)S(1)} %fusion.30), channel_id=1, source_target_pairs={{0,1},{1,0},{2,3},{3,2},{4,5},{5,4},{6,7},{7,6},{8,9},{9,8},{10,11... | collective-permute-start | bytes 393224 | tf_op jit(solution)/shard_map/ppermute | solution.py:309
  108.2 6.6 %collective-permute-start.19 = (bf16[128,512]{1,0:T(8,128)(2,1)S(1)}, bf16[128,512]{1,0:T(8,128)(2,1)S(1)}, u32[]{:S(2)}, u32[]{:S(2)}) collective-permute-start(bf16[128,512]{1,0:T(8,128)(2,1)S(1)} %fusion.30), channel_id=1, source_target_pairs={{0,2},{1,3},{2,0},{3,1},{4,6},{5,7},{6,4},{7,5},{8,10},{9,11},{10,... | collective-permute-start | bytes 393224 | tf_op jit(solution)/shard_map/ppermute | solution.py:309
  108.2 6.6 %collective-permute-start.20 = (bf16[128,512]{1,0:T(8,128)(2,1)S(1)}, bf16[128,512]{1,0:T(8,128)(2,1)S(1)}, u32[]{:S(2)}, u32[]{:S(2)}) collective-permute-start(bf16[128,512]{1,0:T(8,128)(2,1)S(1)} %fusion.30), channel_id=1, source_target_pairs={{0,3},{1,2},{2,1},{3,0},{4,7},{5,6},{6,5},{7,4},{8,11},{9,10},{10,... | collective-permute-start | bytes 393224 | tf_op jit(solution)/shard_map/ppermute | solution.py:309
  118.9 7.1 %collective-permute-start.21 = (bf16[128,512]{1,0:T(8,128)(2,1)S(1)}, bf16[128,512]{1,0:T(8,128)(2,1)S(1)}, u32[]{:S(2)}, u32[]{:S(2)}) collective-permute-start(bf16[128,512]{1,0:T(8,128)(2,1)S(1)} %collective-permute-done.14.refs_9_), channel_id=1, source_target_pairs={{0,4},{2,6},{4,8},{6,10},{8,12},{10,14},{12,16},{14,18},{16,20},{1... | collective-permute-start | bytes 393224 | tf_op jit(solution)/shard_map/ppermute | solution.py:289
  119.2 42.2 %collective-permute-start.16 = (bf16[128,6144]{1,0:T(8,128)(2,1)}, bf16[128,6144]{1,0:T(8,128)(2,1)S(1)}, u32[]{:S(2)}, u32[]{:S(2)}) collective-permute-start(bf16[128,6144]{1,0:T(8,128)(2,1)} %convolution_convert_fusion), channel_id=1, source_target_pairs={{32,0},{64,32},{96,64},{128,96},{160,128},{192,160},{224,192},{33,... | collective-permute-start | bytes 4718600 | tf_op jit(solution)/shard_map/ppermute | solution.py:372
  126.1 2.2 %collective-permute-start.22 = (bf16[512,512]{1,0:T(8,128)(2,1)S(1)}, bf16[512,512]{1,0:T(8,128)(2,1)S(1)}, u32[]{:S(2)}, u32[]{:S(2)}) collective-permute-start(bf16[512,512]{1,0:T(8,128)(2,1)S(1)} %pad_maximum_fusion.1), channel_id=1, source_target_pairs={{0,2},{2,0},{4,6},{6,4},{8,10},{10,8},{12,14},{14,12},{16,18},{18,... | collective-permute-start | bytes 1572872 | tf_op jit(solution)/shard_map/ppermute | solution.py:294
  161.4 1.9 collective-permute-start.23
  163.7 6.1 %collective-permute-start.24 = (bf16[128,512]{1,0:T(8,128)(2,1)S(1)}, bf16[128,512]{1,0:T(8,128)(2,1)S(1)}, u32[]{:S(2)}, u32[]{:S(2)}) collective-permute-start(bf16[128,512]{1,0:T(8,128)(2,1)S(1)} %fusion.33), channel_id=1, source_target_pairs={{0,28},{2,30},{4,0},{6,2},{8,4},{10,6},{12,8},{14,10},{16,12},{18,... | collective-permute-start | bytes 393224 | tf_op jit(solution)/shard_map/ppermute | solution.py:289
  169.8 6.3 %collective-permute-start.25 = (bf16[128,512]{1,0:T(8,128)(2,1)S(1)}, bf16[128,512]{1,0:T(8,128)(2,1)S(1)}, u32[]{:S(2)}, u32[]{:S(2)}) collective-permute-start(bf16[128,512]{1,0:T(8,128)(2,1)S(1)} %fusion.16), channel_id=1, source_target_pairs={{0,28},{2,30},{4,0},{6,2},{8,4},{10,6},{12,8},{14,10},{16,12},{18,... | collective-permute-start | bytes 393224 | tf_op jit(solution)/shard_map/ppermute | solution.py:289
  173.6 18.8 %collective-permute-start.17 = (bf16[128,2048]{1,0:T(8,128)(2,1)}, bf16[128,2048]{1,0:T(8,128)(2,1)}, u32[]{:S(2)}, u32[]{:S(2)}) collective-permute-start(bf16[128,2048]{1,0:T(8,128)(2,1)} %convolution_convert_fusion.2), channel_id=1, source_target_pairs={{32,0},{64,32},{96,64},{128,96},{160,128},{192,160},{224,192},{33,... | collective-permute-start | bytes 1572872 | tf_op jit(solution)/shard_map/ppermute | solution.py:372
  176.2 6.3 %collective-permute-start.26 = (bf16[128,512]{1,0:T(8,128)(2,1)S(1)}, bf16[128,512]{1,0:T(8,128)(2,1)S(1)}, u32[]{:S(2)}, u32[]{:S(2)}) collective-permute-start(bf16[128,512]{1,0:T(8,128)(2,1)S(1)} %fusion.18), channel_id=1, source_target_pairs={{0,28},{2,30},{4,0},{6,2},{8,4},{10,6},{12,8},{14,10},{16,12},{18,... | collective-permute-start | bytes 393224 | tf_op jit(solution)/shard_map/ppermute | solution.py:289
  192.4 5.0 %collective-permute-start.27 = (bf16[128,512]{1,0:T(8,128)(2,1)S(1)}, bf16[128,512]{1,0:T(8,128)(2,1)S(1)}, u32[]{:S(2)}, u32[]{:S(2)}) collective-permute-start(bf16[128,512]{1,0:T(8,128)(2,1)S(1)} %fusion.20), channel_id=1, source_target_pairs={{0,28},{2,30},{4,0},{6,2},{8,4},{10,6},{12,8},{14,10},{16,12},{18,... | collective-permute-start | bytes 393224 | tf_op jit(solution)/shard_map/ppermute | solution.py:289
  192.7 6.6 %collective-permute-start.28 = (bf16[256,512]{1,0:T(8,128)(2,1)}, bf16[256,512]{1,0:T(8,128)(2,1)S(1)}, u32[]{:S(2)}, u32[]{:S(2)}) collective-permute-start(bf16[256,512]{1,0:T(8,128)(2,1)} %reduce-scatter.2.cloned.1.call-done), channel_id=1, source_target_pairs={{0,1},{1,0},{2,3},{3,2},{4,5},{5,4},{6,7},{7,6},{8,9},{9,8},{10,11... | collective-permute-start | bytes 786440 | tf_op jit(solution)/shard_map/ppermute | solution.py:381
  (5 other events, 49.6 us)
Sparse Core Ops, SparseCore 0:
  9.8 64.3 all-gather.2
  119.0 40.7 reduce-scatter.1

commit v2 on v1

--- a/solution.py
+++ b/solution.py
@@ -317,10 +317,12 @@
     return lax.optimization_barrier((value, earlier))[0]
 
 
-def window_of(block, odd):
+def window_of(block, odd, beside=()):
     own = [block]
     for hop in range(HOPS):
         own.append(permuted(own[-1], CORES))
+        if hop == 0 and beside:
+            own[-1] = after(own[-1], *beside)
     given = jnp.concatenate([lax.select(odd, own[hop + 1], own[hop]) for hop in range(HOPS)], axis=0)
     return own + [core_swapped(given)]
 
@@ -335,9 +337,9 @@
 
 def relayed_sum(sums, beside=()):
     total = sums[HOPS]
-    for hop in reversed(range(HOPS)):
-        total = after(total, *beside[HOPS - 1 - hop : HOPS - hop])
-        total = rounded(sums[hop] + permuted(total, -CORES).astype(jnp.float32))
+    for step in range(HOPS):
+        arrived = after(permuted(total, -CORES), *beside[step : step + 1])
+        total = rounded(sums[HOPS - 1 - step] + arrived.astype(jnp.float32))
     return total
 
 
@@ -357,23 +359,20 @@
     weight = lax.all_gather(weight_rows, "fsdp", axis=0, tiled=True)
     quarters = quarters_of(mine, inputs)
     quad_inputs = [quarters[0]] + [quad_partner(quarters[offset], offset) for offset in range(1, 4)]
-    key_window = window_of(after(keys, *quarters), odd)
-
-    queries = after(queries, *quarters)
+    key_window = window_of(keys, odd, quarters)
+
     probs, given, kept = probs_and_value_grad(0, KV, info, queries, grads, key_window)
-    values = rounded(dot(inputs, after(weight, given), NN))
+    sums = chip_sums(after(given, *quad_inputs[1:]), kept, odd)
+    values = rounded(dot(inputs, after(weight, sums[HOPS]), NN))
     value_window = window_of(values, odd)
-    given = after(given, values, *quad_inputs[1:])
-    value_grad = relayed_sum(chip_sums(given, kept, odd), value_window)
+    value_grad = relayed_sum(sums, [values, *value_window[1:HOPS]])
 
     moves = [(section, section - 1) for section in range(1, lax.axis_size("pipe"))]
-    middle = weight.shape[0] * 3 // 4
-    input_grads = [rounded(dot(value_grad, rows, NT)) for rows in (weight[:middle], weight[middle:])]
-    upstreams = [lax.ppermute(part, "pipe", moves) for part in input_grads]
-    upstream = jnp.concatenate(upstreams, axis=1)
+    input_grad = rounded(dot(value_grad, weight, NT))
+    upstream = lax.ppermute(input_grad, "pipe", moves)
 
     quad_grads = [value_grad] + [quad_partner(value_grad, offset) for offset in range(1, 4)]
-    quad_grads = jnp.concatenate(after(quad_grads, *value_window[:HOPS], *input_grads), axis=0)
+    quad_grads = jnp.concatenate(after(quad_grads, *value_window, input_grad), axis=0)
     weight_part = rounded(dot(jnp.concatenate(quad_inputs, axis=0), quad_grads, TN))
     weight_half = lax.psum_scatter(
         weight_part, "fsdp", scatter_dimension=0, tiled=True, axis_index_groups=columns
@@ -383,10 +382,9 @@
     second = lax.select(micro == 0, other_half, weight_half)
     weight_grad = jnp.concatenate([first, second], axis=0)
 
-    queries = after(queries, weight_part)
+    value_window[0] = after(value_window[0], weight_part)
     query_out, given, kept = query_and_key_grad(0, KV, queries, grads, probs, key_window, value_window)
-    given = after(given, upstreams[0])
-    key_grad = relayed_sum(chip_sums(given, kept, odd), [given] * (HOPS - 1) + [upstreams[1]])
+    key_grad = relayed_sum(chip_sums(given, kept, odd), [given, upstream])
     return (
         upstream[None, None],
         query_out[None, None],

time: 207 us -> 194 us (0.937)
  starting transfers between devices: 30 us -> 23.1 us
  waiting for transfers between devices: 95.6 us -> 88.9 us
  local copies, waits for them, and re-layouts: 1.72 us -> 4.22 us
    ppermute x2 -> x1, waiting for transfers between devices: 21.3 us -> 12 us  [shards(): upstream = lax.ppermute(input_grad, 'pipe', moves)]
    ppermute x16, starting transfers between devices: 19.4 us -> 14.3 us  [permuted(): lax.ppermute(value, 'fsdp', [(source, (source + steps) % count) for sourc...]
    ppermute x16, waiting for transfers between devices: 62.8 us -> 67.2 us  [permuted(): lax.ppermute(value, 'fsdp', [(source, (source + steps) % count) for sourc...]
    all_gather x1, waiting for transfers between devices: 4.06 us -> 0.41 us  [shards(): weight = lax.all_gather(weight_rows, 'fsdp', axis=0, tiled=True)]
    broadcast_in_dim x1 -> x0, other arithmetic: 2.51 us -> none  [shards(): upstream[None, None]]
    unnamed x12 -> x23, local copies, waits for them, and re-layouts: 1.68 us -> 4.19 us
    ppermute x6, waiting for transfers between devices: 0.02 us -> 2.27 us  [quad_partner(): return lax.ppermute(value, ('pipe', 'fsdp', 'rep'), moves)]
    ppermute x4, waiting for transfers between devices: 5.47 us -> 3.4 us  [core_swapped(): lax.ppermute(value, 'fsdp', [(source, source ^ 1) for source in range(cou...]
  transfers between devices with their start and end apart: 31 -> 30, of which waited for: 23 -> 22; matrix products, arithmetic and copies ran while one was open for 7% -> 6% of each run, Pallas kernels for 22% -> 24%
where the time goes in v2:
time: 194 us
  waiting for transfers between devices  88.9 us (46%)
  Pallas kernels  46 us (24%)
  starting transfers between devices  23.1 us (12%)
  between operations  14.3 us (7%)
  matrix products  12.9 us (7%)
  other arithmetic  4.55 us (2%)
  local copies, waits for them, and re-layouts  4.22 us (2%)
    ppermute x16, waiting for transfers between devices, permuted(): lax.ppermute(value, 'fsdp', [(source, (source + steps) % count) for sourc...  67.2 us
    pallas_call x2, Pallas kernels, part_call(): pl.pallas_call(kernel, grid=(groups, STEPS), in_specs=in_specs + [pl.Bloc...  42.6 us
    ppermute x16, starting transfers between devices, permuted(): lax.ppermute(value, 'fsdp', [(source, (source + steps) % count) for sourc...  14.3 us
    dot_general x3, matrix products, dot(): lax.dot_general(left, right, numbers, preferred_element_type=jnp.float32)  12.9 us
    ppermute x1, waiting for transfers between devices, shards(): upstream = lax.ppermute(input_grad, 'pipe', moves)  12 us
    ppermute x6, starting transfers between devices, quad_partner(): return lax.ppermute(value, ('pipe', 'fsdp', 'rep'), moves)  4.37 us
    unnamed x23, local copies, waits for them, and re-layouts  4.19 us
  transfers between devices with their start and end apart: 30, of which 22 were waited for; matrix products, arithmetic and copies ran while one was open for 6% of the time, Pallas kernels for 24%

profile of v2, /device:TPU:14, one launch (start us, length us, event | category | flops | bytes accessed | tf_op | source)
XLA Modules:
  0.0 194.0 jit_solution(5701574029128703783)
XLA Ops:
  8.0 2.0 %collective-permute-start = (bf16[128,512]{1,0:T(8,128)(2,1)}, bf16[128,512]{1,0:T(8,128)(2,1)S(1)}, u32[]{:S(2)}, u32[]{:S(2)}) collective-permute-start(bf16[128,512]{1,0:T(8,128)(2,1)} %bitcast.85), channel_id=1, source_target_pairs={{0,4},{2,6},{4,8},{6,10},{8,12},{10,14},{12,16},{14,18},{16,20},{1... | collective-permute-start | bytes 393224 | tf_op jit(solution)/shard_map/ppermute | solution.py:289
  10.0 3.3 %shard_map.93 = (bf16[128,2048]{1,0:T(8,128)(2,1)}, bf16[128,2048]{1,0:T(8,128)(2,1)}, bf16[128,2048]{1,0:T(8,128)(2,1)}, bf16[128,2048]{1,0:T(8,128)(2,1)}) custom-call(s32[1]{0:T(128)} %bitcast.5.mine_ref, bf16[128,8192]{1,0:T(8,128)(2,1)} %bitcast.93), custom_call_target="tpu_custom_call" | custom-call | bytes 4194304 | tf_op jit(solution)/shard_map/pallas_call | solution.py:278
  13.3 4.3 %collective-permute-done.refs_1_ = bf16[128,512]{1,0:T(8,128)(2,1)S(1)} collective-permute-done((bf16[128,512]{1,0:T(8,128)(2,1)}, bf16[128,512]{1,0:T(8,128)(2,1)S(1)}, u32[]{:S(2)}, u32[]{:S(2)}) %collective-permute-start) | collective-permute-done | bytes 131104 | tf_op jit(solution)/shard_map/ppermute | solution.py:289
  17.6 6.2 %collective-permute-done.1.refs_2_ = bf16[128,512]{1,0:T(8,128)(2,1)S(1)} collective-permute-done((bf16[128,512]{1,0:T(8,128)(2,1)S(1)}, bf16[128,512]{1,0:T(8,128)(2,1)S(1)}, u32[]{:S(2)}, u32[]{:S(2)}) %collective-permute-start.1) | collective-permute-done | bytes 131104 | tf_op jit(solution)/shard_map/ppermute | solution.py:289
  23.8 9.2 %collective-permute-done.2.refs_3_ = bf16[128,512]{1,0:T(8,128)(2,1)S(1)} collective-permute-done((bf16[128,512]{1,0:T(8,128)(2,1)S(1)}, bf16[128,512]{1,0:T(8,128)(2,1)S(1)}, u32[]{:S(2)}, u32[]{:S(2)}) %collective-permute-start.2) | collective-permute-done | bytes 131104 | tf_op jit(solution)/shard_map/ppermute | solution.py:289
  33.0 9.0 %collective-permute-done.3.refs_4_ = bf16[128,512]{1,0:T(8,128)(2,1)S(1)} collective-permute-done((bf16[128,512]{1,0:T(8,128)(2,1)S(1)}, bf16[128,512]{1,0:T(8,128)(2,1)S(1)}, u32[]{:S(2)}, u32[]{:S(2)}) %collective-permute-start.3) | collective-permute-done | bytes 131104 | tf_op jit(solution)/shard_map/ppermute | solution.py:289
  45.1 21.0 %shard_map.94 = (bf16[32,1152,256]{2,1,0:T(8,128)(2,1)}, bf16[512,512]{1,0:T(8,128)(2,1)S(1)}, f32[640,512]{1,0:T(8,128)S(1)}) custom-call(s32[5]{0:T(128)S(1)} %pad_add_fusion.info_ref, bf16[128,8192]{1,0:T(8,128)(2,1)S(1)} %bitcast.89, bf16[128,8192]{1,0:T(8,128)(2,1)} %bitcast.96, bf16[128,512]{1,0:T(8,128)(2,1)S(1)} %bitcast.86, ...), custom_call_target="tpu_custom_call" | custom-call | flops 4831838208 | bytes 25165824 | tf_op jit(solution)/shard_map/pallas_call | solution.py:210
  66.1 2.3 %collective-permute-done.7 = bf16[128,2048]{1,0:T(8,128)(2,1)} collective-permute-done((bf16[128,2048]{1,0:T(8,128)(2,1)}, bf16[128,2048]{1,0:T(8,128)(2,1)}, u32[]{:S(2)}, u32[]{:S(2)}) %collective-permute-start.7) | collective-permute-done | bytes 524320 | tf_op jit(solution)/shard_map/ppermute | solution.py:309
  68.9 1.7 collective-permute-done.8
  72.8 4.8 %fusion.7.refs_6_ = bf16[128,512]{1,0:T(8,128)(2,1)S(1)} fusion(bf16[8192,512]{1,0:T(8,128)(2,1)} %bitcast.90, bf16[1,1,128,8192]{3,2,1,0:T(8,128)(2,1)S(1)} %copy-done.4), kind=kOutput, calls=%fused_computation.12 | convolution fusion | flops 1073807360 | bytes 10616832 | tf_op jit(solution)/shard_map/dot_general | solution.py:37
  78.2 1.6 collective-permute-start.10
  80.3 3.2 %collective-permute-done.10 = bf16[128,512]{1,0:T(8,128)(2,1)S(1)} collective-permute-done((bf16[128,512]{1,0:T(8,128)(2,1)S(1)}, bf16[128,512]{1,0:T(8,128)(2,1)S(1)}, u32[]{:S(2)}, u32[]{:S(2)}) %collective-permute-start.10) | collective-permute-done | bytes 131104 | tf_op jit(solution)/shard_map/ppermute | solution.py:289
  83.5 2.4 %collective-permute-done.11.refs_7_ = bf16[128,512]{1,0:T(8,128)(2,1)S(1)} collective-permute-done((bf16[128,512]{1,0:T(8,128)(2,1)S(1)}, bf16[128,512]{1,0:T(8,128)(2,1)S(1)}, u32[]{:S(2)}, u32[]{:S(2)}) %collective-permute-start.11) | collective-permute-done | bytes 131104 | tf_op jit(solution)/shard_map/ppermute | solution.py:289
  88.1 2.9 %collective-permute-done.12 = bf16[128,512]{1,0:T(8,128)(2,1)S(1)} collective-permute-done((bf16[128,512]{1,0:T(8,128)(2,1)S(1)}, bf16[128,512]{1,0:T(8,128)(2,1)S(1)}, u32[]{:S(2)}, u32[]{:S(2)}) %collective-permute-start.12) | collective-permute-done | bytes 131104 | tf_op jit(solution)/shard_map/ppermute | solution.py:289
  91.0 1.8 collective-permute-done.13.refs_8_
  95.0 2.9 %collective-permute-done.14 = bf16[128,512]{1,0:T(8,128)(2,1)S(1)} collective-permute-done((bf16[128,512]{1,0:T(8,128)(2,1)S(1)}, bf16[128,512]{1,0:T(8,128)(2,1)S(1)}, u32[]{:S(2)}, u32[]{:S(2)}) %collective-permute-start.14) | collective-permute-done | bytes 131104 | tf_op jit(solution)/shard_map/ppermute | solution.py:289
  97.9 1.7 collective-permute-done.15.refs_9_
  101.4 2.0 %collective-permute-start.19 = (bf16[128,512]{1,0:T(8,128)(2,1)S(1)}, bf16[128,512]{1,0:T(8,128)(2,1)S(1)}, u32[]{:S(2)}, u32[]{:S(2)}) collective-permute-start(bf16[128,512]{1,0:T(8,128)(2,1)S(1)} %fusion.30), channel_id=1, source_target_pairs={{0,3},{1,2},{2,1},{3,0},{4,7},{5,6},{6,5},{7,4},{8,11},{9,10},{10,... | collective-permute-start | bytes 393224 | tf_op jit(solution)/shard_map/ppermute | solution.py:309
  103.3 2.5 %collective-permute-done.20.refs_10_ = bf16[128,512]{1,0:T(8,128)(2,1)S(1)} collective-permute-done((bf16[128,512]{1,0:T(8,128)(2,1)S(1)}, bf16[128,512]{1,0:T(8,128)(2,1)S(1)}, u32[]{:S(2)}, u32[]{:S(2)}) %collective-permute-start.20) | collective-permute-done | bytes 131104 | tf_op jit(solution)/shard_map/ppermute | solution.py:289
  106.1 4.1 %convolution_convert_fusion = bf16[128,8192]{1,0:T(8,128)(2,1)} fusion(bf16[128,512]{1,0:T(8,128)(2,1)S(1)} %fusion.30, bf16[1,8192,512]{2,1,0:T(8,128)(2,1)S(1)} %bitcast.92), kind=kOutput, calls=%fused_computation | convolution fusion | flops 1074790400 | bytes 10616832 | tf_op jit(solution)/shard_map/dot_general | solution.py:37
  110.3 4.0 %convolution_convert_fusion.1 = bf16[2048,512]{1,0:T(8,128)(2,1)} fusion(bf16[128,2048]{1,0:T(8,128)(2,1)} %collective-permute-done.7, bf16[128,2048]{1,0:T(8,128)(2,1)} %collective-permute-done.6, bf16[128,2048]{1,0:T(8,128)(2,1)} %collective-permute-done.5, bf16[128,2048]{1,0:T(8,128)(2,1)S(1)} %copy-done.7, ...), kind=kOutput, calls=%fused_computation.1 | convolution fusion | flops 1085276160 | bytes 4718592 | tf_op jit(solution)/shard_map/dot_general | solution.py:37
  114.3 3.1 %collective-permute-start.16 = (bf16[128,8192]{1,0:T(8,128)(2,1)}, bf16[128,8192]{1,0:T(8,128)(2,1)}, u32[]{:S(2)}, u32[]{:S(2)}) collective-permute-start(bf16[128,8192]{1,0:T(8,128)(2,1)} %convolution_convert_fusion), channel_id=1, source_target_pairs={{32,0},{64,32},{96,64},{128,96},{160,128},{192,160},{224,192},{33,... | collective-permute-start | bytes 6291464 | tf_op jit(solution)/shard_map/ppermute | solution.py:372
  117.4 21.6 %shard_map.95 = (bf16[128,8192]{1,0:T(8,128)(2,1)}, bf16[512,512]{1,0:T(8,128)(2,1)S(1)}, f32[640,512]{1,0:T(8,128)S(1)}) custom-call(bf16[128,8192]{1,0:T(8,128)(2,1)} %bitcast.88, bf16[128,8192]{1,0:T(8,128)(2,1)} %bitcast.97, bf16[32,1152,256]{2,1,0:T(8,128)(2,1)} %get-tuple-element.41.probs_ref, bf16[128,512]{1,0:T(8,128)(2,1)S(1)} %bitcast.87, ...), custom_call_target="tpu_custom_call" | custom-call | flops 7247757312 | bytes 29360128 | tf_op jit(solution)/shard_map/pallas_call | solution.py:210
  139.2 1.7 collective-permute-done.22
  141.6 7.8 %collective-permute-done.23 = bf16[128,512]{1,0:T(8,128)(2,1)S(1)} collective-permute-done((bf16[128,512]{1,0:T(8,128)(2,1)S(1)}, bf16[128,512]{1,0:T(8,128)(2,1)S(1)}, u32[]{:S(2)}, u32[]{:S(2)}) %collective-permute-start.23) | collective-permute-done | bytes 131104 | tf_op jit(solution)/shard_map/ppermute | solution.py:289
  149.4 2.3 %collective-permute-start.24 = (bf16[128,512]{1,0:T(8,128)(2,1)S(1)}, bf16[128,512]{1,0:T(8,128)(2,1)S(1)}, u32[]{:S(2)}, u32[]{:S(2)}) collective-permute-start(bf16[128,512]{1,0:T(8,128)(2,1)S(1)} %fusion.16), channel_id=1, source_target_pairs={{0,28},{2,30},{4,0},{6,2},{8,4},{10,6},{12,8},{14,10},{16,12},{18,... | collective-permute-start | bytes 393224 | tf_op jit(solution)/shard_map/ppermute | solution.py:289
  151.7 4.6 %collective-permute-done.24 = bf16[128,512]{1,0:T(8,128)(2,1)S(1)} collective-permute-done((bf16[128,512]{1,0:T(8,128)(2,1)S(1)}, bf16[128,512]{1,0:T(8,128)(2,1)S(1)}, u32[]{:S(2)}, u32[]{:S(2)}) %collective-permute-start.24) | collective-permute-done | bytes 131104 | tf_op jit(solution)/shard_map/ppermute | solution.py:289
  156.3 12.0 %collective-permute-done.16 = bf16[128,8192]{1,0:T(8,128)(2,1)} collective-permute-done((bf16[128,8192]{1,0:T(8,128)(2,1)}, bf16[128,8192]{1,0:T(8,128)(2,1)}, u32[]{:S(2)}, u32[]{:S(2)}) %collective-permute-start.16) | collective-permute-done | bytes 2097184 | tf_op jit(solution)/shard_map/ppermute | solution.py:372
  168.5 5.0 %collective-permute-done.25 = bf16[128,512]{1,0:T(8,128)(2,1)S(1)} collective-permute-done((bf16[128,512]{1,0:T(8,128)(2,1)S(1)}, bf16[128,512]{1,0:T(8,128)(2,1)S(1)}, u32[]{:S(2)}, u32[]{:S(2)}) %collective-permute-start.25) | collective-permute-done | bytes 131104 | tf_op jit(solution)/shard_map/ppermute | solution.py:289
  175.6 3.0 %collective-permute-done.26 = bf16[128,512]{1,0:T(8,128)(2,1)S(1)} collective-permute-done((bf16[128,512]{1,0:T(8,128)(2,1)S(1)}, bf16[128,512]{1,0:T(8,128)(2,1)S(1)}, u32[]{:S(2)}, u32[]{:S(2)}) %collective-permute-start.26) | collective-permute-done | bytes 131104 | tf_op jit(solution)/shard_map/ppermute | solution.py:289
  179.2 3.0 %collective-permute-done.27 = bf16[256,512]{1,0:T(8,128)(2,1)S(1)} collective-permute-done((bf16[256,512]{1,0:T(8,128)(2,1)}, bf16[256,512]{1,0:T(8,128)(2,1)S(1)}, u32[]{:S(2)}, u32[]{:S(2)}) %collective-permute-start.27) | collective-permute-done | bytes 262176 | tf_op jit(solution)/shard_map/ppermute | solution.py:380
  184.0 3.1 %copy.11 = bf16[1,1,128,8192]{3,2,1,0:T(8,128)(2,1)} copy(bf16[1,1,128,8192]{3,2,1,0:T(8,128)(2,1)} %bitcast.17) | data formatting | bytes 4194304
  (81 shorter events, 19.5 us)
Async XLA Ops:
  7.2 65.6 %all-gather.3.cloned.1.call-start = ((), (), s32[]{:S(2)}) async-start(), calls=%async_computation.2 | async-start | bytes 8912896 | tf_op jit(solution)/shard_map/all_gather | solution.py:359
  7.9 167.2 %reduce-scatter.2.cloned.1.call-start = ((), (), s32[]{:S(2)}) async-start(), calls=%async_computation.1 | async-start | bytes 2359296 | tf_op jit(solution)/shard_map/reduce_scatter | solution.py:377
  8.0 9.6 %collective-permute-start = (bf16[128,512]{1,0:T(8,128)(2,1)}, bf16[128,512]{1,0:T(8,128)(2,1)S(1)}, u32[]{:S(2)}, u32[]{:S(2)}) collective-permute-start(bf16[128,512]{1,0:T(8,128)(2,1)} %bitcast.85), channel_id=1, source_target_pairs={{0,4},{2,6},{4,8},{6,10},{8,12},{10,14},{12,16},{14,18},{16,20},{1... | collective-permute-start | bytes 393224 | tf_op jit(solution)/shard_map/ppermute | solution.py:289
  9.9 35.1 %copy-start.8 = (s32[1,4]{1,0:T(1,128)S(1)}, s32[1,4]{1,0:T(1,128)}, u32[]{:S(2)}) copy-start(s32[1,4]{1,0:T(1,128)} %param.11) | copy-start | bytes 52
  10.0 35.1 %copy-start.1 = (bf16[1,1,128,8192]{3,2,1,0:T(8,128)(2,1)S(1)}, bf16[1,1,128,8192]{3,2,1,0:T(8,128)(2,1)}, u32[]{:S(2)}) copy-start(bf16[1,1,128,8192]{3,2,1,0:T(8,128)(2,1)} %param.7) | copy-start | bytes 6291460
  17.6 6.2 %collective-permute-start.1 = (bf16[128,512]{1,0:T(8,128)(2,1)S(1)}, bf16[128,512]{1,0:T(8,128)(2,1)S(1)}, u32[]{:S(2)}, u32[]{:S(2)}) collective-permute-start(bf16[128,512]{1,0:T(8,128)(2,1)S(1)} %collective-permute-done.refs_1_), channel_id=1, source_target_pairs={{0,4},{2,6},{4,8},{6,10},{8,12},{10,14},{12,16},{14,18},{16,20},{1... | collective-permute-start | bytes 393224 | tf_op jit(solution)/shard_map/ppermute | solution.py:289
  23.8 9.2 %collective-permute-start.2 = (bf16[128,512]{1,0:T(8,128)(2,1)S(1)}, bf16[128,512]{1,0:T(8,128)(2,1)S(1)}, u32[]{:S(2)}, u32[]{:S(2)}) collective-permute-start(bf16[128,512]{1,0:T(8,128)(2,1)S(1)} %collective-permute-done.1.refs_2_), channel_id=1, source_target_pairs={{0,4},{2,6},{4,8},{6,10},{8,12},{10,14},{12,16},{14,18},{16,20},{1... | collective-permute-start | bytes 393224 | tf_op jit(solution)/shard_map/ppermute | solution.py:289
  33.0 9.0 %collective-permute-start.3 = (bf16[128,512]{1,0:T(8,128)(2,1)S(1)}, bf16[128,512]{1,0:T(8,128)(2,1)S(1)}, u32[]{:S(2)}, u32[]{:S(2)}) collective-permute-start(bf16[128,512]{1,0:T(8,128)(2,1)S(1)} %collective-permute-done.2.refs_3_), channel_id=1, source_target_pairs={{0,4},{2,6},{4,8},{6,10},{8,12},{10,14},{12,16},{14,18},{16,20},{1... | collective-permute-start | bytes 393224 | tf_op jit(solution)/shard_map/ppermute | solution.py:289
  42.9 2.2 %collective-permute-start.4 = (bf16[512,512]{1,0:T(8,128)(2,1)}, bf16[512,512]{1,0:T(8,128)(2,1)S(1)}, u32[]{:S(2)}, u32[]{:S(2)}) collective-permute-start(bf16[512,512]{1,0:T(8,128)(2,1)} %pad_maximum_fusion), channel_id=1, source_target_pairs={{0,2},{2,0},{4,6},{6,4},{8,10},{10,8},{12,14},{14,12},{16,18},{18,... | collective-permute-start | bytes 1572872 | tf_op jit(solution)/shard_map/ppermute | solution.py:294
  42.9 23.2 %collective-permute-start.5 = (bf16[128,2048]{1,0:T(8,128)(2,1)}, bf16[128,2048]{1,0:T(8,128)(2,1)}, u32[]{:S(2)}, u32[]{:S(2)}) collective-permute-start(bf16[128,2048]{1,0:T(8,128)(2,1)} %get-tuple-element.29), channel_id=1, source_target_pairs={{0,1},{1,0},{2,3},{3,2},{4,5},{5,4},{6,7},{7,6},{8,9},{9,8},{10,11... | collective-permute-start | bytes 1572872 | tf_op jit(solution)/shard_map/ppermute | solution.py:309
  43.3 22.8 %collective-permute-start.6 = (bf16[128,2048]{1,0:T(8,128)(2,1)}, bf16[128,2048]{1,0:T(8,128)(2,1)}, u32[]{:S(2)}, u32[]{:S(2)}) collective-permute-start(bf16[128,2048]{1,0:T(8,128)(2,1)} %get-tuple-element.30), channel_id=1, source_target_pairs={{0,2},{1,3},{2,0},{3,1},{4,6},{5,7},{6,4},{7,5},{8,10},{9,11},{10,... | collective-permute-start | bytes 1572872 | tf_op jit(solution)/shard_map/ppermute | solution.py:309
  43.5 24.8 %collective-permute-start.7 = (bf16[128,2048]{1,0:T(8,128)(2,1)}, bf16[128,2048]{1,0:T(8,128)(2,1)}, u32[]{:S(2)}, u32[]{:S(2)}) collective-permute-start(bf16[128,2048]{1,0:T(8,128)(2,1)} %get-tuple-element.31), channel_id=1, source_target_pairs={{0,3},{1,2},{2,1},{3,0},{4,7},{5,6},{6,5},{7,4},{8,11},{9,10},{10,... | collective-permute-start | bytes 1572872 | tf_op jit(solution)/shard_map/ppermute | solution.py:309
  68.4 2.2 %collective-permute-start.8 = (bf16[512,512]{1,0:T(8,128)(2,1)S(1)}, bf16[512,512]{1,0:T(8,128)(2,1)S(1)}, u32[]{:S(2)}, u32[]{:S(2)}) collective-permute-start(bf16[512,512]{1,0:T(8,128)(2,1)S(1)} %get-tuple-element.35), channel_id=1, source_target_pairs={{0,2},{2,0},{4,6},{6,4},{8,10},{10,8},{12,14},{14,12},{16,18},{18,... | collective-permute-start | bytes 1572872 | tf_op jit(solution)/shard_map/ppermute | solution.py:294
  72.1 6.0 %collective-permute-start.9 = (bf16[128,512]{1,0:T(8,128)(2,1)S(1)}, bf16[128,512]{1,0:T(8,128)(2,1)S(1)}, u32[]{:S(2)}, u32[]{:S(2)}) collective-permute-start(bf16[128,512]{1,0:T(8,128)(2,1)S(1)} %fusion.31), channel_id=1, source_target_pairs={{0,28},{2,30},{4,0},{6,2},{8,4},{10,6},{12,8},{14,10},{16,12},{18,... | collective-permute-start | bytes 393224 | tf_op jit(solution)/shard_map/ppermute | solution.py:289
  78.2 5.3 %collective-permute-start.10 = (bf16[128,512]{1,0:T(8,128)(2,1)S(1)}, bf16[128,512]{1,0:T(8,128)(2,1)S(1)}, u32[]{:S(2)}, u32[]{:S(2)}) collective-permute-start(bf16[128,512]{1,0:T(8,128)(2,1)S(1)} %fusion.24), channel_id=1, source_target_pairs={{0,28},{2,30},{4,0},{6,2},{8,4},{10,6},{12,8},{14,10},{16,12},{18,... | collective-permute-start | bytes 393224 | tf_op jit(solution)/shard_map/ppermute | solution.py:289
  79.8 6.2 %collective-permute-start.11 = (bf16[128,512]{1,0:T(8,128)(2,1)S(1)}, bf16[128,512]{1,0:T(8,128)(2,1)S(1)}, u32[]{:S(2)}, u32[]{:S(2)}) collective-permute-start(bf16[128,512]{1,0:T(8,128)(2,1)S(1)} %fusion.7.refs_6_), channel_id=1, source_target_pairs={{0,4},{2,6},{4,8},{6,10},{8,12},{10,14},{12,16},{14,18},{16,20},{1... | collective-permute-start | bytes 393224 | tf_op jit(solution)/shard_map/ppermute | solution.py:289
  86.0 5.0 %collective-permute-start.12 = (bf16[128,512]{1,0:T(8,128)(2,1)S(1)}, bf16[128,512]{1,0:T(8,128)(2,1)S(1)}, u32[]{:S(2)}, u32[]{:S(2)}) collective-permute-start(bf16[128,512]{1,0:T(8,128)(2,1)S(1)} %fusion.26), channel_id=1, source_target_pairs={{0,28},{2,30},{4,0},{6,2},{8,4},{10,6},{12,8},{14,10},{16,12},{18,... | collective-permute-start | bytes 393224 | tf_op jit(solution)/shard_map/ppermute | solution.py:289
  86.7 6.2 %collective-permute-start.13 = (bf16[128,512]{1,0:T(8,128)(2,1)S(1)}, bf16[128,512]{1,0:T(8,128)(2,1)S(1)}, u32[]{:S(2)}, u32[]{:S(2)}) collective-permute-start(bf16[128,512]{1,0:T(8,128)(2,1)S(1)} %collective-permute-done.11.refs_7_), channel_id=1, source_target_pairs={{0,4},{2,6},{4,8},{6,10},{8,12},{10,14},{12,16},{14,18},{16,20},{1... | collective-permute-start | bytes 393224 | tf_op jit(solution)/shard_map/ppermute | solution.py:289
  92.9 5.0 %collective-permute-start.14 = (bf16[128,512]{1,0:T(8,128)(2,1)S(1)}, bf16[128,512]{1,0:T(8,128)(2,1)S(1)}, u32[]{:S(2)}, u32[]{:S(2)}) collective-permute-start(bf16[128,512]{1,0:T(8,128)(2,1)S(1)} %fusion.28), channel_id=1, source_target_pairs={{0,28},{2,30},{4,0},{6,2},{8,4},{10,6},{12,8},{14,10},{16,12},{18,... | collective-permute-start | bytes 393224 | tf_op jit(solution)/shard_map/ppermute | solution.py:289
  93.5 6.2 %collective-permute-start.15 = (bf16[128,512]{1,0:T(8,128)(2,1)S(1)}, bf16[128,512]{1,0:T(8,128)(2,1)S(1)}, u32[]{:S(2)}, u32[]{:S(2)}) collective-permute-start(bf16[128,512]{1,0:T(8,128)(2,1)S(1)} %collective-permute-done.13.refs_8_), channel_id=1, source_target_pairs={{0,4},{2,6},{4,8},{6,10},{8,12},{10,14},{12,16},{14,18},{16,20},{1... | collective-permute-start | bytes 393224 | tf_op jit(solution)/shard_map/ppermute | solution.py:289
  99.7 6.2 %collective-permute-start.20 = (bf16[128,512]{1,0:T(8,128)(2,1)S(1)}, bf16[128,512]{1,0:T(8,128)(2,1)S(1)}, u32[]{:S(2)}, u32[]{:S(2)}) collective-permute-start(bf16[128,512]{1,0:T(8,128)(2,1)S(1)} %collective-permute-done.15.refs_9_), channel_id=1, source_target_pairs={{0,4},{2,6},{4,8},{6,10},{8,12},{10,14},{12,16},{14,18},{16,20},{1... | collective-permute-start | bytes 393224 | tf_op jit(solution)/shard_map/ppermute | solution.py:289
  101.1 9.1 %collective-permute-start.17 = (bf16[128,512]{1,0:T(8,128)(2,1)S(1)}, bf16[128,512]{1,0:T(8,128)(2,1)S(1)}, u32[]{:S(2)}, u32[]{:S(2)}) collective-permute-start(bf16[128,512]{1,0:T(8,128)(2,1)S(1)} %fusion.30), channel_id=1, source_target_pairs={{0,1},{1,0},{2,3},{3,2},{4,5},{5,4},{6,7},{7,6},{8,9},{9,8},{10,11... | collective-permute-start | bytes 393224 | tf_op jit(solution)/shard_map/ppermute | solution.py:309
  101.4 8.9 %collective-permute-start.18 = (bf16[128,512]{1,0:T(8,128)(2,1)S(1)}, bf16[128,512]{1,0:T(8,128)(2,1)S(1)}, u32[]{:S(2)}, u32[]{:S(2)}) collective-permute-start(bf16[128,512]{1,0:T(8,128)(2,1)S(1)} %fusion.30), channel_id=1, source_target_pairs={{0,2},{1,3},{2,0},{3,1},{4,6},{5,7},{6,4},{7,5},{8,10},{9,11},{10,... | collective-permute-start | bytes 393224 | tf_op jit(solution)/shard_map/ppermute | solution.py:309
  101.4 8.9 %collective-permute-start.19 = (bf16[128,512]{1,0:T(8,128)(2,1)S(1)}, bf16[128,512]{1,0:T(8,128)(2,1)S(1)}, u32[]{:S(2)}, u32[]{:S(2)}) collective-permute-start(bf16[128,512]{1,0:T(8,128)(2,1)S(1)} %fusion.30), channel_id=1, source_target_pairs={{0,3},{1,2},{2,1},{3,0},{4,7},{5,6},{6,5},{7,4},{8,11},{9,10},{10,... | collective-permute-start | bytes 393224 | tf_op jit(solution)/shard_map/ppermute | solution.py:309
  106.0 4.3 %collective-permute-start.21 = (bf16[512,512]{1,0:T(8,128)(2,1)S(1)}, bf16[512,512]{1,0:T(8,128)(2,1)S(1)}, u32[]{:S(2)}, u32[]{:S(2)}) collective-permute-start(bf16[512,512]{1,0:T(8,128)(2,1)S(1)} %pad_maximum_fusion.1), channel_id=1, source_target_pairs={{0,2},{2,0},{4,6},{6,4},{8,10},{10,8},{12,14},{14,12},{16,18},{18,... | collective-permute-start | bytes 1572872 | tf_op jit(solution)/shard_map/ppermute | solution.py:294
  114.3 54.0 %collective-permute-start.16 = (bf16[128,8192]{1,0:T(8,128)(2,1)}, bf16[128,8192]{1,0:T(8,128)(2,1)}, u32[]{:S(2)}, u32[]{:S(2)}) collective-permute-start(bf16[128,8192]{1,0:T(8,128)(2,1)} %convolution_convert_fusion), channel_id=1, source_target_pairs={{32,0},{64,32},{96,64},{128,96},{160,128},{192,160},{224,192},{33,... | collective-permute-start | bytes 6291464 | tf_op jit(solution)/shard_map/ppermute | solution.py:372
  139.0 1.9 collective-permute-start.22
  141.3 8.0 %collective-permute-start.23 = (bf16[128,512]{1,0:T(8,128)(2,1)S(1)}, bf16[128,512]{1,0:T(8,128)(2,1)S(1)}, u32[]{:S(2)}, u32[]{:S(2)}) collective-permute-start(bf16[128,512]{1,0:T(8,128)(2,1)S(1)} %fusion.33), channel_id=1, source_target_pairs={{0,28},{2,30},{4,0},{6,2},{8,4},{10,6},{12,8},{14,10},{16,12},{18,... | collective-permute-start | bytes 393224 | tf_op jit(solution)/shard_map/ppermute | solution.py:289
  149.4 6.9 %collective-permute-start.24 = (bf16[128,512]{1,0:T(8,128)(2,1)S(1)}, bf16[128,512]{1,0:T(8,128)(2,1)S(1)}, u32[]{:S(2)}, u32[]{:S(2)}) collective-permute-start(bf16[128,512]{1,0:T(8,128)(2,1)S(1)} %fusion.16), channel_id=1, source_target_pairs={{0,28},{2,30},{4,0},{6,2},{8,4},{10,6},{12,8},{14,10},{16,12},{18,... | collective-permute-start | bytes 393224 | tf_op jit(solution)/shard_map/ppermute | solution.py:289
  168.3 5.2 %collective-permute-start.25 = (bf16[128,512]{1,0:T(8,128)(2,1)S(1)}, bf16[128,512]{1,0:T(8,128)(2,1)S(1)}, u32[]{:S(2)}, u32[]{:S(2)}) collective-permute-start(bf16[128,512]{1,0:T(8,128)(2,1)S(1)} %fusion.18), channel_id=1, source_target_pairs={{0,28},{2,30},{4,0},{6,2},{8,4},{10,6},{12,8},{14,10},{16,12},{18,... | collective-permute-start | bytes 393224 | tf_op jit(solution)/shard_map/ppermute | solution.py:289
  173.5 5.0 %collective-permute-start.26 = (bf16[128,512]{1,0:T(8,128)(2,1)S(1)}, bf16[128,512]{1,0:T(8,128)(2,1)S(1)}, u32[]{:S(2)}, u32[]{:S(2)}) collective-permute-start(bf16[128,512]{1,0:T(8,128)(2,1)S(1)} %fusion.20), channel_id=1, source_target_pairs={{0,28},{2,30},{4,0},{6,2},{8,4},{10,6},{12,8},{14,10},{16,12},{18,... | collective-permute-start | bytes 393224 | tf_op jit(solution)/shard_map/ppermute | solution.py:289
  175.1 7.1 %collective-permute-start.27 = (bf16[256,512]{1,0:T(8,128)(2,1)}, bf16[256,512]{1,0:T(8,128)(2,1)S(1)}, u32[]{:S(2)}, u32[]{:S(2)}) collective-permute-start(bf16[256,512]{1,0:T(8,128)(2,1)} %reduce-scatter.2.cloned.1.call-done), channel_id=1, source_target_pairs={{0,1},{1,0},{2,3},{3,2},{4,5},{5,4},{6,7},{7,6},{8,9},{9,8},{10,11... | collective-permute-start | bytes 786440 | tf_op jit(solution)/shard_map/ppermute | solution.py:380
  (9 other events, 138.3 us)
Sparse Core Ops, SparseCore 0:
  9.8 62.9 all-gather.2
  114.4 43.0 reduce-scatter.1

commit v3 on v2

--- a/solution.py
+++ b/solution.py
@@ -259,7 +259,7 @@
         + [pltpu.VMEM((WINDOW, 2 * TOK), jnp.float32)] * 2
         + [pltpu.VMEM((WINDOW, 2 * TOK), jnp.bfloat16)] * 2,
         earlier,
-        pl.CostEstimate(flops=6 * work * HD, bytes_accessed=groups * (7 << 20), transcendentals=0),
+        pl.CostEstimate(flops=0, bytes_accessed=0, transcendentals=0),
     )
 
 
@@ -368,11 +368,13 @@
     value_grad = relayed_sum(sums, [values, *value_window[1:HOPS]])
 
     moves = [(section, section - 1) for section in range(1, lax.axis_size("pipe"))]
-    input_grad = rounded(dot(value_grad, weight, NT))
-    upstream = lax.ppermute(input_grad, "pipe", moves)
+    middle = weight.shape[0] * 7 // 8
+    input_grads = [rounded(dot(value_grad, rows, NT)) for rows in (weight[:middle], weight[middle:])]
+    upstreams = [lax.ppermute(part, "pipe", moves) for part in input_grads]
+    upstream = jnp.concatenate(upstreams, axis=1)
 
     quad_grads = [value_grad] + [quad_partner(value_grad, offset) for offset in range(1, 4)]
-    quad_grads = jnp.concatenate(after(quad_grads, *value_window, input_grad), axis=0)
+    quad_grads = jnp.concatenate(after(quad_grads, *value_window, *input_grads), axis=0)
     weight_part = rounded(dot(jnp.concatenate(quad_inputs, axis=0), quad_grads, TN))
     weight_half = lax.psum_scatter(
         weight_part, "fsdp", scatter_dimension=0, tiled=True, axis_index_groups=columns
@@ -384,7 +386,8 @@
 
     value_window[0] = after(value_window[0], weight_part)
     query_out, given, kept = query_and_key_grad(0, KV, queries, grads, probs, key_window, value_window)
-    key_grad = relayed_sum(chip_sums(given, kept, odd), [given, upstream])
+    sums = chip_sums(after(given, upstreams[0]), kept, odd)
+    key_grad = relayed_sum(sums, [given, upstreams[1], (upstream, weight_half)])
     return (
         upstream[None, None],
         query_out[None, None],

time: 194 us -> 197 us (1.015)
  starting transfers between devices: 23.1 us -> 30.8 us
  waiting for transfers between devices: 88.9 us -> 82.9 us
    ppermute x16, waiting for transfers between devices: 67.2 us -> 47.1 us  [permuted(): lax.ppermute(value, 'fsdp', [(source, (source + steps) % count) for sourc...]
    ppermute x1 -> x2, waiting for transfers between devices: 12 us -> 25.8 us  [shards(): upstreams = [lax.ppermute(part, 'pipe', moves) for part in input_grads]]
    ppermute x16, starting transfers between devices: 14.3 us -> 20.5 us  [permuted(): lax.ppermute(value, 'fsdp', [(source, (source + steps) % count) for sourc...]
    ppermute x1 -> x2, starting transfers between devices: 3.11 us -> 4.86 us  [shards(): upstreams = [lax.ppermute(part, 'pipe', moves) for part in input_grads]]
    unnamed x23 -> x19, local copies, waits for them, and re-layouts: 4.19 us -> 3.93 us
    dot_general x3 -> x4, matrix products: 12.9 us -> 13 us  [dot(): lax.dot_general(left, right, numbers, preferred_element_type=jnp.float32)]
  transfers between devices with their start and end apart: 30 -> 31, of which waited for: 22 -> 20; matrix products, arithmetic and copies ran while one was open for 6% -> 10% of each run, Pallas kernels for 24% -> 23%
where the time goes in v3:
time: 197 us
  waiting for transfers between devices  82.9 us (42%)
  Pallas kernels  45.8 us (23%)
  starting transfers between devices  30.8 us (16%)
  between operations  14.3 us (7%)
  matrix products  13 us (7%)
  other arithmetic  5.48 us (3%)
  local copies, waits for them, and re-layouts  4.69 us (2%)
    ppermute x16, waiting for transfers between devices, permuted(): lax.ppermute(value, 'fsdp', [(source, (source + steps) % count) for sourc...  47.1 us
    pallas_call x2, Pallas kernels, part_call(): pl.pallas_call(kernel, grid=(groups, STEPS), in_specs=in_specs + [pl.Bloc...  42.5 us
    ppermute x2, waiting for transfers between devices, shards(): upstreams = [lax.ppermute(part, 'pipe', moves) for part in input_grads]  25.8 us
    ppermute x16, starting transfers between devices, permuted(): lax.ppermute(value, 'fsdp', [(source, (source + steps) % count) for sourc...  20.5 us
    dot_general x4, matrix products, dot(): lax.dot_general(left, right, numbers, preferred_element_type=jnp.float32)  13 us
    ppermute x2, starting transfers between devices, shards(): upstreams = [lax.ppermute(part, 'pipe', moves) for part in input_grads]  4.86 us
    ppermute x6, starting transfers between devices, quad_partner(): return lax.ppermute(value, ('pipe', 'fsdp', 'rep'), moves)  4.37 us
  transfers between devices with their start and end apart: 31, of which 20 were waited for; matrix products, arithmetic and copies ran while one was open for 10% of the time, Pallas kernels for 23%

profile of v3, /device:TPU:14, one launch (start us, length us, event | category | flops | bytes accessed | tf_op | source)
XLA Modules:
  0.0 196.9 jit_solution(146142450304532276)
XLA Ops:
  8.0 2.0 %collective-permute-start = (bf16[128,512]{1,0:T(8,128)(2,1)}, bf16[128,512]{1,0:T(8,128)(2,1)S(1)}, u32[]{:S(2)}, u32[]{:S(2)}) collective-permute-start(bf16[128,512]{1,0:T(8,128)(2,1)} %bitcast.92), channel_id=1, source_target_pairs={{0,4},{2,6},{4,8},{6,10},{8,12},{10,14},{12,16},{14,18},{16,20},{1... | collective-permute-start | bytes 393224 | tf_op jit(solution)/shard_map/ppermute | solution.py:289
  10.0 3.3 %shard_map.93 = (bf16[128,2048]{1,0:T(8,128)(2,1)}, bf16[128,2048]{1,0:T(8,128)(2,1)}, bf16[128,2048]{1,0:T(8,128)(2,1)}, bf16[128,2048]{1,0:T(8,128)(2,1)}) custom-call(s32[1]{0:T(128)} %bitcast.5.mine_ref, bf16[128,8192]{1,0:T(8,128)(2,1)} %bitcast.98), custom_call_target="tpu_custom_call" | custom-call | bytes 4194304 | tf_op jit(solution)/shard_map/pallas_call | solution.py:278
  13.3 4.3 %collective-permute-done.refs_1_ = bf16[128,512]{1,0:T(8,128)(2,1)S(1)} collective-permute-done((bf16[128,512]{1,0:T(8,128)(2,1)}, bf16[128,512]{1,0:T(8,128)(2,1)S(1)}, u32[]{:S(2)}, u32[]{:S(2)}) %collective-permute-start) | collective-permute-done | bytes 131104 | tf_op jit(solution)/shard_map/ppermute | solution.py:289
  17.6 6.2 %collective-permute-done.1.refs_2_ = bf16[128,512]{1,0:T(8,128)(2,1)S(1)} collective-permute-done((bf16[128,512]{1,0:T(8,128)(2,1)S(1)}, bf16[128,512]{1,0:T(8,128)(2,1)S(1)}, u32[]{:S(2)}, u32[]{:S(2)}) %collective-permute-start.1) | collective-permute-done | bytes 131104 | tf_op jit(solution)/shard_map/ppermute | solution.py:289
  23.8 9.2 %collective-permute-done.2.refs_3_ = bf16[128,512]{1,0:T(8,128)(2,1)S(1)} collective-permute-done((bf16[128,512]{1,0:T(8,128)(2,1)S(1)}, bf16[128,512]{1,0:T(8,128)(2,1)S(1)}, u32[]{:S(2)}, u32[]{:S(2)}) %collective-permute-start.2) | collective-permute-done | bytes 131104 | tf_op jit(solution)/shard_map/ppermute | solution.py:289
  33.0 9.0 %collective-permute-done.3.refs_4_ = bf16[128,512]{1,0:T(8,128)(2,1)S(1)} collective-permute-done((bf16[128,512]{1,0:T(8,128)(2,1)S(1)}, bf16[128,512]{1,0:T(8,128)(2,1)S(1)}, u32[]{:S(2)}, u32[]{:S(2)}) %collective-permute-start.3) | collective-permute-done | bytes 131104 | tf_op jit(solution)/shard_map/ppermute | solution.py:289
  45.1 20.9 %shard_map.94 = (bf16[32,1152,256]{2,1,0:T(8,128)(2,1)}, bf16[512,512]{1,0:T(8,128)(2,1)S(1)}, f32[640,512]{1,0:T(8,128)S(1)}) custom-call(s32[5]{0:T(128)S(1)} %pad_add_fusion.info_ref, bf16[128,8192]{1,0:T(8,128)(2,1)S(1)} %bitcast.89, bf16[128,8192]{1,0:T(8,128)(2,1)} %bitcast.99, bf16[128,512]{1,0:T(8,128)(2,1)S(1)} %bitcast.93, ...), custom_call_target="tpu_custom_call" | custom-call | flops 4831838208 | bytes 25165824 | tf_op jit(solution)/shard_map/pallas_call | solution.py:210
  66.0 2.4 %collective-permute-done.7 = bf16[128,2048]{1,0:T(8,128)(2,1)} collective-permute-done((bf16[128,2048]{1,0:T(8,128)(2,1)}, bf16[128,2048]{1,0:T(8,128)(2,1)}, u32[]{:S(2)}, u32[]{:S(2)}) %collective-permute-start.7) | collective-permute-done | bytes 524320 | tf_op jit(solution)/shard_map/ppermute | solution.py:309
  72.8 4.8 %fusion.7.refs_6_ = bf16[128,512]{1,0:T(8,128)(2,1)S(1)} fusion(bf16[8192,512]{1,0:T(8,128)(2,1)} %bitcast.95, bf16[1,1,128,8192]{3,2,1,0:T(8,128)(2,1)S(1)} %copy-done.2), kind=kOutput, calls=%fused_computation.14 | convolution fusion | flops 1073807360 | bytes 10616832 | tf_op jit(solution)/shard_map/dot_general | solution.py:37
  77.6 1.7 collective-permute-start.11
  80.3 1.7 collective-permute-start.10
  82.0 2.7 %collective-permute-done.11.refs_7_ = bf16[128,512]{1,0:T(8,128)(2,1)S(1)} collective-permute-done((bf16[128,512]{1,0:T(8,128)(2,1)S(1)}, bf16[128,512]{1,0:T(8,128)(2,1)S(1)}, u32[]{:S(2)}, u32[]{:S(2)}) %collective-permute-start.11) | collective-permute-done | bytes 131104 | tf_op jit(solution)/shard_map/ppermute | solution.py:289
  86.3 2.6 %collective-permute-start.12 = (bf16[128,512]{1,0:T(8,128)(2,1)S(1)}, bf16[128,512]{1,0:T(8,128)(2,1)S(1)}, u32[]{:S(2)}, u32[]{:S(2)}) collective-permute-start(bf16[128,512]{1,0:T(8,128)(2,1)S(1)} %fusion.26), channel_id=1, source_target_pairs={{0,28},{2,30},{4,0},{6,2},{8,4},{10,6},{12,8},{14,10},{16,12},{18,... | collective-permute-start | bytes 393224 | tf_op jit(solution)/shard_map/ppermute | solution.py:289
  88.9 2.9 %collective-permute-done.13.refs_8_ = bf16[128,512]{1,0:T(8,128)(2,1)S(1)} collective-permute-done((bf16[128,512]{1,0:T(8,128)(2,1)S(1)}, bf16[128,512]{1,0:T(8,128)(2,1)S(1)}, u32[]{:S(2)}, u32[]{:S(2)}) %collective-permute-start.13) | collective-permute-done | bytes 131104 | tf_op jit(solution)/shard_map/ppermute | solution.py:289
  91.9 2.4 %collective-permute-start.15 = (bf16[128,512]{1,0:T(8,128)(2,1)S(1)}, bf16[128,512]{1,0:T(8,128)(2,1)S(1)}, u32[]{:S(2)}, u32[]{:S(2)}) collective-permute-start(bf16[128,512]{1,0:T(8,128)(2,1)S(1)} %collective-permute-done.13.refs_8_), channel_id=1, source_target_pairs={{0,4},{2,6},{4,8},{6,10},{8,12},{10,14},{12,16},{14,18},{16,20},{1... | collective-permute-start | bytes 393224 | tf_op jit(solution)/shard_map/ppermute | solution.py:289
  95.3 2.9 %collective-permute-done.15.refs_9_ = bf16[128,512]{1,0:T(8,128)(2,1)S(1)} collective-permute-done((bf16[128,512]{1,0:T(8,128)(2,1)S(1)}, bf16[128,512]{1,0:T(8,128)(2,1)S(1)}, u32[]{:S(2)}, u32[]{:S(2)}) %collective-permute-start.15) | collective-permute-done | bytes 131104 | tf_op jit(solution)/shard_map/ppermute | solution.py:289
  99.3 2.0 %collective-permute-start.21 = (bf16[128,512]{1,0:T(8,128)(2,1)S(1)}, bf16[128,512]{1,0:T(8,128)(2,1)S(1)}, u32[]{:S(2)}, u32[]{:S(2)}) collective-permute-start(bf16[128,512]{1,0:T(8,128)(2,1)S(1)} %collective-permute-done.15.refs_9_), channel_id=1, source_target_pairs={{0,4},{2,6},{4,8},{6,10},{8,12},{10,14},{12,16},{14,18},{16,20},{1... | collective-permute-start | bytes 393224 | tf_op jit(solution)/shard_map/ppermute | solution.py:289
  103.5 1.9 collective-permute-done.21.refs_10_
  105.7 3.7 %convolution_convert_fusion = bf16[128,7168]{1,0:T(8,128)(2,1)} fusion(bf16[128,512]{1,0:T(8,128)(2,1)S(1)} %fusion.30, bf16[1,8192,512]{2,1,0:T(8,128)(2,1)S(1)} %bitcast.97), kind=kOutput, calls=%fused_computation | convolution fusion | flops 940441600 | bytes 9306112 | tf_op jit(solution)/shard_map/dot_general | solution.py:37
  109.4 2.9 %collective-permute-start.16 = (bf16[128,7168]{1,0:T(8,128)(2,1)}, bf16[128,7168]{1,0:T(8,128)(2,1)}, u32[]{:S(2)}, u32[]{:S(2)}) collective-permute-start(bf16[128,7168]{1,0:T(8,128)(2,1)} %convolution_convert_fusion), channel_id=1, source_target_pairs={{32,0},{64,32},{96,64},{128,96},{160,128},{192,160},{224,192},{33,... | collective-permute-start | bytes 5505032 | tf_op jit(solution)/shard_map/ppermute | solution.py:373
  112.9 4.0 %convolution_convert_fusion.1 = bf16[2048,512]{1,0:T(8,128)(2,1)} fusion(bf16[128,2048]{1,0:T(8,128)(2,1)} %collective-permute-done.7, bf16[128,2048]{1,0:T(8,128)(2,1)} %collective-permute-done.6, bf16[128,2048]{1,0:T(8,128)(2,1)} %collective-permute-done.5, bf16[128,2048]{1,0:T(8,128)(2,1)S(1)} %copy-done.5, ...), kind=kOutput, calls=%fused_computation.2 | convolution fusion | flops 1085276160 | bytes 4718592 | tf_op jit(solution)/shard_map/dot_general | solution.py:37
  116.9 21.6 %shard_map.95 = (bf16[128,8192]{1,0:T(8,128)(2,1)}, bf16[512,512]{1,0:T(8,128)(2,1)S(1)}, f32[640,512]{1,0:T(8,128)S(1)}) custom-call(bf16[128,8192]{1,0:T(8,128)(2,1)} %bitcast.88, bf16[128,8192]{1,0:T(8,128)(2,1)} %bitcast.100, bf16[32,1152,256]{2,1,0:T(8,128)(2,1)} %get-tuple-element.43.probs_ref, bf16[128,512]{1,0:T(8,128)(2,1)S(1)} %bitcast.94, ...), custom_call_target="tpu_custom_call" | custom-call | tf_op jit(solution)/shard_map/pallas_call | solution.py:210
  138.5 19.1 %collective-permute-done.16 = bf16[128,7168]{1,0:T(8,128)(2,1)} collective-permute-done((bf16[128,7168]{1,0:T(8,128)(2,1)}, bf16[128,7168]{1,0:T(8,128)(2,1)}, u32[]{:S(2)}, u32[]{:S(2)}) %collective-permute-start.16) | collective-permute-done | bytes 1835040 | tf_op jit(solution)/shard_map/ppermute | solution.py:373
  157.6 1.9 collective-permute-done.23
  161.0 1.9 collective-permute-start.17
  162.9 2.6 %collective-permute-done.24 = bf16[128,512]{1,0:T(8,128)(2,1)S(1)} collective-permute-done((bf16[128,512]{1,0:T(8,128)(2,1)S(1)}, bf16[128,512]{1,0:T(8,128)(2,1)S(1)}, u32[]{:S(2)}, u32[]{:S(2)}) %collective-permute-start.24) | collective-permute-done | bytes 131104 | tf_op jit(solution)/shard_map/ppermute | solution.py:289
  165.6 2.3 %collective-permute-start.25 = (bf16[128,512]{1,0:T(8,128)(2,1)S(1)}, bf16[128,512]{1,0:T(8,128)(2,1)S(1)}, u32[]{:S(2)}, u32[]{:S(2)}) collective-permute-start(bf16[128,512]{1,0:T(8,128)(2,1)S(1)} %fusion.16), channel_id=1, source_target_pairs={{0,28},{2,30},{4,0},{6,2},{8,4},{10,6},{12,8},{14,10},{16,12},{18,... | collective-permute-start | bytes 393224 | tf_op jit(solution)/shard_map/ppermute | solution.py:289
  167.8 6.7 %collective-permute-done.17 = bf16[128,1024]{1,0:T(8,128)(2,1)S(1)} collective-permute-done((bf16[128,1024]{1,0:T(8,128)(2,1)S(1)}, bf16[128,1024]{1,0:T(8,128)(2,1)S(1)}, u32[]{:S(2)}, u32[]{:S(2)}) %collective-permute-start.17) | collective-permute-done | bytes 262176 | tf_op jit(solution)/shard_map/ppermute | solution.py:373
  175.4 2.8 %constant_dynamic-update-slice_fusion.1 = bf16[128,8192]{1,0:T(8,128)(2,1)} fusion(bf16[128,7168]{1,0:T(8,128)(2,1)} %collective-permute-done.16), kind=kLoop, calls=%fused_computation.66 | loop fusion | bytes 3670016
  179.7 2.0 %collective-permute-start.27 = (bf16[128,512]{1,0:T(8,128)(2,1)S(1)}, bf16[128,512]{1,0:T(8,128)(2,1)S(1)}, u32[]{:S(2)}, u32[]{:S(2)}) collective-permute-start(bf16[128,512]{1,0:T(8,128)(2,1)S(1)} %fusion.20), channel_id=1, source_target_pairs={{0,28},{2,30},{4,0},{6,2},{8,4},{10,6},{12,8},{14,10},{16,12},{18,... | collective-permute-start | bytes 393224 | tf_op jit(solution)/shard_map/ppermute | solution.py:289
  182.1 2.7 %collective-permute-done.27 = bf16[128,512]{1,0:T(8,128)(2,1)S(1)} collective-permute-done((bf16[128,512]{1,0:T(8,128)(2,1)S(1)}, bf16[128,512]{1,0:T(8,128)(2,1)S(1)}, u32[]{:S(2)}, u32[]{:S(2)}) %collective-permute-start.27) | collective-permute-done | bytes 131104 | tf_op jit(solution)/shard_map/ppermute | solution.py:289
  185.4 2.9 %collective-permute-done.28 = bf16[256,512]{1,0:T(8,128)(2,1)S(1)} collective-permute-done((bf16[256,512]{1,0:T(8,128)(2,1)}, bf16[256,512]{1,0:T(8,128)(2,1)S(1)}, u32[]{:S(2)}, u32[]{:S(2)}) %collective-permute-start.28) | collective-permute-done | bytes 262176 | tf_op jit(solution)/shard_map/ppermute | solution.py:382
  (81 shorter events, 22.5 us)
Async XLA Ops:
  7.2 65.6 %all-gather.3.cloned.1.call-start = ((), (), s32[]{:S(2)}) async-start(), calls=%async_computation.2 | async-start | bytes 8912896 | tf_op jit(solution)/shard_map/all_gather | solution.py:359
  7.9 171.7 %reduce-scatter.2.cloned.1.call-start = ((), (), s32[]{:S(2)}) async-start(), calls=%async_computation.1 | async-start | bytes 2359296 | tf_op jit(solution)/shard_map/reduce_scatter | solution.py:379
  8.0 9.6 %collective-permute-start = (bf16[128,512]{1,0:T(8,128)(2,1)}, bf16[128,512]{1,0:T(8,128)(2,1)S(1)}, u32[]{:S(2)}, u32[]{:S(2)}) collective-permute-start(bf16[128,512]{1,0:T(8,128)(2,1)} %bitcast.92), channel_id=1, source_target_pairs={{0,4},{2,6},{4,8},{6,10},{8,12},{10,14},{12,16},{14,18},{16,20},{1... | collective-permute-start | bytes 393224 | tf_op jit(solution)/shard_map/ppermute | solution.py:289
  10.0 35.1 %copy-start = (bf16[1,1,128,8192]{3,2,1,0:T(8,128)(2,1)S(1)}, bf16[1,1,128,8192]{3,2,1,0:T(8,128)(2,1)}, u32[]{:S(2)}) copy-start(bf16[1,1,128,8192]{3,2,1,0:T(8,128)(2,1)} %param.7) | copy-start | bytes 6291460
  17.6 6.2 %collective-permute-start.1 = (bf16[128,512]{1,0:T(8,128)(2,1)S(1)}, bf16[128,512]{1,0:T(8,128)(2,1)S(1)}, u32[]{:S(2)}, u32[]{:S(2)}) collective-permute-start(bf16[128,512]{1,0:T(8,128)(2,1)S(1)} %collective-permute-done.refs_1_), channel_id=1, source_target_pairs={{0,4},{2,6},{4,8},{6,10},{8,12},{10,14},{12,16},{14,18},{16,20},{1... | collective-permute-start | bytes 393224 | tf_op jit(solution)/shard_map/ppermute | solution.py:289
  23.8 9.2 %collective-permute-start.2 = (bf16[128,512]{1,0:T(8,128)(2,1)S(1)}, bf16[128,512]{1,0:T(8,128)(2,1)S(1)}, u32[]{:S(2)}, u32[]{:S(2)}) collective-permute-start(bf16[128,512]{1,0:T(8,128)(2,1)S(1)} %collective-permute-done.1.refs_2_), channel_id=1, source_target_pairs={{0,4},{2,6},{4,8},{6,10},{8,12},{10,14},{12,16},{14,18},{16,20},{1... | collective-permute-start | bytes 393224 | tf_op jit(solution)/shard_map/ppermute | solution.py:289
  33.0 9.0 %collective-permute-start.3 = (bf16[128,512]{1,0:T(8,128)(2,1)S(1)}, bf16[128,512]{1,0:T(8,128)(2,1)S(1)}, u32[]{:S(2)}, u32[]{:S(2)}) collective-permute-start(bf16[128,512]{1,0:T(8,128)(2,1)S(1)} %collective-permute-done.2.refs_3_), channel_id=1, source_target_pairs={{0,4},{2,6},{4,8},{6,10},{8,12},{10,14},{12,16},{14,18},{16,20},{1... | collective-permute-start | bytes 393224 | tf_op jit(solution)/shard_map/ppermute | solution.py:289
  42.9 2.2 %collective-permute-start.4 = (bf16[512,512]{1,0:T(8,128)(2,1)}, bf16[512,512]{1,0:T(8,128)(2,1)S(1)}, u32[]{:S(2)}, u32[]{:S(2)}) collective-permute-start(bf16[512,512]{1,0:T(8,128)(2,1)} %pad_maximum_fusion), channel_id=1, source_target_pairs={{0,2},{2,0},{4,6},{6,4},{8,10},{10,8},{12,14},{14,12},{16,18},{18,... | collective-permute-start | bytes 1572872 | tf_op jit(solution)/shard_map/ppermute | solution.py:294
  42.9 23.1 %collective-permute-start.5 = (bf16[128,2048]{1,0:T(8,128)(2,1)}, bf16[128,2048]{1,0:T(8,128)(2,1)}, u32[]{:S(2)}, u32[]{:S(2)}) collective-permute-start(bf16[128,2048]{1,0:T(8,128)(2,1)} %get-tuple-element.31), channel_id=1, source_target_pairs={{0,1},{1,0},{2,3},{3,2},{4,5},{5,4},{6,7},{7,6},{8,9},{9,8},{10,11... | collective-permute-start | bytes 1572872 | tf_op jit(solution)/shard_map/ppermute | solution.py:309
  43.3 22.7 %collective-permute-start.6 = (bf16[128,2048]{1,0:T(8,128)(2,1)}, bf16[128,2048]{1,0:T(8,128)(2,1)}, u32[]{:S(2)}, u32[]{:S(2)}) collective-permute-start(bf16[128,2048]{1,0:T(8,128)(2,1)} %get-tuple-element.32), channel_id=1, source_target_pairs={{0,2},{1,3},{2,0},{3,1},{4,6},{5,7},{6,4},{7,5},{8,10},{9,11},{10,... | collective-permute-start | bytes 1572872 | tf_op jit(solution)/shard_map/ppermute | solution.py:309
  43.5 24.8 %collective-permute-start.7 = (bf16[128,2048]{1,0:T(8,128)(2,1)}, bf16[128,2048]{1,0:T(8,128)(2,1)}, u32[]{:S(2)}, u32[]{:S(2)}) collective-permute-start(bf16[128,2048]{1,0:T(8,128)(2,1)} %get-tuple-element.33), channel_id=1, source_target_pairs={{0,3},{1,2},{2,1},{3,0},{4,7},{5,6},{6,5},{7,4},{8,11},{9,10},{10,... | collective-permute-start | bytes 1572872 | tf_op jit(solution)/shard_map/ppermute | solution.py:309
  68.4 2.2 %collective-permute-start.8 = (bf16[512,512]{1,0:T(8,128)(2,1)S(1)}, bf16[512,512]{1,0:T(8,128)(2,1)S(1)}, u32[]{:S(2)}, u32[]{:S(2)}) collective-permute-start(bf16[512,512]{1,0:T(8,128)(2,1)S(1)} %get-tuple-element.37), channel_id=1, source_target_pairs={{0,2},{2,0},{4,6},{6,4},{8,10},{10,8},{12,14},{14,12},{16,18},{18,... | collective-permute-start | bytes 1572872 | tf_op jit(solution)/shard_map/ppermute | solution.py:294
  72.1 7.2 %collective-permute-start.9 = (bf16[128,512]{1,0:T(8,128)(2,1)S(1)}, bf16[128,512]{1,0:T(8,128)(2,1)}, u32[]{:S(2)}, u32[]{:S(2)}) collective-permute-start(bf16[128,512]{1,0:T(8,128)(2,1)S(1)} %fusion.31), channel_id=1, source_target_pairs={{0,28},{2,30},{4,0},{6,2},{8,4},{10,6},{12,8},{14,10},{16,12},{18,... | collective-permute-start | bytes 393224 | tf_op jit(solution)/shard_map/ppermute | solution.py:289
  77.6 7.0 %collective-permute-start.11 = (bf16[128,512]{1,0:T(8,128)(2,1)S(1)}, bf16[128,512]{1,0:T(8,128)(2,1)S(1)}, u32[]{:S(2)}, u32[]{:S(2)}) collective-permute-start(bf16[128,512]{1,0:T(8,128)(2,1)S(1)} %fusion.7.refs_6_), channel_id=1, source_target_pairs={{0,4},{2,6},{4,8},{6,10},{8,12},{10,14},{12,16},{14,18},{16,20},{1... | collective-permute-start | bytes 393224 | tf_op jit(solution)/shard_map/ppermute | solution.py:289
  80.3 5.3 %collective-permute-start.10 = (bf16[128,512]{1,0:T(8,128)(2,1)S(1)}, bf16[128,512]{1,0:T(8,128)(2,1)S(1)}, u32[]{:S(2)}, u32[]{:S(2)}) collective-permute-start(bf16[128,512]{1,0:T(8,128)(2,1)S(1)} %fusion.24), channel_id=1, source_target_pairs={{0,28},{2,30},{4,0},{6,2},{8,4},{10,6},{12,8},{14,10},{16,12},{18,... | collective-permute-start | bytes 393224 | tf_op jit(solution)/shard_map/ppermute | solution.py:289
  85.6 6.3 %collective-permute-start.13 = (bf16[128,512]{1,0:T(8,128)(2,1)S(1)}, bf16[128,512]{1,0:T(8,128)(2,1)S(1)}, u32[]{:S(2)}, u32[]{:S(2)}) collective-permute-start(bf16[128,512]{1,0:T(8,128)(2,1)S(1)} %collective-permute-done.11.refs_7_), channel_id=1, source_target_pairs={{0,4},{2,6},{4,8},{6,10},{8,12},{10,14},{12,16},{14,18},{16,20},{1... | collective-permute-start | bytes 393224 | tf_op jit(solution)/shard_map/ppermute | solution.py:289
  86.3 5.6 %collective-permute-start.12 = (bf16[128,512]{1,0:T(8,128)(2,1)S(1)}, bf16[128,512]{1,0:T(8,128)(2,1)S(1)}, u32[]{:S(2)}, u32[]{:S(2)}) collective-permute-start(bf16[128,512]{1,0:T(8,128)(2,1)S(1)} %fusion.26), channel_id=1, source_target_pairs={{0,28},{2,30},{4,0},{6,2},{8,4},{10,6},{12,8},{14,10},{16,12},{18,... | collective-permute-start | bytes 393224 | tf_op jit(solution)/shard_map/ppermute | solution.py:289
  91.9 6.3 %collective-permute-start.15 = (bf16[128,512]{1,0:T(8,128)(2,1)S(1)}, bf16[128,512]{1,0:T(8,128)(2,1)S(1)}, u32[]{:S(2)}, u32[]{:S(2)}) collective-permute-start(bf16[128,512]{1,0:T(8,128)(2,1)S(1)} %collective-permute-done.13.refs_8_), channel_id=1, source_target_pairs={{0,4},{2,6},{4,8},{6,10},{8,12},{10,14},{12,16},{14,18},{16,20},{1... | collective-permute-start | bytes 393224 | tf_op jit(solution)/shard_map/ppermute | solution.py:289
  94.3 5.0 %collective-permute-start.14 = (bf16[128,512]{1,0:T(8,128)(2,1)S(1)}, bf16[128,512]{1,0:T(8,128)(2,1)S(1)}, u32[]{:S(2)}, u32[]{:S(2)}) collective-permute-start(bf16[128,512]{1,0:T(8,128)(2,1)S(1)} %fusion.28), channel_id=1, source_target_pairs={{0,28},{2,30},{4,0},{6,2},{8,4},{10,6},{12,8},{14,10},{16,12},{18,... | collective-permute-start | bytes 393224 | tf_op jit(solution)/shard_map/ppermute | solution.py:289
  99.3 6.2 %collective-permute-start.21 = (bf16[128,512]{1,0:T(8,128)(2,1)S(1)}, bf16[128,512]{1,0:T(8,128)(2,1)S(1)}, u32[]{:S(2)}, u32[]{:S(2)}) collective-permute-start(bf16[128,512]{1,0:T(8,128)(2,1)S(1)} %collective-permute-done.15.refs_9_), channel_id=1, source_target_pairs={{0,4},{2,6},{4,8},{6,10},{8,12},{10,14},{12,16},{14,18},{16,20},{1... | collective-permute-start | bytes 393224 | tf_op jit(solution)/shard_map/ppermute | solution.py:289
  101.3 11.5 %collective-permute-start.18 = (bf16[128,512]{1,0:T(8,128)(2,1)S(1)}, bf16[128,512]{1,0:T(8,128)(2,1)S(1)}, u32[]{:S(2)}, u32[]{:S(2)}) collective-permute-start(bf16[128,512]{1,0:T(8,128)(2,1)S(1)} %fusion.30), channel_id=1, source_target_pairs={{0,1},{1,0},{2,3},{3,2},{4,5},{5,4},{6,7},{7,6},{8,9},{9,8},{10,11... | collective-permute-start | bytes 393224 | tf_op jit(solution)/shard_map/ppermute | solution.py:309
  101.9 10.9 %collective-permute-start.19 = (bf16[128,512]{1,0:T(8,128)(2,1)S(1)}, bf16[128,512]{1,0:T(8,128)(2,1)S(1)}, u32[]{:S(2)}, u32[]{:S(2)}) collective-permute-start(bf16[128,512]{1,0:T(8,128)(2,1)S(1)} %fusion.30), channel_id=1, source_target_pairs={{0,2},{1,3},{2,0},{3,1},{4,6},{5,7},{6,4},{7,5},{8,10},{9,11},{10,... | collective-permute-start | bytes 393224 | tf_op jit(solution)/shard_map/ppermute | solution.py:309
  101.9 10.9 %collective-permute-start.20 = (bf16[128,512]{1,0:T(8,128)(2,1)S(1)}, bf16[128,512]{1,0:T(8,128)(2,1)S(1)}, u32[]{:S(2)}, u32[]{:S(2)}) collective-permute-start(bf16[128,512]{1,0:T(8,128)(2,1)S(1)} %fusion.30), channel_id=1, source_target_pairs={{0,3},{1,2},{2,1},{3,0},{4,7},{5,6},{6,5},{7,4},{8,11},{9,10},{10,... | collective-permute-start | bytes 393224 | tf_op jit(solution)/shard_map/ppermute | solution.py:309
  105.5 7.3 %collective-permute-start.22 = (bf16[512,512]{1,0:T(8,128)(2,1)S(1)}, bf16[512,512]{1,0:T(8,128)(2,1)S(1)}, u32[]{:S(2)}, u32[]{:S(2)}) collective-permute-start(bf16[512,512]{1,0:T(8,128)(2,1)S(1)} %pad_maximum_fusion.1), channel_id=1, source_target_pairs={{0,2},{2,0},{4,6},{6,4},{8,10},{10,8},{12,14},{14,12},{16,18},{18,... | collective-permute-start | bytes 1572872 | tf_op jit(solution)/shard_map/ppermute | solution.py:294
  109.4 48.2 %collective-permute-start.16 = (bf16[128,7168]{1,0:T(8,128)(2,1)}, bf16[128,7168]{1,0:T(8,128)(2,1)}, u32[]{:S(2)}, u32[]{:S(2)}) collective-permute-start(bf16[128,7168]{1,0:T(8,128)(2,1)} %convolution_convert_fusion), channel_id=1, source_target_pairs={{32,0},{64,32},{96,64},{128,96},{160,128},{192,160},{224,192},{33,... | collective-permute-start | bytes 5505032 | tf_op jit(solution)/shard_map/ppermute | solution.py:373
  157.6 1.9 collective-permute-start.23
  159.9 5.6 %collective-permute-start.24 = (bf16[128,512]{1,0:T(8,128)(2,1)S(1)}, bf16[128,512]{1,0:T(8,128)(2,1)S(1)}, u32[]{:S(2)}, u32[]{:S(2)}) collective-permute-start(bf16[128,512]{1,0:T(8,128)(2,1)S(1)} %fusion.33), channel_id=1, source_target_pairs={{0,28},{2,30},{4,0},{6,2},{8,4},{10,6},{12,8},{14,10},{16,12},{18,... | collective-permute-start | bytes 393224 | tf_op jit(solution)/shard_map/ppermute | solution.py:289
  161.0 13.6 %collective-permute-start.17 = (bf16[128,1024]{1,0:T(8,128)(2,1)S(1)}, bf16[128,1024]{1,0:T(8,128)(2,1)S(1)}, u32[]{:S(2)}, u32[]{:S(2)}) collective-permute-start(bf16[128,1024]{1,0:T(8,128)(2,1)S(1)} %convolution_convert_fusion.2), channel_id=1, source_target_pairs={{32,0},{64,32},{96,64},{128,96},{160,128},{192,160},{224,192},{33,... | collective-permute-start | bytes 786440 | tf_op jit(solution)/shard_map/ppermute | solution.py:373
  165.6 9.0 %collective-permute-start.25 = (bf16[128,512]{1,0:T(8,128)(2,1)S(1)}, bf16[128,512]{1,0:T(8,128)(2,1)S(1)}, u32[]{:S(2)}, u32[]{:S(2)}) collective-permute-start(bf16[128,512]{1,0:T(8,128)(2,1)S(1)} %fusion.16), channel_id=1, source_target_pairs={{0,28},{2,30},{4,0},{6,2},{8,4},{10,6},{12,8},{14,10},{16,12},{18,... | collective-permute-start | bytes 393224 | tf_op jit(solution)/shard_map/ppermute | solution.py:289
  174.6 5.0 %collective-permute-start.26 = (bf16[128,512]{1,0:T(8,128)(2,1)S(1)}, bf16[128,512]{1,0:T(8,128)(2,1)S(1)}, u32[]{:S(2)}, u32[]{:S(2)}) collective-permute-start(bf16[128,512]{1,0:T(8,128)(2,1)S(1)} %fusion.18), channel_id=1, source_target_pairs={{0,28},{2,30},{4,0},{6,2},{8,4},{10,6},{12,8},{14,10},{16,12},{18,... | collective-permute-start | bytes 393224 | tf_op jit(solution)/shard_map/ppermute | solution.py:289
  179.7 5.0 %collective-permute-start.27 = (bf16[128,512]{1,0:T(8,128)(2,1)S(1)}, bf16[128,512]{1,0:T(8,128)(2,1)S(1)}, u32[]{:S(2)}, u32[]{:S(2)}) collective-permute-start(bf16[128,512]{1,0:T(8,128)(2,1)S(1)} %fusion.20), channel_id=1, source_target_pairs={{0,28},{2,30},{4,0},{6,2},{8,4},{10,6},{12,8},{14,10},{16,12},{18,... | collective-permute-start | bytes 393224 | tf_op jit(solution)/shard_map/ppermute | solution.py:289
  181.7 6.6 %collective-permute-start.28 = (bf16[256,512]{1,0:T(8,128)(2,1)}, bf16[256,512]{1,0:T(8,128)(2,1)S(1)}, u32[]{:S(2)}, u32[]{:S(2)}) collective-permute-start(bf16[256,512]{1,0:T(8,128)(2,1)} %reduce-scatter.2.cloned.1.call-done), channel_id=1, source_target_pairs={{0,1},{1,0},{2,3},{3,2},{4,5},{5,4},{6,7},{7,6},{8,9},{9,8},{10,11... | collective-permute-start | bytes 786440 | tf_op jit(solution)/shard_map/ppermute | solution.py:382
  (8 other events, 152.6 us)
Sparse Core Ops, SparseCore 0:
  9.8 62.9 all-gather.2
  117.0 41.5 reduce-scatter.1

commit v4 on v2

--- a/solution.py
+++ b/solution.py
@@ -274,6 +274,25 @@
             quarter_ref[:, chip * SLAB : (chip + 1) * SLAB] = whole_ref[:, quarter_columns(mine_ref[0], offset, chip)]
 
 
+def interleave_kernel(long_ref, short_ref, out_ref):
+    places = short_ref.shape[1] // TOK
+    long = long_ref.shape[1] // places
+    for place in range(places):
+        start = place * (long + TOK)
+        out_ref[:, start : start + long] = long_ref[:, place * long : (place + 1) * long]
+        out_ref[:, start + long : start + long + TOK] = short_ref[:, place * TOK : (place + 1) * TOK]
+
+
+def interleaved(long, short):
+    return pl.pallas_call(
+        interleave_kernel,
+        in_specs=[pl.BlockSpec(memory_space=pltpu.VMEM)] * 2,
+        out_specs=pl.BlockSpec(memory_space=pltpu.VMEM),
+        out_shape=jax.ShapeDtypeStruct((TOK, long.shape[1] + short.shape[1]), jnp.bfloat16),
+        cost_estimate=pl.CostEstimate(flops=0, bytes_accessed=4 << 20, transcendentals=0),
+    )(long, short)
+
+
 def quarters_of(mine, whole):
     return pl.pallas_call(
         quarters_kernel,
@@ -361,15 +380,21 @@
     quad_inputs = [quarters[0]] + [quad_partner(quarters[offset], offset) for offset in range(1, 4)]
     key_window = window_of(keys, odd, quarters)
 
+    moves = [(section, section - 1) for section in range(1, lax.axis_size("pipe"))]
+    share = lax.ppermute(weight_rows[-TOK:], "pipe", moves)
+    info = after(info, share)
     probs, given, kept = probs_and_value_grad(0, KV, info, queries, grads, key_window)
+    next_weight = lax.all_gather(after(share, given), "fsdp", axis=0, tiled=True)
     sums = chip_sums(after(given, *quad_inputs[1:]), kept, odd)
     values = rounded(dot(inputs, after(weight, sums[HOPS]), NN))
     value_window = window_of(values, odd)
     value_grad = relayed_sum(sums, [values, *value_window[1:HOPS]])
 
-    moves = [(section, section - 1) for section in range(1, lax.axis_size("pipe"))]
-    input_grad = rounded(dot(value_grad, weight, NT))
-    upstream = lax.ppermute(input_grad, "pipe", moves)
+    sent_weight = weight.reshape(CHIPS * CORES, -1, weight.shape[1])[:, :-TOK].reshape(-1, weight.shape[1])
+    input_grad = rounded(dot(value_grad, sent_weight, NT))
+    arrived = lax.ppermute(input_grad, "pipe", moves)
+    next_grad = lax.ppermute(value_grad, "pipe", moves)
+    upstream = interleaved(arrived, rounded(dot(next_grad, next_weight, NT)))
 
     quad_grads = [value_grad] + [quad_partner(value_grad, offset) for offset in range(1, 4)]
     quad_grads = jnp.concatenate(after(quad_grads, *value_window, input_grad), axis=0)
@@ -384,7 +409,7 @@
 
     value_window[0] = after(value_window[0], weight_part)
     query_out, given, kept = query_and_key_grad(0, KV, queries, grads, probs, key_window, value_window)
-    key_grad = relayed_sum(chip_sums(given, kept, odd), [given, upstream])
+    key_grad = relayed_sum(chip_sums(given, kept, odd), [given, arrived, (upstream, weight_half)])
     return (
         upstream[None, None],
         query_out[None, None],

time: 194 us -> 202 us (1.041)
  matrix products: 12.9 us -> 15.8 us
  Pallas kernels: 46 us -> 48.7 us
  starting transfers between devices: 23.1 us -> 25.7 us
    ppermute x1 -> x3, starting transfers between devices: 3.11 us -> 6.75 us  [the longest x1 2.7 us: shards(): share = lax.ppermute(weight_rows[-TOK:], 'pipe', moves)]
    pallas_call x0 -> x1, Pallas kernels: none -> 3.08 us  [interleaved(): pl.pallas_call(interleave_kernel, in_specs=[pl.BlockSpec(memory_space=plt...]
    dot_general x3 -> x4, matrix products: 12.9 us -> 15.8 us  [dot(): lax.dot_general(left, right, numbers, preferred_element_type=jnp.float32)]
    ppermute x1 -> x3, waiting for transfers between devices: 12 us -> 12.6 us  [the longest x1 6.45 us: shards(): share = lax.ppermute(weight_rows[-TOK:], 'pipe', moves)]
    unnamed x23 -> x22, local copies, waits for them, and re-layouts: 4.19 us -> 4.15 us
  transfers between devices with their start and end apart: 30 -> 33, of which waited for: 22 -> 21; matrix products, arithmetic and copies ran while one was open for 6% -> 10% of each run, Pallas kernels for 24% -> 24%
where the time goes in v4:
time: 202 us
  waiting for transfers between devices  87.3 us (43%)
  Pallas kernels  48.7 us (24%)
  starting transfers between devices  25.7 us (13%)
  matrix products  15.8 us (8%)
  between operations  14 us (7%)
  local copies, waits for them, and re-layouts  5.69 us (3%)
  other arithmetic  4.64 us (2%)
    ppermute x16, waiting for transfers between devices, permuted(): lax.ppermute(value, 'fsdp', [(source, (source + steps) % count) for sourc...  65.6 us
    pallas_call x2, Pallas kernels, part_call(): pl.pallas_call(kernel, grid=(groups, STEPS), in_specs=in_specs + [pl.Bloc...  42.4 us
    dot_general x4, matrix products, dot(): lax.dot_general(left, right, numbers, preferred_element_type=jnp.float32)  15.8 us
    ppermute x16, starting transfers between devices, permuted(): lax.ppermute(value, 'fsdp', [(source, (source + steps) % count) for sourc...  13.4 us
    ppermute x1, waiting for transfers between devices, shards(): share = lax.ppermute(weight_rows[-TOK:], 'pipe', moves)  6.45 us
    ppermute x6, starting transfers between devices, quad_partner(): return lax.ppermute(value, ('pipe', 'fsdp', 'rep'), moves)  4.45 us
    unnamed x22, local copies, waits for them, and re-layouts  4.15 us
  transfers between devices with their start and end apart: 33, of which 21 were waited for; matrix products, arithmetic and copies ran while one was open for 10% of the time, Pallas kernels for 24%

profile of v4, /device:TPU:14, one launch (start us, length us, event | category | flops | bytes accessed | tf_op | source)
XLA Modules:
  0.0 201.8 jit_solution(2389302910898270904)
XLA Ops:
  8.0 2.0 collective-permute-start.1
  10.0 3.2 %shard_map.93 = (bf16[128,2048]{1,0:T(8,128)(2,1)}, bf16[128,2048]{1,0:T(8,128)(2,1)}, bf16[128,2048]{1,0:T(8,128)(2,1)}, bf16[128,2048]{1,0:T(8,128)(2,1)}) custom-call(s32[1]{0:T(128)} %bitcast.6.mine_ref, bf16[128,8192]{1,0:T(8,128)(2,1)} %bitcast.100), custom_call_target="tpu_custom_call" | custom-call | bytes 4194304 | tf_op jit(solution)/shard_map/pallas_call | solution.py:297
  13.1 4.4 %collective-permute-done.1.refs_1_ = bf16[128,512]{1,0:T(8,128)(2,1)S(1)} collective-permute-done((bf16[128,512]{1,0:T(8,128)(2,1)}, bf16[128,512]{1,0:T(8,128)(2,1)S(1)}, u32[]{:S(2)}, u32[]{:S(2)}) %collective-permute-start.1) | collective-permute-done | bytes 131104 | tf_op jit(solution)/shard_map/ppermute | solution.py:308
  17.6 6.2 %collective-permute-done.2.refs_2_ = bf16[128,512]{1,0:T(8,128)(2,1)S(1)} collective-permute-done((bf16[128,512]{1,0:T(8,128)(2,1)S(1)}, bf16[128,512]{1,0:T(8,128)(2,1)S(1)}, u32[]{:S(2)}, u32[]{:S(2)}) %collective-permute-start.2) | collective-permute-done | bytes 131104 | tf_op jit(solution)/shard_map/ppermute | solution.py:308
  23.8 9.2 %collective-permute-done.3.refs_3_ = bf16[128,512]{1,0:T(8,128)(2,1)S(1)} collective-permute-done((bf16[128,512]{1,0:T(8,128)(2,1)S(1)}, bf16[128,512]{1,0:T(8,128)(2,1)S(1)}, u32[]{:S(2)}, u32[]{:S(2)}) %collective-permute-start.3) | collective-permute-done | bytes 131104 | tf_op jit(solution)/shard_map/ppermute | solution.py:308
  33.0 9.0 %collective-permute-done.4.refs_4_ = bf16[128,512]{1,0:T(8,128)(2,1)S(1)} collective-permute-done((bf16[128,512]{1,0:T(8,128)(2,1)S(1)}, bf16[128,512]{1,0:T(8,128)(2,1)S(1)}, u32[]{:S(2)}, u32[]{:S(2)}) %collective-permute-start.4) | collective-permute-done | bytes 131104 | tf_op jit(solution)/shard_map/ppermute | solution.py:308
  43.1 2.7 %collective-permute-start = (bf16[128,512]{1,0:T(8,128)(2,1)S(1)}, bf16[128,512]{1,0:T(8,128)(2,1)S(1)}, u32[]{:S(2)}, u32[]{:S(2)}) collective-permute-start(bf16[128,512]{1,0:T(8,128)(2,1)S(1)} %slice_bitcast_fusion.8), channel_id=1, source_target_pairs={{32,0},{64,32},{96,64},{128,96},{160,128},{192,160},{224,192},{33,... | collective-permute-start | bytes 393224 | tf_op jit(solution)/shard_map/ppermute | solution.py:384
  48.1 6.5 %collective-permute-done = bf16[128,512]{1,0:T(8,128)(2,1)S(1)} collective-permute-done((bf16[128,512]{1,0:T(8,128)(2,1)S(1)}, bf16[128,512]{1,0:T(8,128)(2,1)S(1)}, u32[]{:S(2)}, u32[]{:S(2)}) %collective-permute-start) | collective-permute-done | bytes 131104 | tf_op jit(solution)/shard_map/ppermute | solution.py:384
  56.9 20.8 %shard_map.94 = (bf16[32,1152,256]{2,1,0:T(8,128)(2,1)}, bf16[512,512]{1,0:T(8,128)(2,1)S(1)}, f32[640,512]{1,0:T(8,128)S(1)}) custom-call(s32[5]{0:T(128)S(1)} %pad_add_fusion.info_ref, bf16[128,8192]{1,0:T(8,128)(2,1)S(1)} %bitcast.94, bf16[128,8192]{1,0:T(8,128)(2,1)} %bitcast.104, bf16[128,512]{1,0:T(8,128)(2,1)S(1)} %bitcast.91, ...), custom_call_target="tpu_custom_call" | custom-call | flops 4831838208 | bytes 25165824 | tf_op jit(solution)/shard_map/pallas_call | solution.py:210
  78.6 1.8 collective-permute-done.9
  82.2 5.4 %fusion.7.refs_6_ = bf16[128,512]{1,0:T(8,128)(2,1)S(1)} fusion(bf16[8192,512]{1,0:T(8,128)(2,1)} %bitcast.95, bf16[1,1,128,8192]{3,2,1,0:T(8,128)(2,1)} %param.6), kind=kOutput, calls=%fused_computation.13 | convolution fusion | flops 1073807360 | bytes 10616832 | tf_op jit(solution)/shard_map/dot_general | solution.py:37
  89.8 5.4 %collective-permute-done.11 = bf16[128,512]{1,0:T(8,128)(2,1)S(1)} collective-permute-done((bf16[128,512]{1,0:T(8,128)(2,1)S(1)}, bf16[128,512]{1,0:T(8,128)(2,1)S(1)}, u32[]{:S(2)}, u32[]{:S(2)}) %collective-permute-start.11) | collective-permute-done | bytes 131104 | tf_op jit(solution)/shard_map/ppermute | solution.py:308
  95.2 2.1 %collective-permute-done.12.refs_7_ = bf16[128,512]{1,0:T(8,128)(2,1)S(1)} collective-permute-done((bf16[128,512]{1,0:T(8,128)(2,1)S(1)}, bf16[128,512]{1,0:T(8,128)(2,1)S(1)}, u32[]{:S(2)}, u32[]{:S(2)}) %collective-permute-start.12) | collective-permute-done | bytes 131104 | tf_op jit(solution)/shard_map/ppermute | solution.py:308
  99.5 3.1 %collective-permute-done.13 = bf16[128,512]{1,0:T(8,128)(2,1)S(1)} collective-permute-done((bf16[128,512]{1,0:T(8,128)(2,1)S(1)}, bf16[128,512]{1,0:T(8,128)(2,1)S(1)}, u32[]{:S(2)}, u32[]{:S(2)}) %collective-permute-start.13) | collective-permute-done | bytes 131104 | tf_op jit(solution)/shard_map/ppermute | solution.py:308
  102.6 3.6 %collective-permute-done.14.refs_8_ = bf16[128,512]{1,0:T(8,128)(2,1)S(1)} collective-permute-done((bf16[128,512]{1,0:T(8,128)(2,1)S(1)}, bf16[128,512]{1,0:T(8,128)(2,1)S(1)}, u32[]{:S(2)}, u32[]{:S(2)}) %collective-permute-start.14) | collective-permute-done | bytes 131104 | tf_op jit(solution)/shard_map/ppermute | solution.py:308
  106.3 3.3 %collective-permute-start.15 = (bf16[128,512]{1,0:T(8,128)(2,1)S(1)}, bf16[128,512]{1,0:T(8,128)(2,1)S(1)}, u32[]{:S(2)}, u32[]{:S(2)}) collective-permute-start(bf16[128,512]{1,0:T(8,128)(2,1)S(1)} %fusion.28), channel_id=1, source_target_pairs={{0,28},{2,30},{4,0},{6,2},{8,4},{10,6},{12,8},{14,10},{16,12},{18,... | collective-permute-start | bytes 393224 | tf_op jit(solution)/shard_map/ppermute | solution.py:308
  109.6 3.5 %collective-permute-done.16.refs_9_ = bf16[128,512]{1,0:T(8,128)(2,1)S(1)} collective-permute-done((bf16[128,512]{1,0:T(8,128)(2,1)S(1)}, bf16[128,512]{1,0:T(8,128)(2,1)S(1)}, u32[]{:S(2)}, u32[]{:S(2)}) %collective-permute-start.16) | collective-permute-done | bytes 131104 | tf_op jit(solution)/shard_map/ppermute | solution.py:308
  113.6 5.6 %collective-permute-done.22.refs_10_ = bf16[128,512]{1,0:T(8,128)(2,1)S(1)} collective-permute-done((bf16[128,512]{1,0:T(8,128)(2,1)S(1)}, bf16[128,512]{1,0:T(8,128)(2,1)S(1)}, u32[]{:S(2)}, u32[]{:S(2)}) %collective-permute-start.22) | collective-permute-done | bytes 131104 | tf_op jit(solution)/shard_map/ppermute | solution.py:308
  122.6 3.3 %convolution_convert_fusion = bf16[128,6144]{1,0:T(8,128)(2,1)} fusion(bf16[128,512]{1,0:T(8,128)(2,1)S(1)} %fusion.30, bf16[6144,512]{1,0:T(8,128)(2,1)S(1)} %bitcast.99), kind=kOutput, calls=%fused_computation | convolution fusion | flops 806092800 | bytes 7995392 | tf_op jit(solution)/shard_map/dot_general | solution.py:37
  126.8 2.0 collective-permute-done.21
  128.8 3.9 %convolution_convert_fusion.1 = bf16[2048,512]{1,0:T(8,128)(2,1)} fusion(bf16[128,2048]{1,0:T(8,128)(2,1)} %collective-permute-done.8, bf16[128,2048]{1,0:T(8,128)(2,1)} %collective-permute-done.7, bf16[128,2048]{1,0:T(8,128)(2,1)S(1)} %copy-done.7, bf16[128,2048]{1,0:T(8,128)(2,1)S(1)} %copy-done.5, bf16[128,512]{1,0:T(8,128)(2,1)S(1)} %collective-permute-done.21, ...), kind=kOutput, calls=%fused_computation.1 | convolution fusion | flops 1085276160 | bytes 4718592 | tf_op jit(solution)/shard_map/dot_general | solution.py:37
  132.7 2.1 %collective-permute-start.17 = (bf16[128,6144]{1,0:T(8,128)(2,1)}, bf16[128,6144]{1,0:T(8,128)(2,1)}, u32[]{:S(2)}, u32[]{:S(2)}) collective-permute-start(bf16[128,6144]{1,0:T(8,128)(2,1)} %convolution_convert_fusion), channel_id=1, source_target_pairs={{32,0},{64,32},{96,64},{128,96},{160,128},{192,160},{224,192},{33,... | collective-permute-start | bytes 4718600 | tf_op jit(solution)/shard_map/ppermute | solution.py:395
  134.8 21.6 %shard_map.96 = (bf16[128,8192]{1,0:T(8,128)(2,1)}, bf16[512,512]{1,0:T(8,128)(2,1)S(1)}, f32[640,512]{1,0:T(8,128)S(1)}) custom-call(bf16[128,8192]{1,0:T(8,128)(2,1)} %bitcast.93, bf16[128,8192]{1,0:T(8,128)(2,1)} %bitcast.105, bf16[32,1152,256]{2,1,0:T(8,128)(2,1)} %get-tuple-element.46.probs_ref, bf16[128,512]{1,0:T(8,128)(2,1)S(1)} %bitcast.92, ...), custom_call_target="tpu_custom_call" | custom-call | flops 7247757312 | bytes 29360128 | tf_op jit(solution)/shard_map/pallas_call | solution.py:210
  158.9 7.7 %collective-permute-done.25 = bf16[128,512]{1,0:T(8,128)(2,1)S(1)} collective-permute-done((bf16[128,512]{1,0:T(8,128)(2,1)S(1)}, bf16[128,512]{1,0:T(8,128)(2,1)S(1)}, u32[]{:S(2)}, u32[]{:S(2)}) %collective-permute-start.25) | collective-permute-done | bytes 131104 | tf_op jit(solution)/shard_map/ppermute | solution.py:308
  166.6 2.3 %collective-permute-start.26 = (bf16[128,512]{1,0:T(8,128)(2,1)S(1)}, bf16[128,512]{1,0:T(8,128)(2,1)S(1)}, u32[]{:S(2)}, u32[]{:S(2)}) collective-permute-start(bf16[128,512]{1,0:T(8,128)(2,1)S(1)} %fusion.16), channel_id=1, source_target_pairs={{0,28},{2,30},{4,0},{6,2},{8,4},{10,6},{12,8},{14,10},{16,12},{18,... | collective-permute-start | bytes 393224 | tf_op jit(solution)/shard_map/ppermute | solution.py:308
  168.8 1.9 collective-permute-start.18
  172.4 2.6 %collective-permute-done.17.long_ref = bf16[128,6144]{1,0:T(8,128)(2,1)} collective-permute-done((bf16[128,6144]{1,0:T(8,128)(2,1)}, bf16[128,6144]{1,0:T(8,128)(2,1)}, u32[]{:S(2)}, u32[]{:S(2)}) %collective-permute-start.17) | collective-permute-done | bytes 1572896 | tf_op jit(solution)/shard_map/ppermute | solution.py:395
  175.9 3.5 %collective-permute-done.18 = bf16[128,512]{1,0:T(8,128)(2,1)S(1)} collective-permute-done((bf16[128,512]{1,0:T(8,128)(2,1)S(1)}, bf16[128,512]{1,0:T(8,128)(2,1)S(1)}, u32[]{:S(2)}, u32[]{:S(2)}) %collective-permute-start.18) | collective-permute-done | bytes 131104 | tf_op jit(solution)/shard_map/ppermute | solution.py:396
  179.5 3.2 %convolution_convert_fusion.2.short_ref = bf16[128,2048]{1,0:T(8,128)(2,1)} fusion(bf16[128,512]{1,0:T(8,128)(2,1)S(1)} %collective-permute-done.18, bf16[2048,512]{1,0:T(8,128)(2,1)} %all-gather.4.cloned.1.call-done), kind=kOutput, calls=%fused_computation.2 | convolution fusion | flops 268697600 | bytes 2752512 | tf_op jit(solution)/shard_map/dot_general | solution.py:37
  182.7 3.1 %shard_map.95 = bf16[128,8192]{1,0:T(8,128)(2,1)} custom-call(bf16[128,6144]{1,0:T(8,128)(2,1)} %collective-permute-done.17.long_ref, bf16[128,2048]{1,0:T(8,128)(2,1)} %convolution_convert_fusion.2.short_ref), custom_call_target="tpu_custom_call" | custom-call | bytes 4194304 | tf_op jit(solution)/shard_map/pallas_call | solution.py:287
  186.7 4.1 %collective-permute-done.28 = bf16[128,512]{1,0:T(8,128)(2,1)S(1)} collective-permute-done((bf16[128,512]{1,0:T(8,128)(2,1)S(1)}, bf16[128,512]{1,0:T(8,128)(2,1)S(1)}, u32[]{:S(2)}, u32[]{:S(2)}) %collective-permute-start.28) | collective-permute-done | bytes 131104 | tf_op jit(solution)/shard_map/ppermute | solution.py:308
  191.5 2.0 collective-permute-done.29
  (91 shorter events, 26.7 us)
Async XLA Ops:
  7.2 75.0 %all-gather.6.cloned.1.call-start = ((), (), s32[]{:S(2)}) async-start(), calls=%async_computation.3 | async-start | bytes 8912896 | tf_op jit(solution)/shard_map/all_gather | solution.py:378
  7.9 168.0 %all-gather.4.cloned.1.call-start = ((), (), s32[]{:S(2)}) async-start(), calls=%async_computation.1 | async-start | bytes 2228224 | tf_op jit(solution)/shard_map/all_gather | solution.py:387
  8.0 9.6 %collective-permute-start.1 = (bf16[128,512]{1,0:T(8,128)(2,1)}, bf16[128,512]{1,0:T(8,128)(2,1)S(1)}, u32[]{:S(2)}, u32[]{:S(2)}) collective-permute-start(bf16[128,512]{1,0:T(8,128)(2,1)} %bitcast.90), channel_id=1, source_target_pairs={{0,4},{2,6},{4,8},{6,10},{8,12},{10,14},{12,16},{14,18},{16,20},{1... | collective-permute-start | bytes 393224 | tf_op jit(solution)/shard_map/ppermute | solution.py:308
  17.6 6.2 %collective-permute-start.2 = (bf16[128,512]{1,0:T(8,128)(2,1)S(1)}, bf16[128,512]{1,0:T(8,128)(2,1)S(1)}, u32[]{:S(2)}, u32[]{:S(2)}) collective-permute-start(bf16[128,512]{1,0:T(8,128)(2,1)S(1)} %collective-permute-done.1.refs_1_), channel_id=1, source_target_pairs={{0,4},{2,6},{4,8},{6,10},{8,12},{10,14},{12,16},{14,18},{16,20},{1... | collective-permute-start | bytes 393224 | tf_op jit(solution)/shard_map/ppermute | solution.py:308
  23.8 9.2 %collective-permute-start.3 = (bf16[128,512]{1,0:T(8,128)(2,1)S(1)}, bf16[128,512]{1,0:T(8,128)(2,1)S(1)}, u32[]{:S(2)}, u32[]{:S(2)}) collective-permute-start(bf16[128,512]{1,0:T(8,128)(2,1)S(1)} %collective-permute-done.2.refs_2_), channel_id=1, source_target_pairs={{0,4},{2,6},{4,8},{6,10},{8,12},{10,14},{12,16},{14,18},{16,20},{1... | collective-permute-start | bytes 393224 | tf_op jit(solution)/shard_map/ppermute | solution.py:308
  33.0 9.0 %collective-permute-start.4 = (bf16[128,512]{1,0:T(8,128)(2,1)S(1)}, bf16[128,512]{1,0:T(8,128)(2,1)S(1)}, u32[]{:S(2)}, u32[]{:S(2)}) collective-permute-start(bf16[128,512]{1,0:T(8,128)(2,1)S(1)} %collective-permute-done.3.refs_3_), channel_id=1, source_target_pairs={{0,4},{2,6},{4,8},{6,10},{8,12},{10,14},{12,16},{14,18},{16,20},{1... | collective-permute-start | bytes 393224 | tf_op jit(solution)/shard_map/ppermute | solution.py:308
  42.1 12.5 %collective-permute-start.5 = (bf16[512,512]{1,0:T(8,128)(2,1)S(1)}, bf16[512,512]{1,0:T(8,128)(2,1)S(1)}, u32[]{:S(2)}, u32[]{:S(2)}) collective-permute-start(bf16[512,512]{1,0:T(8,128)(2,1)S(1)} %pad_maximum_fusion), channel_id=1, source_target_pairs={{0,2},{2,0},{4,6},{6,4},{8,10},{10,8},{12,14},{14,12},{16,18},{18,... | collective-permute-start | bytes 1572872 | tf_op jit(solution)/shard_map/ppermute | solution.py:313
  43.1 11.5 %collective-permute-start = (bf16[128,512]{1,0:T(8,128)(2,1)S(1)}, bf16[128,512]{1,0:T(8,128)(2,1)S(1)}, u32[]{:S(2)}, u32[]{:S(2)}) collective-permute-start(bf16[128,512]{1,0:T(8,128)(2,1)S(1)} %slice_bitcast_fusion.8), channel_id=1, source_target_pairs={{32,0},{64,32},{96,64},{128,96},{160,128},{192,160},{224,192},{33,... | collective-permute-start | bytes 393224 | tf_op jit(solution)/shard_map/ppermute | solution.py:384
  45.8 31.8 %collective-permute-start.6 = (bf16[128,2048]{1,0:T(8,128)(2,1)}, bf16[128,2048]{1,0:T(8,128)(2,1)S(1)}, u32[]{:S(2)}, u32[]{:S(2)}) collective-permute-start(bf16[128,2048]{1,0:T(8,128)(2,1)} %get-tuple-element.33), channel_id=1, source_target_pairs={{0,1},{1,0},{2,3},{3,2},{4,5},{5,4},{6,7},{7,6},{8,9},{9,8},{10,11... | collective-permute-start | bytes 1572872 | tf_op jit(solution)/shard_map/ppermute | solution.py:328
  46.3 31.4 %collective-permute-start.7 = (bf16[128,2048]{1,0:T(8,128)(2,1)}, bf16[128,2048]{1,0:T(8,128)(2,1)}, u32[]{:S(2)}, u32[]{:S(2)}) collective-permute-start(bf16[128,2048]{1,0:T(8,128)(2,1)} %get-tuple-element.34), channel_id=1, source_target_pairs={{0,2},{1,3},{2,0},{3,1},{4,6},{5,7},{6,4},{7,5},{8,10},{9,11},{10,... | collective-permute-start | bytes 1572872 | tf_op jit(solution)/shard_map/ppermute | solution.py:328
  46.3 31.4 %collective-permute-start.8 = (bf16[128,2048]{1,0:T(8,128)(2,1)}, bf16[128,2048]{1,0:T(8,128)(2,1)}, u32[]{:S(2)}, u32[]{:S(2)}) collective-permute-start(bf16[128,2048]{1,0:T(8,128)(2,1)} %get-tuple-element.35), channel_id=1, source_target_pairs={{0,3},{1,2},{2,1},{3,0},{4,7},{5,6},{6,5},{7,4},{8,11},{9,10},{10,... | collective-permute-start | bytes 1572872 | tf_op jit(solution)/shard_map/ppermute | solution.py:328
  78.5 1.9 collective-permute-start.9
  78.5 107.2 %reduce-scatter.2.cloned.1.call-start = ((), (), s32[]{:S(2)}) async-start(), calls=%async_computation.2 | async-start | bytes 2359296 | tf_op jit(solution)/shard_map/reduce_scatter | solution.py:402
  81.9 5.8 %collective-permute-start.10 = (bf16[128,512]{1,0:T(8,128)(2,1)S(1)}, bf16[128,512]{1,0:T(8,128)(2,1)S(1)}, u32[]{:S(2)}, u32[]{:S(2)}) collective-permute-start(bf16[128,512]{1,0:T(8,128)(2,1)S(1)} %fusion.31), channel_id=1, source_target_pairs={{0,28},{2,30},{4,0},{6,2},{8,4},{10,6},{12,8},{14,10},{16,12},{18,... | collective-permute-start | bytes 393224 | tf_op jit(solution)/shard_map/ppermute | solution.py:308
  87.7 7.5 %collective-permute-start.11 = (bf16[128,512]{1,0:T(8,128)(2,1)S(1)}, bf16[128,512]{1,0:T(8,128)(2,1)S(1)}, u32[]{:S(2)}, u32[]{:S(2)}) collective-permute-start(bf16[128,512]{1,0:T(8,128)(2,1)S(1)} %fusion.24), channel_id=1, source_target_pairs={{0,28},{2,30},{4,0},{6,2},{8,4},{10,6},{12,8},{14,10},{16,12},{18,... | collective-permute-start | bytes 393224 | tf_op jit(solution)/shard_map/ppermute | solution.py:308
  89.3 8.0 %collective-permute-start.12 = (bf16[128,512]{1,0:T(8,128)(2,1)S(1)}, bf16[128,512]{1,0:T(8,128)(2,1)S(1)}, u32[]{:S(2)}, u32[]{:S(2)}) collective-permute-start(bf16[128,512]{1,0:T(8,128)(2,1)S(1)} %fusion.7.refs_6_), channel_id=1, source_target_pairs={{0,4},{2,6},{4,8},{6,10},{8,12},{10,14},{12,16},{14,18},{16,20},{1... | collective-permute-start | bytes 393224 | tf_op jit(solution)/shard_map/ppermute | solution.py:308
  97.3 5.2 %collective-permute-start.13 = (bf16[128,512]{1,0:T(8,128)(2,1)S(1)}, bf16[128,512]{1,0:T(8,128)(2,1)S(1)}, u32[]{:S(2)}, u32[]{:S(2)}) collective-permute-start(bf16[128,512]{1,0:T(8,128)(2,1)S(1)} %fusion.26), channel_id=1, source_target_pairs={{0,28},{2,30},{4,0},{6,2},{8,4},{10,6},{12,8},{14,10},{16,12},{18,... | collective-permute-start | bytes 393224 | tf_op jit(solution)/shard_map/ppermute | solution.py:308
  98.8 7.4 %collective-permute-start.14 = (bf16[128,512]{1,0:T(8,128)(2,1)S(1)}, bf16[128,512]{1,0:T(8,128)(2,1)S(1)}, u32[]{:S(2)}, u32[]{:S(2)}) collective-permute-start(bf16[128,512]{1,0:T(8,128)(2,1)S(1)} %collective-permute-done.12.refs_7_), channel_id=1, source_target_pairs={{0,4},{2,6},{4,8},{6,10},{8,12},{10,14},{12,16},{14,18},{16,20},{1... | collective-permute-start | bytes 393224 | tf_op jit(solution)/shard_map/ppermute | solution.py:308
  106.2 6.8 %collective-permute-start.16 = (bf16[128,512]{1,0:T(8,128)(2,1)S(1)}, bf16[128,512]{1,0:T(8,128)(2,1)S(1)}, u32[]{:S(2)}, u32[]{:S(2)}) collective-permute-start(bf16[128,512]{1,0:T(8,128)(2,1)S(1)} %collective-permute-done.14.refs_8_), channel_id=1, source_target_pairs={{0,4},{2,6},{4,8},{6,10},{8,12},{10,14},{12,16},{14,18},{16,20},{1... | collective-permute-start | bytes 393224 | tf_op jit(solution)/shard_map/ppermute | solution.py:308
  106.3 7.4 %collective-permute-start.15 = (bf16[128,512]{1,0:T(8,128)(2,1)S(1)}, bf16[128,512]{1,0:T(8,128)(2,1)S(1)}, u32[]{:S(2)}, u32[]{:S(2)}) collective-permute-start(bf16[128,512]{1,0:T(8,128)(2,1)S(1)} %fusion.28), channel_id=1, source_target_pairs={{0,28},{2,30},{4,0},{6,2},{8,4},{10,6},{12,8},{14,10},{16,12},{18,... | collective-permute-start | bytes 393224 | tf_op jit(solution)/shard_map/ppermute | solution.py:308
  113.0 6.2 %collective-permute-start.22 = (bf16[128,512]{1,0:T(8,128)(2,1)S(1)}, bf16[128,512]{1,0:T(8,128)(2,1)S(1)}, u32[]{:S(2)}, u32[]{:S(2)}) collective-permute-start(bf16[128,512]{1,0:T(8,128)(2,1)S(1)} %collective-permute-done.16.refs_9_), channel_id=1, source_target_pairs={{0,4},{2,6},{4,8},{6,10},{8,12},{10,14},{12,16},{14,18},{16,20},{1... | collective-permute-start | bytes 393224 | tf_op jit(solution)/shard_map/ppermute | solution.py:308
  119.3 9.5 %collective-permute-start.23 = (bf16[512,512]{1,0:T(8,128)(2,1)S(1)}, bf16[512,512]{1,0:T(8,128)(2,1)S(1)}, u32[]{:S(2)}, u32[]{:S(2)}) collective-permute-start(bf16[512,512]{1,0:T(8,128)(2,1)S(1)} %pad_maximum_fusion.1), channel_id=1, source_target_pairs={{0,2},{2,0},{4,6},{6,4},{8,10},{10,8},{12,14},{14,12},{16,18},{18,... | collective-permute-start | bytes 1572872 | tf_op jit(solution)/shard_map/ppermute | solution.py:313
  120.4 6.4 %collective-permute-start.19 = (bf16[128,512]{1,0:T(8,128)(2,1)S(1)}, bf16[128,512]{1,0:T(8,128)(2,1)S(1)}, u32[]{:S(2)}, u32[]{:S(2)}) collective-permute-start(bf16[128,512]{1,0:T(8,128)(2,1)S(1)} %fusion.30), channel_id=1, source_target_pairs={{0,1},{1,0},{2,3},{3,2},{4,5},{5,4},{6,7},{7,6},{8,9},{9,8},{10,11... | collective-permute-start | bytes 393224 | tf_op jit(solution)/shard_map/ppermute | solution.py:328
  121.2 5.6 %collective-permute-start.20 = (bf16[128,512]{1,0:T(8,128)(2,1)S(1)}, bf16[128,512]{1,0:T(8,128)(2,1)S(1)}, u32[]{:S(2)}, u32[]{:S(2)}) collective-permute-start(bf16[128,512]{1,0:T(8,128)(2,1)S(1)} %fusion.30), channel_id=1, source_target_pairs={{0,2},{1,3},{2,0},{3,1},{4,6},{5,7},{6,4},{7,5},{8,10},{9,11},{10,... | collective-permute-start | bytes 393224 | tf_op jit(solution)/shard_map/ppermute | solution.py:328
  121.4 7.4 %collective-permute-start.21 = (bf16[128,512]{1,0:T(8,128)(2,1)S(1)}, bf16[128,512]{1,0:T(8,128)(2,1)S(1)}, u32[]{:S(2)}, u32[]{:S(2)}) collective-permute-start(bf16[128,512]{1,0:T(8,128)(2,1)S(1)} %fusion.30), channel_id=1, source_target_pairs={{0,3},{1,2},{2,1},{3,0},{4,7},{5,6},{6,5},{7,4},{8,11},{9,10},{10,... | collective-permute-start | bytes 393224 | tf_op jit(solution)/shard_map/ppermute | solution.py:328
  132.7 42.3 %collective-permute-start.17 = (bf16[128,6144]{1,0:T(8,128)(2,1)}, bf16[128,6144]{1,0:T(8,128)(2,1)}, u32[]{:S(2)}, u32[]{:S(2)}) collective-permute-start(bf16[128,6144]{1,0:T(8,128)(2,1)} %convolution_convert_fusion), channel_id=1, source_target_pairs={{32,0},{64,32},{96,64},{128,96},{160,128},{192,160},{224,192},{33,... | collective-permute-start | bytes 4718600 | tf_op jit(solution)/shard_map/ppermute | solution.py:395
  158.8 7.8 %collective-permute-start.25 = (bf16[128,512]{1,0:T(8,128)(2,1)S(1)}, bf16[128,512]{1,0:T(8,128)(2,1)S(1)}, u32[]{:S(2)}, u32[]{:S(2)}) collective-permute-start(bf16[128,512]{1,0:T(8,128)(2,1)S(1)} %fusion.33), channel_id=1, source_target_pairs={{0,28},{2,30},{4,0},{6,2},{8,4},{10,6},{12,8},{14,10},{16,12},{18,... | collective-permute-start | bytes 393224 | tf_op jit(solution)/shard_map/ppermute | solution.py:308
  166.6 5.8 %collective-permute-start.26 = (bf16[128,512]{1,0:T(8,128)(2,1)S(1)}, bf16[128,512]{1,0:T(8,128)(2,1)S(1)}, u32[]{:S(2)}, u32[]{:S(2)}) collective-permute-start(bf16[128,512]{1,0:T(8,128)(2,1)S(1)} %fusion.16), channel_id=1, source_target_pairs={{0,28},{2,30},{4,0},{6,2},{8,4},{10,6},{12,8},{14,10},{16,12},{18,... | collective-permute-start | bytes 393224 | tf_op jit(solution)/shard_map/ppermute | solution.py:308
  168.8 10.6 %collective-permute-start.18 = (bf16[128,512]{1,0:T(8,128)(2,1)S(1)}, bf16[128,512]{1,0:T(8,128)(2,1)S(1)}, u32[]{:S(2)}, u32[]{:S(2)}) collective-permute-start(bf16[128,512]{1,0:T(8,128)(2,1)S(1)} %fusion.30), channel_id=1, source_target_pairs={{32,0},{64,32},{96,64},{128,96},{160,128},{192,160},{224,192},{33,... | collective-permute-start | bytes 393224 | tf_op jit(solution)/shard_map/ppermute | solution.py:396
  175.0 10.7 %collective-permute-start.27 = (bf16[128,512]{1,0:T(8,128)(2,1)S(1)}, bf16[128,512]{1,0:T(8,128)(2,1)S(1)}, u32[]{:S(2)}, u32[]{:S(2)}) collective-permute-start(bf16[128,512]{1,0:T(8,128)(2,1)S(1)} %fusion.18), channel_id=1, source_target_pairs={{0,28},{2,30},{4,0},{6,2},{8,4},{10,6},{12,8},{14,10},{16,12},{18,... | collective-permute-start | bytes 393224 | tf_op jit(solution)/shard_map/ppermute | solution.py:308
  185.8 5.0 %collective-permute-start.28 = (bf16[128,512]{1,0:T(8,128)(2,1)S(1)}, bf16[128,512]{1,0:T(8,128)(2,1)S(1)}, u32[]{:S(2)}, u32[]{:S(2)}) collective-permute-start(bf16[128,512]{1,0:T(8,128)(2,1)S(1)} %fusion.20), channel_id=1, source_target_pairs={{0,28},{2,30},{4,0},{6,2},{8,4},{10,6},{12,8},{14,10},{16,12},{18,... | collective-permute-start | bytes 393224 | tf_op jit(solution)/shard_map/ppermute | solution.py:308
  186.2 7.3 %collective-permute-start.29 = (bf16[256,512]{1,0:T(8,128)(2,1)}, bf16[256,512]{1,0:T(8,128)(2,1)S(1)}, u32[]{:S(2)}, u32[]{:S(2)}) collective-permute-start(bf16[256,512]{1,0:T(8,128)(2,1)} %reduce-scatter.2.cloned.1.call-done), channel_id=1, source_target_pairs={{0,1},{1,0},{2,3},{3,2},{4,5},{5,4},{6,7},{7,6},{8,9},{9,8},{10,11... | collective-permute-start | bytes 786440 | tf_op jit(solution)/shard_map/ppermute | solution.py:405
  (12 other events, 158.5 us)
Sparse Core Ops, SparseCore 0:
  9.8 62.9 all-gather.5
  78.6 38.7 all-gather.3
  132.8 41.3 reduce-scatter.1
